TPU v7x, 128 devices: a whole 4x4x4 slice. The times are simulated.
128 devices in a mesh: role: 2 (over y_hi), tile: 64 (over y_lo, x, z, core).
Axes of the slice: x: 4, y: 4 (y_hi: 2, y_lo: 2; y = y_hi * 2 + y_lo), z: 4, core: 2. Of those that a mesh axis runs over, the one named last changes fastest.
Arguments:
- fields_pair: float32 [2, 512, 65536], P('role', None, 'tile'), may hold values from 0 to 1
- velocity: float32 [65536], P('tile'), may hold values from -0.5 to 0.5
- growth: float32 [65536], P('tile'), may hold values from 0.05 to 0.5
- features: bfloat16 [512, 1024], replicated, may hold values from -6 to 6
- assignment: int32 [512], replicated, may hold values from 0 to 511, each once
- out_pair: float32 [2, 1024, 65536], P('role', None, 'tile'), may hold values from -0.1875 to 0.1875
- hidden_pair: float32 [2, 5, 1024, 1024], P('role', None, 'tile'), may hold values from -0.1875 to 0.1875
Outputs:
- fields_next: float32 [2, 512, 65536], P('role', None, 'tile')
- out_next: float32 [2, 1024, 65536], P('role', None, 'tile')
- hidden_next: float32 [2, 5, 1024, 1024], P('role', None, 'tile')
Inputs may be any that keep to these rules, and one draw needn't show every extreme that they name: `assignment`: a permutation of the 512 members.
All inputs are finite; a program needn't handle non-finite values.
Results may differ from a plain program's by a relative error of at most 0.0022.
The roundings to bfloat16 on the way count: a program that leaves them out, or rounds other values in their place, can miss the bound.
Values may be sent and summed in bfloat16 or wider, within the bound.
No kernel may reach another device: no remote copies, remote signals or barrier semaphores. Data moves between devices by JAX's collectives and lax.ppermute only.
A program may use at most 192 MiB of HBM per device.

v0:
```python
import jax
import jax.numpy as jnp
from jax import lax
from jax.sharding import Mesh
from jax.sharding import PartitionSpec as P

BATCH = 512
TILE = ("tile_0", "tile_1", "tile_2", "tile_3")


momentum_decay = 0.9
step_size = 0.1


def extended(value, sides, width):
    for axis, dim in sides:
        count, length = (lax.axis_size(axis), value.shape[dim])
        up = [(i, (i + 1) % count) for i in range(count)]
        down = [(j, i) for i, j in up]
        last = lax.slice_in_dim(value, length - width, length, axis=dim)
        leading = lax.slice_in_dim(value, 0, width, axis=dim)
        before = lax.ppermute(last, axis, up)
        after = lax.ppermute(leading, axis, down)
        value = jnp.concatenate([before, value, after], axis=dim)
    return value


def from_root(value, axis, root):
    return lax.dynamic_index_in_dim(lax.all_gather(value, axis), root, 0, keepdims=False)


def rows_for(lines, count):
    spare = -lines.shape[0] % count
    if not spare:
        return lines
    return jnp.concatenate([lines, jnp.zeros((spare, *lines.shape[1:]), lines.dtype)])


def from_everyone(value, axis):
    copies = jnp.broadcast_to(value, (lax.axis_size(axis), *value.shape))
    return lax.all_to_all(copies, axis, split_axis=0, concat_axis=0, tiled=True)


def joined_along(parts, dim):
    parts = jnp.moveaxis(parts, 0, dim)
    dims = parts.shape
    return parts.reshape(*dims[:dim], dims[dim] * dims[dim + 1], *dims[dim + 2 :])


def gather_axes(value, axes, dim):
    far, near = axes
    parts = from_everyone(from_everyone(value, far), near)
    return joined_along(parts.swapaxes(0, 1).reshape(-1, *value.shape), dim)


def split_up(value, dim, count):
    before, after = (value.shape[:dim], value.shape[dim + 1 :])
    return jnp.moveaxis(value.reshape(*before, count, -1, *after), dim, 0)


def sent_and_summed(value, axis, dim):
    parts = split_up(value, dim, lax.axis_size(axis))
    arrived = lax.all_to_all(parts, axis, split_axis=0, concat_axis=0, tiled=True)
    return arrived.sum(axis=0)


def summed_rows(value, axes, dim):
    far, near = axes
    own = sent_and_summed(split_up(value, dim, lax.axis_size(far)), near, dim + 1)
    return jnp.sum(lax.all_to_all(own, far, 0, 0, tiled=True), axis=0)


def nested_sum(value, axes):
    lines = value.reshape(-1, value.shape[-1])
    padded = rows_for(lines, lax.axis_size(axes[0]) * lax.axis_size(axes[1]))
    whole = gather_axes(summed_rows(padded, axes, 0), axes, 0)
    return lax.slice_in_dim(whole, 0, len(lines)).reshape(value.shape)


def partner(value, axis, distance):
    return lax.ppermute(value, axis, [(i, i ^ 1 << distance) for i in range(lax.axis_size(axis))])


def guarded(flag, action, *operands):

    def skipped(*values):
        return jax.tree.map(jnp.zeros_like, action(*values))

    return lax.cond(flag, action, skipped, *operands)


def silu_slope(values):
    logistic = jax.nn.sigmoid(values)
    return logistic * (1.0 + values * (1.0 - logistic))


def advance(padded, growth):
    states = padded[:-1]
    velocity_row = padded[-1]
    outflow = (
        jnp.maximum(velocity_row[:-1], 0.0) * states[:, :-1]
        + jnp.minimum(velocity_row[:-1], 0.0) * states[:, 1:]
    )
    carried = states[:, 1:-1] - outflow[:, 1:] + outflow[:, :-1]
    return carried + growth * carried * (1.0 - carried)


def body(fields_pair, velocity, growth, features, assignment, out_pair, hidden_pair):
    solver_side = lax.axis_index("role") == 0
    trainer_side = jnp.logical_not(solver_side)
    own_fields = fields_pair[0]
    own_out = out_pair[0]
    own_hidden = hidden_pair[0]
    layer_count = own_hidden.shape[0]
    unit_rows = own_hidden.shape[1]
    first_unit = lax.axis_index(TILE) * unit_rows
    stacked = jnp.concatenate([own_fields, velocity[None, :]], axis=0)
    padded = extended(stacked, ((TILE, 1),), 1)
    advanced = guarded(solver_side, advance, padded, growth)
    fresh_fields = from_root(advanced, "role", 0)
    out_narrow = own_out.astype(jnp.bfloat16)
    hidden_narrow = own_hidden.astype(jnp.bfloat16)
    full_hidden = lax.all_gather(hidden_narrow, TILE, axis=1, tiled=True)

    def forward(features, full_hidden, out_narrow, target):
        inputs = []
        summed_list = []
        activation = features
        for layer_index in range(layer_count):
            inputs.append(activation)
            summed = jnp.dot(
                activation, full_hidden[layer_index], preferred_element_type=jnp.float32
            )
            summed_list.append(summed)
            activation = jax.nn.silu(summed).astype(jnp.bfloat16)
        predicted = jnp.dot(activation, out_narrow, preferred_element_type=jnp.float32)
        residual = ((predicted - target) / BATCH).astype(jnp.bfloat16)
        grad_out = jnp.dot(activation.T, residual, preferred_element_type=jnp.float32)
        partial_grad = lax.dot_general(
            residual, out_narrow, (((1,), (1,)), ((), ())), preferred_element_type=jnp.float32
        )
        return (jnp.stack(summed_list), jnp.stack(inputs), grad_out, partial_grad)

    summed_all, inputs_all, grad_out, partial_grad = guarded(
        trainer_side, forward, features, full_hidden, out_narrow, own_fields
    )
    upstream = nested_sum(partial_grad, (("tile_0", "tile_1", "tile_2"), "tile_3"))

    def backward(summed_all, inputs_all, upstream, full_hidden, first_unit):
        gradients = []
        for layer_index in reversed(range(layer_count)):
            slope = (upstream * silu_slope(summed_all[layer_index])).astype(jnp.bfloat16)
            own_inputs = lax.dynamic_slice_in_dim(inputs_all[layer_index], first_unit, unit_rows, 1)
            gradients.append(jnp.dot(own_inputs.T, slope, preferred_element_type=jnp.float32))
            if layer_index > 0:
                upstream = lax.dot_general(
                    slope,
                    full_hidden[layer_index],
                    (((1,), (1,)), ((), ())),
                    preferred_element_type=jnp.float32,
                )
        return jnp.stack(gradients[::-1])

    grad_hidden = guarded(
        trainer_side, backward, summed_all, inputs_all, upstream, full_hidden, first_unit
    )
    solver_pack = jnp.concatenate([own_out.reshape(-1), own_hidden.reshape(-1)])
    trainer_pack = jnp.concatenate([grad_out.reshape(-1), grad_hidden.reshape(-1)])
    payload = jnp.where(solver_side, solver_pack, trainer_pack)
    received = partner(payload, "role", 0)
    out_length = own_out.size
    other_out = received[:out_length].reshape(own_out.shape)
    other_hidden = received[out_length:].reshape(own_hidden.shape)
    out_next = jnp.where(
        solver_side,
        momentum_decay * own_out + other_out,
        own_out - step_size * (momentum_decay * other_out + grad_out),
    )
    hidden_next = jnp.where(
        solver_side,
        momentum_decay * own_hidden + other_hidden,
        own_hidden - step_size * (momentum_decay * other_hidden + grad_hidden),
    )
    fields_next = jnp.where(solver_side, advanced, jnp.take(fresh_fields, assignment, axis=0))
    return (fields_next[None], out_next[None], hidden_next[None])


def solution(mesh):
    finer = Mesh(
        mesh.devices.reshape(mesh.shape["role"], 2, 4, 4, 2),
        ("role", "tile_0", "tile_1", "tile_2", "tile_3"),
    )
    in_specs = (
        P("role", None, TILE),
        P(TILE),
        P(TILE),
        P(),
        P(),
        P("role", None, TILE),
        P("role", None, TILE, None),
    )
    out_specs = (P("role", None, TILE), P("role", None, TILE), P("role", None, TILE, None))
    return jax.shard_map(body, mesh=finer, in_specs=in_specs, out_specs=out_specs, check_vma=False)
```

profile of v0, /device:TPU:1, one launch (start us, length us, event | category | flops | bytes accessed | tf_op | source)
XLA Modules:
  0.0 405.7 jit_solution(4291175389253201771)
XLA Ops:
  8.0 0.0 all-gather.4.cloned.1.call-start
  8.0 1.7 bitcast_convert_fusion
  9.7 119.9 %all-gather.4.cloned.1.call-done = bf16[5,1024,1024]{2,1,0:T(8,128)(2,1)} async-done(((bf16[5,16,1024]{2,1,0:T(8,128)(2,1)}), bf16[5,1024,1024]{2,1,0:T(8,128)(2,1)}) %all-gather.4.cloned.1.call-update) | async-done | bytes 10485776 | tf_op jit(solution)/shard_map/all_gather | solution.py:123
  129.7 11.4 %conditional.4 = (f32[5,512,1024]{2,1,0:T(8,128)}, bf16[5,512,1024]{2,1,0:T(8,128)(2,1)}, f32[1024,1024]{1,0:T(8,128)}, f32[512,1024]{1,0:T(8,128)S(1)}, f32[1048576]{0:T(1024)S(1)}) conditional(s32[]{:T(128)} %convert_element_type.57, () %tuple.54, (bf16[5,1024,1024]{2,1,0:T(8,128)(2,1)}, bf16[512,1024]{1,0:T(8,128)(2,1)}, f32[1024,1024]{1,0:T(8,128)}, ...), branch_computations={%region_2.3_spmd, %region_3.4_spmd} | conditional | flops 8619819008 | bytes 165675232 | solution.py:89
  129.7 5.2 %broadcast.54 = f32[5,512,1024]{2,1,0:T(8,128)} broadcast(f32[]{:T(128)} %constant.80.clone), dimensions={} | broadcast | bytes 10485764 | tf_op jit(solution)/shard_map/broadcast.15
  134.9 3.0 broadcast.55
  137.9 2.5 broadcast.56
  140.4 0.3 reshape.56
  140.7 0.2 broadcast.57
  141.1 0.2 copy.15
  141.4 1.8 copy-done.2
  143.2 5.3 %all_to_all.20 = f32[2,32,8,1024]{3,2,1,0:T(8,128)S(1)} all-to-all(f32[2,32,8,1024]{3,2,1,0:T(8,128)S(1)} %copy.15), channel_id=1, replica_groups=mesh['role'=2,'tile_0'=2,'tile_1'=4,'tile_2'=4,'tile_3'=2] {'tile_3'}, dimensions={0} | all-to-all | bytes 4194304 | tf_op jit(solution)/shard_map/all_to_all | solution.py:63
  148.5 1.2 reduce_sum.18
  149.7 21.2 %all_to_all.21 = f32[32,8,1024]{2,1,0:T(8,128)S(1)} all-to-all(f32[32,8,1024]{2,1,0:T(8,128)} %reduce_sum.18), channel_id=1, replica_groups=mesh['role'=2,'tile_0'=2,'tile_1'=4,'tile_2'=4,'tile_3'=2] {'tile_0','ti..., dimensions={0} | all-to-all | bytes 2097152 | tf_op jit(solution)/shard_map/all_to_all | solution.py:70
  170.9 0.1 reduce_sum.19
  171.0 1.1 broadcast_in_dim.38
  172.1 4.7 %all-to-all-start.2 = ((f32[32,8,1024]{2,1,0:T(8,128)}), f32[32,8,1024]{2,1,0:T(8,128)S(1)}, u32[]{:S(2)}, u32[]{:S(2)}) async-start(f32[32,8,1024]{2,1,0:T(8,128)} %broadcast_in_dim.38), calls=%async_computation.2 | async-start | bytes 2097152 | tf_op jit(solution)/shard_map/all_to_all | solution.py:41
  176.8 0.0 all-gather.6.cloned.1.call-start
  176.9 0.9 fusion.96
  177.8 3.4 collective-permute-start
  181.1 1.5 pad_maximum_fusion
  182.6 5.2 %copy.19 = f32[128,8,8,128]{3,1,2,0:T(8,128)} copy(f32[128,8,8,128]{3,2,1,0:T(8,128)} %bitcast.227) | data formatting | bytes 8388608
  187.8 0.8 copy.20
  188.6 3.5 collective-permute-done
  192.1 0.7 copy-done.12
  192.8 1.8 collective-permute-done.1
  194.6 3.1 concatenate.13
  197.6 3.2 conditional.3
  197.7 0.7 multiply_add_fusion
  198.4 2.5 multiply_add_fusion.1
  200.9 0.3 broadcast_in_dim.39
  201.2 9.4 %all_to_all.22 = f32[2,32,8,1024]{3,2,1,0:T(8,128)S(1)} all-to-all(f32[2,32,8,1024]{3,2,1,0:T(8,128)S(1)} %broadcast_in_dim.39), channel_id=1, replica_groups=mesh['role'=2,'tile_0'=2,'tile_1'=4,'tile_2'=4,'tile_3'=2] {'tile_3'}, dimensions={0} | all-to-all | bytes 4194304 | tf_op jit(solution)/shard_map/all_to_all | solution.py:41
  210.6 1.5 conditional.5
  210.6 0.7 broadcast.59
  211.4 0.8 reshape.58
  212.1 5.7 %maximum_select_fusion = f32[1130496]{0:T(1024)} fusion(f32[81920]{0:T(1024)S(1)} %bitcast.240, f32[1048576]{0:T(1024)} %bitcast.229, f32[81920]{0:T(1024)} %get-tuple-element.91, f32[1048576]{0:T(1024)} %copy-done.2, pred[]{:T(512)S(6)} %eq.3), kind=kLoop, calls=%fused_computation.118 | loop fusion | flops 3391488 | bytes 13565953 | tf_op jit(solution)/shard_map/jit(_where)/select_n | solution.py:169
  217.9 53.5 %collective-permute-start.2 = (f32[1130496]{0:T(1024)}, f32[1130496]{0:T(1024)}, u32[]{:S(2)}, u32[]{:S(2)}) collective-permute-start(f32[1130496]{0:T(1024)} %maximum_select_fusion), channel_id=1, source_target_pairs={{0,64},{64,0},{1,65},{65,1},{2,66},{66,2},{3,67},{67,3},{4,68},{68... | collective-permute-start | bytes 13565960 | tf_op jit(solution)/shard_map/ppermute | solution.py:81
  271.4 15.9 %all-gather.6.cloned.1.call-done = f32[1024,1024]{1,0:T(8,128)} async-done(((f32[512,1024]{1,0:T(8,128)}), f32[1024,1024]{1,0:T(8,128)}) %all-gather.6.cloned.1.call-update) | async-done | bytes 4194320 | tf_op jit(solution)/shard_map/all_gather | solution.py:29
  287.3 1.6 slice-done
  288.9 2.7 gather_fusion
  291.6 3.8 select_bitcast_fusion.1
  295.4 81.9 %collective-permute-done.2 = f32[1130496]{0:T(1024)} collective-permute-done((f32[1130496]{0:T(1024)}, f32[1130496]{0:T(1024)}, u32[]{:S(2)}, u32[]{:S(2)}) %collective-permute-start.2) | collective-permute-done | bytes 4522016 | tf_op jit(solution)/shard_map/ppermute | solution.py:81
  377.2 1.0 slice.147
  378.2 0.1 slice.135
  378.3 4.4 %slice.146 = f32[1048576]{0:T(1024)} slice(f32[1130496]{0:T(1024)} %collective-permute-done.2), slice={[0:1048576]} | slice | bytes 8388608 | tf_op jit(solution)/shard_map/slice | solution.py:172
  382.7 5.0 %slice.133 = f32[1024,1024]{1,0:T(8,128)} reshape(f32[1048576]{0:T(1024)} %slice.146) | data formatting | bytes 8388608 | tf_op jit(solution)/shard_map/slice | solution.py:172
  387.8 1.8 fusion.94
  389.5 8.7 %select_bitcast_fusion = f32[1,1024,1024]{2,1,0:T(8,128)} fusion(f32[1024,1024]{1,0:T(8,128)} %get-tuple-element.92, f32[1024,1024]{1,0:T(8,128)} %slice.133, pred[]{:T(512)S(6)} %eq.3, f32[1,1024,1024]{2,1,0:T(8,128)} %param.18), kind=kLoop, calls=%fused_computation.119 | loop fusion | flops 7340032 | bytes 16777216 | tf_op jit(solution)/shard_map/broadcast_in_dim | solution.py:185
  (25 shorter events, 0.1 us)
Async XLA Ops:
  8.0 121.7 %all-gather.4.cloned.1.call-start = ((), (), s32[]{:S(2)}) async-start(), calls=%async_computation.4 | async-start | bytes 10649600 | tf_op jit(solution)/shard_map/all_gather | solution.py:123
  141.1 2.1 copy-start.2
  170.9 5.9 %copy-start.3 = (f32[1,512,1024]{2,1,0:T(8,128)S(1)}, f32[1,512,1024]{2,1,0:T(8,128)}, u32[]{:S(2)}) copy-start(f32[1,512,1024]{2,1,0:T(8,128)} %param.13) | copy-start | bytes 6291460
  170.9 5.9 %copy-start.13 = (f32[1024]{0:T(1024)S(1)}, f32[1024]{0:T(1024)}, u32[]{:S(2)}) copy-start(f32[1024]{0:T(1024)} %param.14) | copy-start | bytes 12292
  172.1 28.8 %all-to-all-start.2 = ((f32[32,8,1024]{2,1,0:T(8,128)}), f32[32,8,1024]{2,1,0:T(8,128)S(1)}, u32[]{:S(2)}, u32[]{:S(2)}) async-start(f32[32,8,1024]{2,1,0:T(8,128)} %broadcast_in_dim.38), calls=%async_computation.2 | async-start | bytes 2097152 | tf_op jit(solution)/shard_map/all_to_all | solution.py:41
  176.8 110.5 %all-gather.6.cloned.1.call-start = ((), (), s32[]{:S(2)}) async-start(), calls=%async_computation.5 | async-start | bytes 6291456 | tf_op jit(solution)/shard_map/all_gather | solution.py:29
  177.8 14.3 %collective-permute-start = (f32[513,1]{1,0:T(8,128)}, f32[513,1]{1,0:T(8,128)S(1)}, u32[]{:S(2)}, u32[]{:S(2)}) collective-permute-start(f32[513,1]{1,0:T(8,128)} %get-tuple-element.140), channel_id=1, source_target_pairs={{0,1},{1,2},{2,3},{3,4},{4,5},{5,6},{6,7},{7,8},{8,9},{9,10},{10,1... | collective-permute-start | bytes 6164 | tf_op jit(solution)/shard_map/ppermute | solution.py:22
  181.1 13.4 %collective-permute-start.1 = (f32[513,1]{1,0:T(8,128)}, f32[513,1]{1,0:T(8,128)}, u32[]{:S(2)}, u32[]{:S(2)}) collective-permute-start(f32[513,1]{1,0:T(8,128)} %get-tuple-element.139), channel_id=1, source_target_pairs={{1,0},{2,1},{3,2},{4,3},{5,4},{6,5},{7,6},{8,7},{9,8},{10,9},{11,1... | collective-permute-start | bytes 6164 | tf_op jit(solution)/shard_map/ppermute | solution.py:23
  182.6 5.2 %copy-start.5 = (f32[1,5,16,1024]{3,2,1,0:T(8,128)S(1)}, f32[1,5,16,1024]{3,2,1,0:T(8,128)}, u32[]{:S(2)}) copy-start(f32[1,5,16,1024]{3,2,1,0:T(8,128)} %param.19) | copy-start | bytes 983044
  188.6 9.1 %copy-start.15 = (f32[1024]{0:T(1024)S(1)}, f32[1024]{0:T(1024)}, u32[]{:S(2)}) copy-start(f32[1024]{0:T(1024)} %param.15) | copy-start | bytes 12292
  192.1 0.7 copy-start.12
  210.6 1.5 copy-start.7
  212.1 59.3 %copy-start.14 = (s32[512]{0:T(512)S(1)}, s32[512]{0:T(512)}, u32[]{:S(2)}) copy-start(s32[512]{0:T(512)} %param.17) | copy-start | bytes 6148
  217.9 159.4 %collective-permute-start.2 = (f32[1130496]{0:T(1024)}, f32[1130496]{0:T(1024)}, u32[]{:S(2)}, u32[]{:S(2)}) collective-permute-start(f32[1130496]{0:T(1024)} %maximum_select_fusion), channel_id=1, source_target_pairs={{0,64},{64,0},{1,65},{65,1},{2,66},{66,2},{3,67},{67,3},{4,68},{68... | collective-permute-start | bytes 13565960 | tf_op jit(solution)/shard_map/ppermute | solution.py:81
  287.3 1.6 slice-start
  382.7 5.0 %copy-start.6 = (f32[1,5,16,1024]{3,2,1,0:T(8,128)S(1)}, f32[1,5,16,1024]{3,2,1,0:T(8,128)}, u32[]{:S(2)}) copy-start(f32[1,5,16,1024]{3,2,1,0:T(8,128)} %param.19) | copy-start | bytes 983044
Sparse Core Ops, SparseCore 0:
  11.1 118.5 all-gather.3
Sparse Core Ops, SparseCore 1:
  201.0 86.3 all-gather.5
where the time goes:
time: 407 us; the launch traced here: 406 us
  waiting for transfers between devices  223 us (55%)
  starting transfers between devices  61.7 us (15%)
  local copies, waits for them, and re-layouts  40.8 us (10%)
  blocking collectives  35.9 us (9%)
  other arithmetic  28.5 us (7%)
  between operations  15.6 us (4%)
    all_gather x1, waiting for transfers between devices, body(): full_hidden = lax.all_gather(hidden_narrow, TILE, axis=1, tiled=True)  120 us
    ppermute x1, waiting for transfers between devices, partner(): lax.ppermute(value, axis, [(i, i ^ 1 << distance) for i in range(lax.axis...  81.9 us
    ppermute x1, starting transfers between devices, partner(): lax.ppermute(value, axis, [(i, i ^ 1 << distance) for i in range(lax.axis...  53.5 us
    all_to_all x1, blocking collectives, summed_rows(): return jnp.sum(lax.all_to_all(own, far, 0, 0, tiled=True), axis=0)  21.2 us
    all_gather x1, waiting for transfers between devices, from_root(): lax.all_gather(value, axis)  15.9 us
    broadcast_in_dim x3, other arithmetic, body(): return (fields_next[None], out_next[None], hidden_next[None])  14.3 us
    another operation x5, local copies, waits for them, and re-layouts  11.7 us
    slice x2, local copies, waits for them, and re-layouts, body(): other_out = received[:out_length].reshape(own_out.shape)  9.46 us
  transfers between devices with their start and end apart: 6, of which 5 were waited for; matrix products, arithmetic and copies ran while one was open for 7% of the time, Pallas kernels for 0%

commit v1 on v0

v1 whole, which is shorter than its diff:
```python
import itertools

import jax
import jax.numpy as jnp
from jax import lax
from jax.experimental import pallas as pl
from jax.experimental.pallas import tpu as pltpu
from jax.sharding import Mesh
from jax.sharding import PartitionSpec as P

BATCH = 512
LAYERS = 5
TILE = ("tile_0", "tile_1", "tile_2", "tile_3")
CHIPS = ("tile_0", "tile_1", "tile_2")
ALL = ("role", *TILE)

momentum_decay = 0.9
step_size = 0.1


def to_trainer(value):
    return lax.ppermute(value, "role", [(0, 1)])


def to_solver(value):
    return lax.ppermute(value, "role", [(1, 0)])


def swapped(value, axis):
    return lax.ppermute(value, axis, [(0, 1), (1, 0)])


def from_everyone(value, axes):
    copies = jnp.broadcast_to(value, (lax.axis_size(axes), *value.shape))
    return lax.all_to_all(copies, axes, split_axis=0, concat_axis=0, tiled=True)


def ordered(mine, other, place, axis):
    return jnp.where(
        place == 0, jnp.stack([mine, other], axis), jnp.stack([other, mine], axis)
    )


def advance(fields, before, after, velocity, growth):
    states = jnp.concatenate([before[:BATCH, -1:], fields, after[:, :1]], axis=1)
    speeds = jnp.concatenate([before[BATCH, -1:], velocity])
    outflow = (
        jnp.maximum(speeds, 0.0) * states[:, :-1] + jnp.minimum(speeds, 0.0) * states[:, 1:]
    )
    carried = fields - outflow[:, 1:] + outflow[:, :-1]
    return carried + growth * carried * (1.0 - carried)


def along(value, plane_axis, step):
    sizes = [lax.axis_size(name) for name in ALL]
    pairs = []
    for role, pair, x, z, core in itertools.product(*map(range, sizes)):
        if role == 0:
            continue
        to_x, to_z = (x, (z + step) % sizes[3])
        if (core == 0) == (plane_axis == 0):
            to_x, to_z = ((x + step) % sizes[2], z)
        pairs.append((flat(sizes, (role, pair, x, z, core)), flat(sizes, (role, pair, to_x, to_z, core))))
    return lax.ppermute(value, ALL, pairs)


def flat(sizes, place):
    index = 0
    for size, coordinate in zip(sizes, place):
        index = index * size + coordinate
    return index


def trainers_swap(value, axis):
    sizes = [lax.axis_size(name) for name in ALL]
    which = ALL.index(axis)
    pairs = []
    for place in itertools.product(*map(range, sizes)):
        if place[0] == 1:
            other = list(place)
            other[which] = 1 - other[which]
            pairs.append((flat(sizes, place), flat(sizes, other)))
    return lax.ppermute(value, ALL, pairs)


def tied(value, *others):
    return lax.optimization_barrier((value, *others))[0]


UNITS = 16
COLUMNS = 256


def forward_kernel(*refs):
    pieces, features_ref = refs[:8], refs[8]
    inputs_ref, slopes_ref, weights_out, weights, first_sem, rest_sem, out_sem = refs[9:]
    pair = lax.axis_index("tile_0")
    x = lax.axis_index("tile_1")
    z = lax.axis_index("tile_2")
    core = lax.axis_index("tile_3")

    def start(first, layers, sem):
        for number, piece in enumerate(pieces):
            far = number % 4
            owner = core if number < 4 else 1 - core

            def step(index, carry, piece=piece, far=far, owner=owner):
                near = index // 2
                plane = lax.rem(pair + lax.rem(index, 2), 2)
                by_x = jnp.where(owner == 0, far, near)
                by_z = jnp.where(owner == 0, near, far)
                row = ((plane * 4 + lax.rem(x - by_x + 4, 4)) * 4 + lax.rem(z - by_z + 4, 4)) * 2 + owner
                row = pl.multiple_of(row * UNITS, UNITS)
                pltpu.make_async_copy(
                    piece.at[near, lax.rem(index, 2), pl.ds(first, layers)],
                    weights.at[pl.ds(first, layers), pl.ds(row, UNITS)],
                    sem,
                ).start()
                return carry

            lax.fori_loop(0, 8, step, 0)

    def finish(first, layers, sem):
        part = weights.at[pl.ds(first, layers)]
        pltpu.make_async_copy(part, part, sem).wait()

    start(0, 1, first_sem)
    start(1, LAYERS - 1, rest_sem)
    inputs_ref[0] = features_ref[...]
    finish(0, 1, first_sem)
    for layer in range(LAYERS):
        if layer == 1:
            finish(1, LAYERS - 1, rest_sem)
            keep = pltpu.make_async_copy(weights, weights_out, out_sem)
            keep.start()

        def block(index, carry, layer=layer):
            columns = pl.ds(pl.multiple_of(index * COLUMNS, COLUMNS), COLUMNS)
            total = jnp.dot(
                inputs_ref[layer], weights[layer, :, columns], preferred_element_type=jnp.float32
            )
            logistic = 1.0 / (1.0 + jnp.exp(-total))
            inputs_ref[layer + 1, :, columns] = (total * logistic).astype(jnp.bfloat16)
            slopes_ref[layer, :, columns] = logistic * (1.0 + total * (1.0 - logistic))
            return carry

        lax.fori_loop(0, weights.shape[2] // COLUMNS, block, 0)
    keep.wait()


def forward(pieces, features):
    rows, width = features.shape
    return pl.pallas_call(
        forward_kernel,
        out_shape=(
            jax.ShapeDtypeStruct((LAYERS + 1, rows, width), jnp.bfloat16),
            jax.ShapeDtypeStruct((LAYERS, rows, width), jnp.float32),
            jax.ShapeDtypeStruct((LAYERS, width, width), jnp.bfloat16),
        ),
        in_specs=[pl.BlockSpec(memory_space=pl.ANY)] * 8 + [pl.BlockSpec(memory_space=pltpu.VMEM)],
        out_specs=(
            pl.BlockSpec(memory_space=pltpu.VMEM),
            pl.BlockSpec(memory_space=pltpu.VMEM),
            pl.BlockSpec(memory_space=pl.ANY),
        ),
        scratch_shapes=[
            pltpu.VMEM((LAYERS, width, width), jnp.bfloat16),
            pltpu.SemaphoreType.DMA(()),
            pltpu.SemaphoreType.DMA(()),
            pltpu.SemaphoreType.DMA(()),
        ],
        compiler_params=pltpu.CompilerParams(vmem_limit_bytes=40 * 1024 * 1024),
        cost_estimate=pl.CostEstimate(
            flops=2 * LAYERS * rows * width * width,
            bytes_accessed=LAYERS * width * (4 * width + 6 * rows),
            transcendentals=LAYERS * rows * width,
        ),
    )(*pieces, features)


def body(fields_pair, velocity, growth, features, assignment, out_pair, hidden_pair):
    solver_side = lax.axis_index("role") == 0
    core = lax.axis_index("tile_3")
    chip = lax.axis_index(CHIPS)
    fields = fields_pair[0]
    own_out = out_pair[0]
    own_hidden = hidden_pair[0]
    units = own_hidden.shape[1]
    width = own_hidden.shape[2]
    half = BATCH // 2

    hidden_narrow = own_hidden.astype(jnp.bfloat16)
    out_narrow = own_out.astype(jnp.bfloat16)
    packed = jnp.concatenate([hidden_narrow.reshape(-1, width), out_narrow], axis=0)
    cut = 552
    edge = jnp.concatenate(
        [fields[:, -128:], jnp.broadcast_to(velocity[None, -128:], (8, 128))], axis=0
    )

    near = jnp.stack([hidden_narrow, trainers_swap(hidden_narrow, "tile_0")])
    momentum_a = to_trainer(packed[:cut])
    count = lax.axis_size(TILE)
    up = [(i, (i + 1) % count) for i in range(count)]
    down = [(j, i) for i, j in up]
    before = lax.ppermute(edge, TILE, up)
    after = lax.ppermute(fields[:, :128], TILE, down)
    stage = [near, *(along(near, 1, step) for step in (1, 2, 3))]
    stage, before, after, momentum_a = lax.optimization_barrier((stage, before, after, momentum_a))

    momentum_b = to_trainer(tied(packed[cut:], momentum_a))
    far = jnp.stack(stage)
    mine = [far, *(along(far, 0, step) for step in (1, 2, 3))]
    advanced = advance(fields, before, after, velocity, growth)
    carried = jnp.take(advanced.astype(jnp.bfloat16), assignment, axis=0)
    other = [trainers_swap(piece, "tile_3") for piece in mine]
    mine, other, carried, momentum_b = lax.optimization_barrier((mine, other, carried, momentum_b))
    next_batch = to_trainer(carried)
    inputs, slopes, weights = forward(
        [*mine, *other], lax.dynamic_slice_in_dim(features, core * half, half, 0)
    )
    activation = inputs[LAYERS]

    last = ordered(activation, swapped(activation, "tile_3"), core, 0).reshape(BATCH, width)
    predicted = jnp.dot(last, out_narrow, preferred_element_type=jnp.float32)
    residual = ((predicted - fields) / BATCH).astype(jnp.bfloat16)
    partial_grad = lax.dot_general(
        residual, out_narrow, (((1,), (1,)), ((), ())), preferred_element_type=jnp.float32
    )
    grad_out = lax.dot_general(
        last, residual, (((0,), (0,)), ((), ())), preferred_element_type=jnp.float32
    )
    grad_out_far = to_solver(grad_out.astype(jnp.bfloat16))

    kept = lax.dynamic_slice_in_dim(partial_grad, core * half, half, 0)
    given = lax.dynamic_slice_in_dim(partial_grad, (1 - core) * half, half, 0)
    chip_sum = kept + swapped(given, "tile_3")
    chips = lax.axis_size(CHIPS)
    rows = half // chips
    upstream = lax.all_to_all(
        chip_sum.reshape(chips, rows, width), CHIPS, split_axis=0, concat_axis=0, tiled=True
    ).sum(axis=0)
    upstream, next_batch = lax.optimization_barrier((upstream, next_batch))
    own_factor = lax.dynamic_slice_in_dim(slopes[LAYERS - 1], chip * rows, rows, 0)
    own_slope = (upstream * own_factor).astype(jnp.bfloat16)
    slope = from_everyone(own_slope, CHIPS).reshape(half, width)

    gradients = []
    for layer in reversed(range(LAYERS)):
        own_inputs = lax.dynamic_slice_in_dim(inputs[layer], chip * 2 * units, 2 * units, 1)
        gradients.append(
            lax.dot_general(
                own_inputs, slope, (((0,), (0,)), ((), ())), preferred_element_type=jnp.float32
            )
        )
        if layer > 0:
            upstream = lax.dot_general(
                slope, weights[layer], (((1,), (1,)), ((), ())), preferred_element_type=jnp.float32
            )
            slope = (upstream * slopes[layer - 1]).astype(jnp.bfloat16)
    pair_grad = jnp.stack(gradients[::-1])
    kept = lax.dynamic_slice_in_dim(pair_grad, core * units, units, 1)
    given = lax.dynamic_slice_in_dim(pair_grad, (1 - core) * units, units, 1)
    grad_hidden = kept + swapped(given, "tile_3")
    grad_hidden_far = to_solver(grad_hidden.astype(jnp.bfloat16))

    hidden_rows = packed.shape[0] - own_out.shape[0]
    momentum = jnp.concatenate([momentum_a, momentum_b], axis=0)
    other_hidden = momentum[:hidden_rows].reshape(own_hidden.shape).astype(jnp.float32)
    other_out = momentum[hidden_rows:].astype(jnp.float32)
    out_next = jnp.where(
        solver_side,
        momentum_decay * own_out + grad_out_far.astype(jnp.float32),
        own_out - step_size * (momentum_decay * other_out + grad_out),
    )
    hidden_next = jnp.where(
        solver_side,
        momentum_decay * own_hidden + grad_hidden_far.astype(jnp.float32),
        own_hidden - step_size * (momentum_decay * other_hidden + grad_hidden),
    )
    fields_next = jnp.where(solver_side, advanced, next_batch.astype(jnp.float32))
    return (fields_next[None], out_next[None], hidden_next[None])


def solution(mesh):
    finer = Mesh(
        mesh.devices.reshape(mesh.shape["role"], 2, 4, 4, 2),
        ALL,
    )
    in_specs = (
        P("role", None, TILE),
        P(TILE),
        P(TILE),
        P(),
        P(),
        P("role", None, TILE),
        P("role", None, TILE, None),
    )
    out_specs = (P("role", None, TILE), P("role", None, TILE), P("role", None, TILE, None))
    return jax.shard_map(body, mesh=finer, in_specs=in_specs, out_specs=out_specs, check_vma=False)
```

time: 407 us -> 232 us (0.57)
  waiting for transfers between devices: 223 us -> 71.8 us
  blocking collectives: 35.9 us -> 0 us
  matrix products: 0 us -> 29.4 us
  local copies, waits for them, and re-layouts: 40.8 us -> 13 us
  between operations: 15.6 us -> 1.06 us
  Pallas kernels: 0 us -> 13.5 us
  starting transfers between devices: 61.7 us -> 69.8 us
    all_gather x2 -> x0, waiting for transfers between devices: 136 us -> none  [the longest x1 120 us: body(): full_hidden = lax.all_gather(hidden_narrow, TILE, axis=1, tiled=True)]
    ppermute x3 -> x21, waiting for transfers between devices: 87.1 us -> 42.2 us  [the longest x3 17.6 us: to_trainer(): return lax.ppermute(value, 'role', [(0, 1)])]
    all_to_all x3 -> x0, blocking collectives: 35.9 us -> none  [the longest x1 21.2 us: summed_rows(): return jnp.sum(lax.all_to_all(own, far, 0, 0, tiled=True), axis=0)]
    all_to_all x1 -> x2, waiting for transfers between devices: 0.01 us -> 29.6 us  [the longest x1 26.7 us: body(): lax.all_to_all(chip_sum.reshape(chips, rows, width), CHIPS, split_axis=0,...]
    dot_general x0 -> x11, matrix products: none -> 29.4 us  [the longest x5 11.5 us: body(): lax.dot_general(own_inputs, slope, (((0,), (0,)), ((), ())), preferred_el...]
    pallas_call x0 -> x1, Pallas kernels: none -> 13.5 us  [forward(): pl.pallas_call(forward_kernel, out_shape=(jax.ShapeDtypeStruct((LAYERS +...]
    another operation x5 -> x0, local copies, waits for them, and re-layouts: 11.7 us -> none
    all_to_all x1 -> x2, starting transfers between devices: 4.7 us -> 11.3 us  [the longest x1 7.17 us: body(): lax.all_to_all(chip_sum.reshape(chips, rows, width), CHIPS, split_axis=0,...]
  transfers between devices with their start and end apart: 6 -> 23, of which waited for: 5 -> 8; matrix products, arithmetic and copies ran while one was open for 7% -> 23% of each run, Pallas kernels for 0% -> 0%
where the time goes in v1:
time: 232 us; the launch traced here: 228 us
  waiting for transfers between devices  71.8 us (31%)
  starting transfers between devices  69.8 us (30%)
  matrix products  29.4 us (13%)
  other arithmetic  29 us (12%)
  Pallas kernels  13.5 us (6%)
  local copies, waits for them, and re-layouts  13 us (6%)
    ppermute x3, starting transfers between devices, to_trainer(): return lax.ppermute(value, 'role', [(0, 1)])  35.6 us
    all_to_all x1, waiting for transfers between devices, body(): lax.all_to_all(chip_sum.reshape(chips, rows, width), CHIPS, split_axis=0,...  26.7 us
    ppermute x3, waiting for transfers between devices, to_trainer(): return lax.ppermute(value, 'role', [(0, 1)])  17.6 us
    ppermute x2, waiting for transfers between devices, to_solver(): return lax.ppermute(value, 'role', [(1, 0)])  14.7 us
    pallas_call x1, Pallas kernels, forward(): pl.pallas_call(forward_kernel, out_shape=(jax.ShapeDtypeStruct((LAYERS +...  13.5 us
    dot_general x5, matrix products, body(): lax.dot_general(own_inputs, slope, (((0,), (0,)), ((), ())), preferred_el...  11.5 us
    broadcast_in_dim x3, other arithmetic, body(): return (fields_next[None], out_next[None], hidden_next[None])  9.84 us
    dot_general x3, matrix products, body(): lax.dot_general(slope, weights[layer], (((1,), (1,)), ((), ())), preferre...  8.95 us
  transfers between devices with their start and end apart: 23, of which 8 were waited for; matrix products, arithmetic and copies ran while one was open for 23% of the time, Pallas kernels for 0%

profile of v1, /device:TPU:1, one launch (start us, length us, event | category | flops | bytes accessed | tf_op | source)
XLA Modules:
  0.0 227.6 jit_solution(15927756315752236862)
XLA Ops:
  0.6 1.2 fusion.88
  1.9 2.5 %bitcast_convert_fusion = bf16[1024,1024]{1,0:T(8,128)(2,1)S(1)} fusion(f32[1,1024,1024]{2,1,0:T(8,128)} %param.12), kind=kLoop, calls=%fused_computation.3 | loop fusion | flops 1048576 | bytes 6291456 | tf_op jit(solution)/shard_map/convert_element_type | solution.py:193
  4.4 1.4 fusion.86
  6.1 5.7 %collective-permute-start.6 = (bf16[552,1024]{1,0:T(8,128)(2,1)S(1)}, bf16[552,1024]{1,0:T(8,128)(2,1)S(1)}, u32[]{:S(2)}, u32[]{:S(2)}) collective-permute-start(bf16[552,1024]{1,0:T(8,128)(2,1)S(1)} %get-tuple-element.59), channel_id=1, source_target_pairs={{0,64},{1,65},{2,66},{3,67},{4,68},{5,69},{6,70},{7,71},{8,72},{9,... | collective-permute-start | bytes 3391496 | tf_op jit(solution)/shard_map/ppermute | solution.py:22
  16.7 3.4 %collective-permute-done.5 = f32[512,128]{1,0:T(8,128)S(1)} collective-permute-done((f32[512,128]{1,0:T(8,128)S(1)}, f32[512,128]{1,0:T(8,128)S(1)}, u32[]{:S(2)}, u32[]{:S(2)}) %collective-permute-start.5) | collective-permute-done | bytes 262176 | tf_op jit(solution)/shard_map/ppermute | solution.py:206
  20.2 4.9 %collective-permute-done.4 = f32[520,128]{1,0:T(8,128)S(1)} collective-permute-done((f32[520,128]{1,0:T(8,128)S(1)}, f32[520,128]{1,0:T(8,128)S(1)}, u32[]{:S(2)}, u32[]{:S(2)}) %collective-permute-start.4) | collective-permute-done | bytes 266272 | tf_op jit(solution)/shard_map/ppermute | solution.py:205
  25.1 10.2 %collective-permute-done.6 = bf16[552,1024]{1,0:T(8,128)(2,1)S(1)} collective-permute-done((bf16[552,1024]{1,0:T(8,128)(2,1)S(1)}, bf16[552,1024]{1,0:T(8,128)(2,1)S(1)}, u32[]{:S(2)}, u32[]{:S(2)}) %collective-permute-start.6) | collective-permute-done | bytes 1130528 | tf_op jit(solution)/shard_map/ppermute | solution.py:22
  36.5 1.8 collective-permute-start.7
  38.2 1.8 collective-permute-start.8
  40.0 1.7 collective-permute-start.9
  42.5 1.8 collective-permute-start.10
  44.4 15.8 %collective-permute-start.14 = (bf16[552,1024]{1,0:T(8,128)(2,1)}, bf16[552,1024]{1,0:T(8,128)(2,1)}, u32[]{:S(2)}, u32[]{:S(2)}) collective-permute-start(bf16[552,1024]{1,0:T(8,128)(2,1)} %get-tuple-element.33), channel_id=1, source_target_pairs={{0,64},{1,65},{2,66},{3,67},{4,68},{5,69},{6,70},{7,71},{8,72},{9,... | collective-permute-start | bytes 3391496 | tf_op jit(solution)/shard_map/ppermute | solution.py:22
  60.2 1.7 collective-permute-start.11
  61.9 1.7 collective-permute-start.12
  63.6 1.8 collective-permute-start.13
  66.1 3.1 %fusion.3 = f32[512,1025]{1,0:T(8,128)S(1)} fusion(f32[512,1024]{1,0:T(8,128)} %bitcast.155, f32[512,1]{1,0:T(8,128)S(1)} %slice.90, f32[512,1]{1,0:T(8,128)S(1)} %bitcast.165, f32[1025]{0:T(1024)S(1)} %get-tuple-element.65, f32[1025]{0:T(1024)S(1)} %get-tuple-element.64), kind=kLoop, calls=%fused_computation.8 | loop fusion | flops 2624000 | bytes 4208648 | tf_op jit(solution)/shard_map/add | solution.py:48
  69.2 2.0 fusion.84
  71.3 2.8 %gather_fusion = bf16[512,1024]{1,0:T(8,128)(2,1)} fusion(bf16[512,1024]{1,0:T(8,128)(2,1)S(1)} %get-tuple-element.49, s32[1024]{0:T(1024)S(1)} %pad_clamp_fusion), kind=kCustom, calls=%fused_computation | custom fusion | bytes 2099200 | tf_op jit(solution)/shard_map/jit(_take)/gather | solution.py:214
  74.0 2.4 %broadcast_select_fusion = bf16[512,1024]{1,0:T(8,128)(2,1)} fusion(bf16[512,1024]{1,0:T(8,128)(2,1)} %gather_fusion, pred[512]{0:T(512)(128)(4,1)S(1)} %compare_and_fusion), kind=kLoop, calls=%fused_computation.56 | loop fusion | flops 524288 | bytes 2097664 | tf_op jit(solution)/shard_map/jit(_take)/select_n | solution.py:214
  76.4 7.4 %collective-permute-done.14 = bf16[552,1024]{1,0:T(8,128)(2,1)} collective-permute-done((bf16[552,1024]{1,0:T(8,128)(2,1)}, bf16[552,1024]{1,0:T(8,128)(2,1)}, u32[]{:S(2)}, u32[]{:S(2)}) %collective-permute-start.14) | collective-permute-done | bytes 1130528 | tf_op jit(solution)/shard_map/ppermute | solution.py:22
  83.8 13.5 %shard_map.94 = (bf16[6,256,1024]{2,1,0:T(8,128)(2,1)S(1)}, f32[5,256,1024]{2,1,0:T(8,128)}, bf16[5,1024,1024]{2,1,0:T(8,128)(2,1)}) custom-call(bf16[4,2,5,16,1024]{4,3,2,1,0:T(8,128)(2,1)S(1)} %pad_maximum_fusion.1.refs_0_, bf16[4,2,5,16,1024]{4,3,2,1,0:T(8,128)(2,1)} %collective-permute-done.7.refs_1_, ...), custom_call_target="tpu_custom_call" | custom-call | flops 2684354560 | bytes 28835840 | tf_op jit(solution)/shard_map/pallas_call | solution.py:153
  97.3 1.9 fusion.85
  100.0 1.5 collective-permute-done.15
  102.4 1.8 maximum_select_fusion
  104.2 3.6 %multiply_convert_fusion = bf16[512,1024]{1,0:T(8,128)(2,1)S(1)} fusion(bf16[512,1024]{1,0:T(8,128)(2,1)S(1)} %bitcast.156, f32[1,1024,1024]{2,1,0:T(8,128)} %param.12, f32[1,512,1024]{2,1,0:T(8,128)S(1)} %copy-done.5), kind=kOutput, calls=%fused_computation.28 | convolution fusion | flops 1076363264 | bytes 8388608 | tf_op jit(solution)/shard_map/dot_general | solution.py:224
  107.8 1.3 fusion.90
  109.7 14.0 %collective-permute-start.17 = (bf16[512,1024]{1,0:T(8,128)(2,1)}, bf16[512,1024]{1,0:T(8,128)(2,1)}, u32[]{:S(2)}, u32[]{:S(2)}) collective-permute-start(bf16[512,1024]{1,0:T(8,128)(2,1)} %broadcast_select_fusion), channel_id=1, source_target_pairs={{0,64},{1,65},{2,66},{3,67},{4,68},{5,69},{6,70},{7,71},{8,72},{9,... | collective-permute-start | bytes 3145736 | tf_op jit(solution)/shard_map/ppermute | solution.py:22
  123.7 1.1 add_bitcast_fusion
  124.8 7.2 %all-to-all-start = ((f32[32,8,1024]{2,1,0:T(8,128)}), f32[32,8,1024]{2,1,0:T(8,128)S(1)}, u32[]{:S(2)}, u32[]{:S(2)}) async-start(f32[32,8,1024]{2,1,0:T(8,128)} %add_bitcast_fusion), calls=%async_computation | async-start | bytes 2097152 | tf_op jit(solution)/shard_map/all_to_all | solution.py:239
  132.0 2.3 %slice.98 = f32[1,256,1024]{2,1,0:T(8,128)} slice(f32[5,256,1024]{2,1,0:T(8,128)} %get-tuple-element.47), slice={[4:5], [0:256], [0:1024]} | slice | bytes 2097152 | tf_op jit(solution)/shard_map/slice | solution.py:243
  134.4 26.7 %all-to-all-done = f32[32,8,1024]{2,1,0:T(8,128)S(1)} async-done(((f32[32,8,1024]{2,1,0:T(8,128)}), f32[32,8,1024]{2,1,0:T(8,128)S(1)}, u32[]{:S(2)}, u32[]{:S(2)}) %all-to-all-start) | async-done | bytes 1048608 | tf_op jit(solution)/shard_map/all_to_all | solution.py:239
  162.7 4.1 %all-to-all-start.1 = ((bf16[32,8,1024]{2,1,0:T(8,128)(2,1)}), bf16[32,8,1024]{2,1,0:T(8,128)(2,1)S(1)}, u32[]{:S(2)}, u32[]{:S(2)}) async-start(bf16[32,8,1024]{2,1,0:T(8,128)(2,1)} %broadcast_in_dim.39), calls=%async_computation.1 | async-start | bytes 1048576 | tf_op jit(solution)/shard_map/all_to_all | solution.py:35
  167.8 4.1 %fusion.89 = (bf16[1024,1024]{1,0:T(8,128)(2,1)}, f32[1024,1024]{1,0:T(8,128)}) fusion(bf16[512,1024]{1,0:T(8,128)(2,1)S(1)} %bitcast.157, bf16[512,1024]{1,0:T(8,128)(2,1)S(1)} %copy-done.10), kind=kOutput, calls=%fused_computation.102 | convolution fusion | flops 1074790400 | bytes 8388608 | tf_op jit(solution)/shard_map/dot_general | solution.py:229
  171.9 1.3 collective-permute-start.18
  173.2 2.9 %all-to-all-done.1 = bf16[32,8,1024]{2,1,0:T(8,128)(2,1)S(1)} async-done(((bf16[32,8,1024]{2,1,0:T(8,128)(2,1)}), bf16[32,8,1024]{2,1,0:T(8,128)(2,1)S(1)}, u32[]{:S(2)}, u32[]{:S(2)}) %all-to-all-start.1) | async-done | bytes 524320 | tf_op jit(solution)/shard_map/all_to_all | solution.py:35
  176.1 2.8 %fusion.42 = bf16[256,1024]{1,0:T(8,128)(2,1)S(1)} fusion(bf16[5,1024,1024]{2,1,0:T(8,128)(2,1)} %get-tuple-element.48, f32[5,256,1024]{2,1,0:T(8,128)} %get-tuple-element.47, bf16[32,8,1024]{2,1,0:T(8,128)(2,1)S(1)} %all-to-all-done.1), kind=kOutput, calls=%fused_computation.39 | convolution fusion | flops 537395200 | bytes 4194304 | tf_op jit(solution)/shard_map/dot_general | solution.py:256
  178.9 2.6 %fusion.39 = bf16[256,1024]{1,0:T(8,128)(2,1)S(1)} fusion(bf16[256,1024]{1,0:T(8,128)(2,1)S(1)} %fusion.42, bf16[5,1024,1024]{2,1,0:T(8,128)(2,1)} %get-tuple-element.48, f32[5,256,1024]{2,1,0:T(8,128)} %get-tuple-element.47), kind=kOutput, calls=%fused_computation.38 | convolution fusion | flops 537395200 | bytes 4194304 | tf_op jit(solution)/shard_map/dot_general | solution.py:256
  181.5 3.6 %fusion.36 = bf16[256,1024]{1,0:T(8,128)(2,1)} fusion(bf16[256,1024]{1,0:T(8,128)(2,1)S(1)} %fusion.39, bf16[5,1024,1024]{2,1,0:T(8,128)(2,1)} %get-tuple-element.48, f32[5,256,1024]{2,1,0:T(8,128)} %get-tuple-element.47), kind=kOutput, calls=%fused_computation.37 | convolution fusion | flops 537395200 | bytes 4194304 | tf_op jit(solution)/shard_map/dot_general | solution.py:256
  185.1 3.7 %fusion.55 = f32[5,32,1024]{2,1,0:T(8,128)} fusion(bf16[256,1024]{1,0:T(8,128)(2,1)} %fusion.36, bf16[5,1024,1024]{2,1,0:T(8,128)(2,1)} %get-tuple-element.48, f32[5,256,1024]{2,1,0:T(8,128)} %get-tuple-element.47, bf16[1,256,1024]{2,1,0:T(8,128)(2,1)} %get-tuple-element.56, s32[]{:T(128)S(6)} %select_n.87), kind=kOutput, calls=%fused_computation.50 | convolution fusion | flops 554172416 | bytes 3866628 | tf_op jit(solution)/shard_map/dot_general | solution.py:251
  188.8 2.1 fusion.51
  190.9 2.2 fusion.50
  193.0 1.8 fusion.49
  194.8 1.8 fusion.48
  197.6 3.1 %collective-permute-start.19 = (f32[5,16,1024]{2,1,0:T(8,128)S(1)}, f32[5,16,1024]{2,1,0:T(8,128)S(1)}, u32[]{:S(2)}, u32[]{:S(2)}) collective-permute-start(f32[5,16,1024]{2,1,0:T(8,128)S(1)} %constant_dynamic-slice_fusion), channel_id=1, source_target_pairs={{0,1},{1,0},{2,3},{3,2},{4,5},{5,4},{6,7},{7,6},{8,9},{9,8},{10,11... | collective-permute-start | bytes 983048 | tf_op jit(solution)/shard_map/ppermute | solution.py:30
  200.7 3.0 %select_bitcast_fusion = f32[1,512,1024]{2,1,0:T(8,128)} fusion(f32[512,1024]{1,0:T(8,128)S(1)} %copy-done.8, bf16[512,1024]{1,0:T(8,128)(2,1)} %collective-permute-done.17, pred[]{:T(512)S(6)} %eq.6), kind=kLoop, calls=%fused_computation.27 | loop fusion | flops 1048576 | bytes 5242881 | tf_op jit(solution)/shard_map/broadcast_in_dim | solution.py:281
  204.7 1.3 collective-permute-start.20
  206.0 14.7 %collective-permute-done.18 = bf16[1024,1024]{1,0:T(8,128)(2,1)} collective-permute-done((bf16[1024,1024]{1,0:T(8,128)(2,1)}, bf16[1024,1024]{1,0:T(8,128)(2,1)}, u32[]{:S(2)}, u32[]{:S(2)}) %collective-permute-start.18) | collective-permute-done | bytes 2097184 | tf_op jit(solution)/shard_map/ppermute | solution.py:26
  220.8 6.0 %fusion.2 = f32[1,1024,1024]{2,1,0:T(8,128)} fusion(f32[1,1024,1024]{2,1,0:T(8,128)S(1)} %copy-done.2, f32[1024,1024]{1,0:T(8,128)S(1)} %copy-done.3, bf16[1024,1024]{1,0:T(8,128)(2,1)} %collective-permute-done.18, bf16[552,1024]{1,0:T(8,128)(2,1)} %collective-permute-done.14, bf16[552,1024]{1,0:T(8,128)(2,1)} %copy-done.13, pred[]{:T(512)S(6)} %eq.6), kind=kLoop, calls=%fused_computation.6 | loop fusion | flops 12582912 | bytes 16941056 | tf_op jit(solution)/shard_map/broadcast_in_dim | solution.py:281
  (86 shorter events, 15.7 us)
Async XLA Ops:
  0.6 41.1 %copy-start = (bf16[512,1024]{1,0:T(8,128)(2,1)S(1)}, bf16[512,1024]{1,0:T(8,128)(2,1)}, u32[]{:S(2)}) copy-start(bf16[512,1024]{1,0:T(8,128)(2,1)} %param.10) | copy-start | bytes 3145732
  4.4 1.7 copy-start.6
  4.4 10.2 %copy-start.20 = (f32[1024]{0:T(1024)S(1)}, f32[1024]{0:T(1024)}, u32[]{:S(2)}) copy-start(f32[1024]{0:T(1024)} %param.8) | copy-start | bytes 12292
  6.1 29.2 %collective-permute-start.6 = (bf16[552,1024]{1,0:T(8,128)(2,1)S(1)}, bf16[552,1024]{1,0:T(8,128)(2,1)S(1)}, u32[]{:S(2)}, u32[]{:S(2)}) collective-permute-start(bf16[552,1024]{1,0:T(8,128)(2,1)S(1)} %get-tuple-element.59), channel_id=1, source_target_pairs={{0,64},{1,65},{2,66},{3,67},{4,68},{5,69},{6,70},{7,71},{8,72},{9,... | collective-permute-start | bytes 3391496 | tf_op jit(solution)/shard_map/ppermute | solution.py:22
  11.8 2.8 %collective-permute-start = (bf16[5,16,1024]{2,1,0:T(8,128)(2,1)S(1)}, bf16[5,16,1024]{2,1,0:T(8,128)(2,1)S(1)}, u32[]{:S(2)}, u32[]{:S(2)}) collective-permute-start(bf16[5,16,1024]{2,1,0:T(8,128)(2,1)S(1)} %get-tuple-element.63), channel_id=1, source_target_pairs={{64,96},{65,97},{66,98},{67,99},{68,100},{69,101},{70,102},{71,103... | collective-permute-start | bytes 491528 | tf_op jit(solution)/shard_map/ppermute | solution.py:83
  13.5 28.2 %copy-start.18 = (s32[512]{0:T(512)S(1)}, s32[512]{0:T(512)}, u32[]{:S(2)}) copy-start(s32[512]{0:T(512)} %param.11) | copy-start | bytes 6148
  13.5 6.6 %collective-permute-start.5 = (f32[512,128]{1,0:T(8,128)S(1)}, f32[512,128]{1,0:T(8,128)S(1)}, u32[]{:S(2)}, u32[]{:S(2)}) collective-permute-start(f32[512,128]{1,0:T(8,128)S(1)} %get-tuple-element.60), channel_id=1, source_target_pairs={{1,0},{2,1},{3,2},{4,3},{5,4},{6,5},{7,6},{8,7},{9,8},{10,9},{11,1... | collective-permute-start | bytes 786440 | tf_op jit(solution)/shard_map/ppermute | solution.py:206
  14.6 10.4 %collective-permute-start.1 = (bf16[2,5,16,1024]{3,2,1,0:T(8,128)(2,1)S(1)}, bf16[2,5,16,1024]{3,2,1,0:T(8,128)(2,1)S(1)}, u32[]{:S(2)}, u32[]{:S(2)}) collective-permute-start(bf16[2,5,16,1024]{3,2,1,0:T(8,128)(2,1)S(1)} %pad_maximum_fusion.3), channel_id=1, source_target_pairs={{64,66},{65,73},{66,68},{67,75},{68,70},{69,77},{70,64},{71,79},{7... | collective-permute-start | bytes 983048 | tf_op jit(solution)/shard_map/ppermute | solution.py:64
  15.3 9.7 %collective-permute-start.2 = (bf16[2,5,16,1024]{3,2,1,0:T(8,128)(2,1)S(1)}, bf16[2,5,16,1024]{3,2,1,0:T(8,128)(2,1)S(1)}, u32[]{:S(2)}, u32[]{:S(2)}) collective-permute-start(bf16[2,5,16,1024]{3,2,1,0:T(8,128)(2,1)S(1)} %pad_maximum_fusion.3), channel_id=1, source_target_pairs={{64,68},{65,81},{66,70},{67,83},{68,64},{69,85},{70,66},{71,87},{7... | collective-permute-start | bytes 983048 | tf_op jit(solution)/shard_map/ppermute | solution.py:64
  16.0 9.1 %collective-permute-start.3 = (bf16[2,5,16,1024]{3,2,1,0:T(8,128)(2,1)S(1)}, bf16[2,5,16,1024]{3,2,1,0:T(8,128)(2,1)S(1)}, u32[]{:S(2)}, u32[]{:S(2)}) collective-permute-start(bf16[2,5,16,1024]{3,2,1,0:T(8,128)(2,1)S(1)} %pad_maximum_fusion.3), channel_id=1, source_target_pairs={{64,70},{65,89},{66,64},{67,91},{68,66},{69,93},{70,68},{71,95},{7... | collective-permute-start | bytes 983048 | tf_op jit(solution)/shard_map/ppermute | solution.py:64
  20.2 4.9 %collective-permute-start.4 = (f32[520,128]{1,0:T(8,128)S(1)}, f32[520,128]{1,0:T(8,128)S(1)}, u32[]{:S(2)}, u32[]{:S(2)}) collective-permute-start(f32[520,128]{1,0:T(8,128)S(1)} %pad_maximum_fusion.4), channel_id=1, source_target_pairs={{0,1},{1,2},{2,3},{3,4},{4,5},{5,6},{6,7},{7,8},{8,9},{9,10},{10,1... | collective-permute-start | bytes 798728 | tf_op jit(solution)/shard_map/ppermute | solution.py:205
  35.3 1.0 copy-start.13
  36.5 23.7 %collective-permute-start.7 = (bf16[4,2,5,16,1024]{4,3,2,1,0:T(8,128)(2,1)S(1)}, bf16[4,2,5,16,1024]{4,3,2,1,0:T(8,128)(2,1)}, u32[]{:S(2)}, u32[]{:S(2)}) collective-permute-start(bf16[4,2,5,16,1024]{4,3,2,1,0:T(8,128)(2,1)S(1)} %pad_maximum_fusion.1.refs_0_), channel_id=1, source_target_pairs={{64,72},{65,67},{66,74},{67,69},{68,76},{69,71},{70,78},{71,65},{7... | collective-permute-start | bytes 3932168 | tf_op jit(solution)/shard_map/ppermute | solution.py:64
  38.2 23.7 %collective-permute-start.8 = (bf16[4,2,5,16,1024]{4,3,2,1,0:T(8,128)(2,1)S(1)}, bf16[4,2,5,16,1024]{4,3,2,1,0:T(8,128)(2,1)}, u32[]{:S(2)}, u32[]{:S(2)}) collective-permute-start(bf16[4,2,5,16,1024]{4,3,2,1,0:T(8,128)(2,1)S(1)} %pad_maximum_fusion.1.refs_0_), channel_id=1, source_target_pairs={{64,80},{65,69},{66,82},{67,71},{68,84},{69,65},{70,86},{71,67},{7... | collective-permute-start | bytes 3932168 | tf_op jit(solution)/shard_map/ppermute | solution.py:64
  40.0 23.6 %collective-permute-start.9 = (bf16[4,2,5,16,1024]{4,3,2,1,0:T(8,128)(2,1)S(1)}, bf16[4,2,5,16,1024]{4,3,2,1,0:T(8,128)(2,1)}, u32[]{:S(2)}, u32[]{:S(2)}) collective-permute-start(bf16[4,2,5,16,1024]{4,3,2,1,0:T(8,128)(2,1)S(1)} %pad_maximum_fusion.1.refs_0_), channel_id=1, source_target_pairs={{64,88},{65,71},{66,90},{67,65},{68,92},{69,67},{70,94},{71,69},{7... | collective-permute-start | bytes 3932168 | tf_op jit(solution)/shard_map/ppermute | solution.py:64
  42.5 41.3 %collective-permute-start.10 = (bf16[4,2,5,16,1024]{4,3,2,1,0:T(8,128)(2,1)S(1)}, bf16[4,2,5,16,1024]{4,3,2,1,0:T(8,128)(2,1)}, u32[]{:S(2)}, u32[]{:S(2)}) collective-permute-start(bf16[4,2,5,16,1024]{4,3,2,1,0:T(8,128)(2,1)S(1)} %pad_maximum_fusion.1.refs_0_), channel_id=1, source_target_pairs={{64,65},{65,64},{66,67},{67,66},{68,69},{69,68},{70,71},{71,70},{7... | collective-permute-start | bytes 3932168 | tf_op jit(solution)/shard_map/ppermute | solution.py:83
  44.4 39.5 %collective-permute-start.14 = (bf16[552,1024]{1,0:T(8,128)(2,1)}, bf16[552,1024]{1,0:T(8,128)(2,1)}, u32[]{:S(2)}, u32[]{:S(2)}) collective-permute-start(bf16[552,1024]{1,0:T(8,128)(2,1)} %get-tuple-element.33), channel_id=1, source_target_pairs={{0,64},{1,65},{2,66},{3,67},{4,68},{5,69},{6,70},{7,71},{8,72},{9,... | collective-permute-start | bytes 3391496 | tf_op jit(solution)/shard_map/ppermute | solution.py:22
  60.2 23.6 %collective-permute-start.11 = (bf16[4,2,5,16,1024]{4,3,2,1,0:T(8,128)(2,1)}, bf16[4,2,5,16,1024]{4,3,2,1,0:T(8,128)(2,1)}, u32[]{:S(2)}, u32[]{:S(2)}) collective-permute-start(bf16[4,2,5,16,1024]{4,3,2,1,0:T(8,128)(2,1)} %collective-permute-done.7.refs_1_), channel_id=1, source_target_pairs={{64,65},{65,64},{66,67},{67,66},{68,69},{69,68},{70,71},{71,70},{7... | collective-permute-start | bytes 3932168 | tf_op jit(solution)/shard_map/ppermute | solution.py:83
  61.9 21.9 %collective-permute-start.12 = (bf16[4,2,5,16,1024]{4,3,2,1,0:T(8,128)(2,1)}, bf16[4,2,5,16,1024]{4,3,2,1,0:T(8,128)(2,1)}, u32[]{:S(2)}, u32[]{:S(2)}) collective-permute-start(bf16[4,2,5,16,1024]{4,3,2,1,0:T(8,128)(2,1)} %collective-permute-done.8.refs_2_), channel_id=1, source_target_pairs={{64,65},{65,64},{66,67},{67,66},{68,69},{69,68},{70,71},{71,70},{7... | collective-permute-start | bytes 3932168 | tf_op jit(solution)/shard_map/ppermute | solution.py:83
  63.6 20.2 %collective-permute-start.13 = (bf16[4,2,5,16,1024]{4,3,2,1,0:T(8,128)(2,1)}, bf16[4,2,5,16,1024]{4,3,2,1,0:T(8,128)(2,1)}, u32[]{:S(2)}, u32[]{:S(2)}) collective-permute-start(bf16[4,2,5,16,1024]{4,3,2,1,0:T(8,128)(2,1)} %collective-permute-done.9.refs_3_), channel_id=1, source_target_pairs={{64,65},{65,64},{66,67},{67,66},{68,69},{69,68},{70,71},{71,70},{7... | collective-permute-start | bytes 3932168 | tf_op jit(solution)/shard_map/ppermute | solution.py:83
  66.1 3.1 %copy-start.4 = (f32[1,512,1024]{2,1,0:T(8,128)S(1)}, f32[1,512,1024]{2,1,0:T(8,128)}, u32[]{:S(2)}) copy-start(f32[1,512,1024]{2,1,0:T(8,128)} %param.7) | copy-start | bytes 6291460
  66.1 3.1 %copy-start.19 = (f32[1024]{0:T(1024)S(1)}, f32[1024]{0:T(1024)}, u32[]{:S(2)}) copy-start(f32[1024]{0:T(1024)} %param.9) | copy-start | bytes 12292
  99.2 4.9 %copy-start.5 = (f32[1,512,1024]{2,1,0:T(8,128)S(1)}, f32[1,512,1024]{2,1,0:T(8,128)}, u32[]{:S(2)}) copy-start(f32[1,512,1024]{2,1,0:T(8,128)} %param.7) | copy-start | bytes 6291460
  99.2 2.3 %collective-permute-start.15 = (bf16[256,1024]{1,0:T(8,128)(2,1)S(1)}, bf16[256,1024]{1,0:T(8,128)(2,1)S(1)}, u32[]{:S(2)}, u32[]{:S(2)}) collective-permute-start(bf16[256,1024]{1,0:T(8,128)(2,1)S(1)} %get-tuple-element.52), channel_id=1, source_target_pairs={{0,1},{1,0},{2,3},{3,2},{4,5},{5,4},{6,7},{7,6},{8,9},{9,8},{10,11... | collective-permute-start | bytes 1572872 | tf_op jit(solution)/shard_map/ppermute | solution.py:30
  101.5 0.8 copy-start.16
  104.2 3.6 %copy-start.7 = (bf16[1024,1024]{1,0:T(8,128)(2,1)S(1)}, bf16[1024,1024]{1,0:T(8,128)(2,1)}, u32[]{:S(2)}) copy-start(bf16[1024,1024]{1,0:T(8,128)(2,1)} %copy-done.6) | copy-start | bytes 6291460
  107.8 1.3 copy-start.9
  109.2 14.5 %collective-permute-start.16 = (f32[256,1024]{1,0:T(8,128)S(1)}, f32[256,1024]{1,0:T(8,128)S(1)}, u32[]{:S(2)}, u32[]{:S(2)}) collective-permute-start(f32[256,1024]{1,0:T(8,128)S(1)} %constant_dynamic-slice_fusion.1), channel_id=1, source_target_pairs={{0,1},{1,0},{2,3},{3,2},{4,5},{5,4},{6,7},{7,6},{8,9},{9,8},{10,11... | collective-permute-start | bytes 3145736 | tf_op jit(solution)/shard_map/ppermute | solution.py:30
  109.7 51.4 %collective-permute-start.17 = (bf16[512,1024]{1,0:T(8,128)(2,1)}, bf16[512,1024]{1,0:T(8,128)(2,1)}, u32[]{:S(2)}, u32[]{:S(2)}) collective-permute-start(bf16[512,1024]{1,0:T(8,128)(2,1)} %broadcast_select_fusion), channel_id=1, source_target_pairs={{0,64},{1,65},{2,66},{3,67},{4,68},{5,69},{6,70},{7,71},{8,72},{9,... | collective-permute-start | bytes 3145736 | tf_op jit(solution)/shard_map/ppermute | solution.py:22
  124.8 36.2 %all-to-all-start = ((f32[32,8,1024]{2,1,0:T(8,128)}), f32[32,8,1024]{2,1,0:T(8,128)S(1)}, u32[]{:S(2)}, u32[]{:S(2)}) async-start(f32[32,8,1024]{2,1,0:T(8,128)} %add_bitcast_fusion), calls=%async_computation | async-start | bytes 2097152 | tf_op jit(solution)/shard_map/all_to_all | solution.py:239
  134.4 33.5 %copy-start.10 = (bf16[512,1024]{1,0:T(8,128)(2,1)S(1)}, bf16[512,1024]{1,0:T(8,128)(2,1)}, u32[]{:S(2)}) copy-start(bf16[512,1024]{1,0:T(8,128)(2,1)} %copy-done.9) | copy-start | bytes 3145732
  162.7 13.4 %all-to-all-start.1 = ((bf16[32,8,1024]{2,1,0:T(8,128)(2,1)}), bf16[32,8,1024]{2,1,0:T(8,128)(2,1)S(1)}, u32[]{:S(2)}, u32[]{:S(2)}) async-start(bf16[32,8,1024]{2,1,0:T(8,128)(2,1)} %broadcast_in_dim.39), calls=%async_computation.1 | async-start | bytes 1048576 | tf_op jit(solution)/shard_map/all_to_all | solution.py:35
  171.9 48.8 %collective-permute-start.18 = (bf16[1024,1024]{1,0:T(8,128)(2,1)}, bf16[1024,1024]{1,0:T(8,128)(2,1)}, u32[]{:S(2)}, u32[]{:S(2)}) collective-permute-start(bf16[1024,1024]{1,0:T(8,128)(2,1)} %get-tuple-element.66), channel_id=1, source_target_pairs={{64,0},{65,1},{66,2},{67,3},{68,4},{69,5},{70,6},{71,7},{72,8},{73... | collective-permute-start | bytes 6291464 | tf_op jit(solution)/shard_map/ppermute | solution.py:26
  176.1 2.8 %copy-start.11 = (bf16[32,8,1024]{2,1,0:T(8,128)(2,1)}, bf16[32,8,1024]{2,1,0:T(8,128)(2,1)S(1)}, u32[]{:S(2)}) copy-start(bf16[32,8,1024]{2,1,0:T(8,128)(2,1)S(1)} %all-to-all-done.1) | copy-start | bytes 1572868
  181.5 3.6 %copy-start.17 = (bf16[256,1024]{1,0:T(8,128)(2,1)}, bf16[256,1024]{1,0:T(8,128)(2,1)S(1)}, u32[]{:S(2)}) copy-start(bf16[256,1024]{1,0:T(8,128)(2,1)S(1)} %fusion.39) | copy-start | bytes 1572868
  185.1 15.6 %copy-start.8 = (f32[512,1024]{1,0:T(8,128)S(1)}, f32[512,1024]{1,0:T(8,128)}, u32[]{:S(2)}) copy-start(f32[512,1024]{1,0:T(8,128)} %get-tuple-element.50) | copy-start | bytes 6291460
  188.8 6.0 %copy-start.12 = (bf16[32,8,1024]{2,1,0:T(8,128)(2,1)S(1)}, bf16[32,8,1024]{2,1,0:T(8,128)(2,1)}, u32[]{:S(2)}) copy-start(bf16[32,8,1024]{2,1,0:T(8,128)(2,1)} %copy-done.11) | copy-start | bytes 1572868
  190.9 29.9 %copy-start.3 = (f32[1024,1024]{1,0:T(8,128)S(1)}, f32[1024,1024]{1,0:T(8,128)}, u32[]{:S(2)}) copy-start(f32[1024,1024]{1,0:T(8,128)} %get-tuple-element.67) | copy-start | bytes 12582916
  197.6 6.1 %collective-permute-start.19 = (f32[5,16,1024]{2,1,0:T(8,128)S(1)}, f32[5,16,1024]{2,1,0:T(8,128)S(1)}, u32[]{:S(2)}, u32[]{:S(2)}) collective-permute-start(f32[5,16,1024]{2,1,0:T(8,128)S(1)} %constant_dynamic-slice_fusion), channel_id=1, source_target_pairs={{0,1},{1,0},{2,3},{3,2},{4,5},{5,4},{6,7},{7,6},{8,9},{9,8},{10,11... | collective-permute-start | bytes 983048 | tf_op jit(solution)/shard_map/ppermute | solution.py:30
  200.7 20.0 %copy-start.2 = (f32[1,1024,1024]{2,1,0:T(8,128)S(1)}, f32[1,1024,1024]{2,1,0:T(8,128)}, u32[]{:S(2)}) copy-start(f32[1,1024,1024]{2,1,0:T(8,128)} %param.12) | copy-start | bytes 12582916
  204.7 22.0 %collective-permute-start.20 = (bf16[5,16,1024]{2,1,0:T(8,128)(2,1)S(1)}, bf16[5,16,1024]{2,1,0:T(8,128)(2,1)S(1)}, u32[]{:S(2)}, u32[]{:S(2)}) collective-permute-start(bf16[5,16,1024]{2,1,0:T(8,128)(2,1)S(1)} %fusion.65), channel_id=1, source_target_pairs={{64,0},{65,1},{66,2},{67,3},{68,4},{69,5},{70,6},{71,7},{72,8},{73... | collective-permute-start | bytes 491528 | tf_op jit(solution)/shard_map/ppermute | solution.py:26
  220.7 6.0 %copy-start.14 = (f32[5,32,1024]{2,1,0:T(8,128)S(1)}, f32[5,32,1024]{2,1,0:T(8,128)}, u32[]{:S(2)}) copy-start(f32[5,32,1024]{2,1,0:T(8,128)} %fusion.48) | copy-start | bytes 1966084
  220.8 6.0 %copy-start.15 = (f32[1,5,16,1024]{3,2,1,0:T(8,128)S(1)}, f32[1,5,16,1024]{3,2,1,0:T(8,128)}, u32[]{:S(2)}) copy-start(f32[1,5,16,1024]{3,2,1,0:T(8,128)} %param.13) | copy-start | bytes 983044
  220.8 6.9 %copy-start.1 = (bf16[512,1024]{1,0:T(8,128)(2,1)S(1)}, bf16[512,1024]{1,0:T(8,128)(2,1)}, u32[]{:S(2)}) copy-start(bf16[512,1024]{1,0:T(8,128)(2,1)} %param.10) | copy-start | bytes 3145732

commit v2 on v1

v2 whole, which is shorter than its diff:
```python
import itertools

import jax
import jax.numpy as jnp
from jax import lax
from jax.experimental import pallas as pl
from jax.experimental.pallas import tpu as pltpu
from jax.sharding import Mesh
from jax.sharding import PartitionSpec as P

BATCH = 512
LAYERS = 5
TILE = ("tile_0", "tile_1", "tile_2", "tile_3")
PLANE = ("tile_1", "tile_2", "tile_3")
FLOOR = ("tile_1", "tile_2")
CHIPS = ("tile_0", "tile_1", "tile_2")
ALL = ("role", *TILE)

momentum_decay = 0.9
step_size = 0.1


def to_trainer(value):
    return lax.ppermute(value, "role", [(0, 1)])


def to_solver(value):
    return lax.ppermute(value, "role", [(1, 0)])


def swapped(value, axis):
    return lax.ppermute(value, axis, [(0, 1), (1, 0)])


def from_everyone(value, axes):
    copies = jnp.broadcast_to(value, (lax.axis_size(axes), *value.shape))
    return lax.all_to_all(copies, axes, split_axis=0, concat_axis=0, tiled=True)


def ordered(mine, other, place, axis):
    return jnp.where(
        place == 0, jnp.stack([mine, other], axis), jnp.stack([other, mine], axis)
    )


def advance(fields, before, after, velocity, growth):
    states = jnp.concatenate([before[:BATCH, -1:], fields, after[:, :1]], axis=1)
    speeds = jnp.concatenate([before[BATCH, -1:], velocity])
    outflow = (
        jnp.maximum(speeds, 0.0) * states[:, :-1] + jnp.minimum(speeds, 0.0) * states[:, 1:]
    )
    carried = fields - outflow[:, 1:] + outflow[:, :-1]
    return carried + growth * carried * (1.0 - carried)


def from_trainers(value, role):
    pairs = []
    for plane, *place in itertools.product(*map(range, SIZES[1:])):
        pairs.append((flat(SIZES, (1, plane, *place)), flat(SIZES, (role, 1 - plane, *place))))
    return lax.ppermute(value, ALL, pairs)


def flat(sizes, place):
    index = 0
    for size, coordinate in zip(sizes, place):
        index = index * size + coordinate
    return index


def tied(value, *others):
    return lax.optimization_barrier((value, *others))[0]


SIZES = (2, 2, 4, 4, 2)
UNITS = 16
COLUMNS = 256
LANES = 128
VMEM_BYTES = 24 * 1024 * 1024
WIDE_VMEM = 60 * 1024 * 1024


def forward_kernel(
    gathered, features_ref, tiles_ref, last_ref, slopes_out, weights_out,
    weights, inputs, slopes, first_sem, rest_sem, out_sems,
):
    chip = lax.axis_index(CHIPS)
    own_tile = pl.ds(pl.multiple_of((chip * 2 * UNITS // LANES) * LANES, LANES), LANES)
    places = gathered.shape[0]
    plane = lax.axis_index("tile_0")

    def start(first, layers, sem):
        def step(place, carry):
            for number, half in enumerate((plane, 1 - plane)):
                row = pl.multiple_of((half * places + place) * UNITS, UNITS)
                pltpu.make_async_copy(
                    gathered.at[place, number, pl.ds(first, layers)],
                    weights.at[pl.ds(first, layers), pl.ds(row, UNITS)],
                    sem,
                ).start()
            return carry

        lax.fori_loop(0, places, step, 0)

    def finish(first, layers, sem):
        part = weights.at[pl.ds(first, layers)]
        pltpu.make_async_copy(part, part, sem).wait()

    start(0, 1, first_sem)
    start(1, LAYERS - 1, rest_sem)
    inputs[0] = features_ref[...]
    finish(0, 1, first_sem)
    kept = []
    for layer in range(LAYERS):
        if layer == 1:
            finish(1, LAYERS - 1, rest_sem)
            kept.append(
                pltpu.make_async_copy(weights.at[pl.ds(1, LAYERS - 1)], weights_out, out_sems.at[LAYERS])
            )
            kept[-1].start()
        for first in range(0, weights.shape[2], COLUMNS):
            columns = pl.ds(first, COLUMNS)
            total = jnp.dot(
                inputs[layer], weights[layer, :, columns], preferred_element_type=jnp.float32
            )
            logistic = 0.5 + 0.5 * jnp.tanh(0.5 * total)
            activation = total * logistic
            if layer + 1 < LAYERS:
                inputs[layer + 1, :, columns] = activation.astype(jnp.bfloat16)
            else:
                last_ref[:, columns] = activation.astype(jnp.bfloat16)
            slopes[layer, :, columns] = logistic + activation * (1.0 - logistic)
        kept.append(pltpu.make_async_copy(slopes.at[layer], slopes_out.at[layer], out_sems.at[layer]))
        kept[-1].start()
        tiles_ref[layer] = inputs[layer, :, own_tile]
    for copy in kept:
        copy.wait()


def forward(gathered, features):
    rows, width = features.shape
    vmem = pl.BlockSpec(memory_space=pltpu.VMEM)
    hbm = pl.BlockSpec(memory_space=pltpu.HBM)
    return pl.pallas_call(
        forward_kernel,
        out_shape=(
            jax.ShapeDtypeStruct((LAYERS, rows, LANES), jnp.bfloat16),
            jax.ShapeDtypeStruct((rows, width), jnp.bfloat16),
            jax.ShapeDtypeStruct((LAYERS, rows, width), jnp.float32),
            jax.ShapeDtypeStruct((LAYERS - 1, width, width), jnp.bfloat16),
        ),
        in_specs=[hbm, vmem],
        out_specs=(vmem, vmem, hbm, hbm),
        scratch_shapes=[
            pltpu.VMEM((LAYERS, width, width), jnp.bfloat16),
            pltpu.VMEM((LAYERS, rows, width), jnp.bfloat16),
            pltpu.VMEM((LAYERS, rows, width), jnp.float32),
            pltpu.SemaphoreType.DMA(()),
            pltpu.SemaphoreType.DMA(()),
            pltpu.SemaphoreType.DMA((LAYERS + 1,)),
        ],
        compiler_params=pltpu.CompilerParams(vmem_limit_bytes=WIDE_VMEM),
        cost_estimate=pl.CostEstimate(
            flops=2 * LAYERS * rows * width * width,
            bytes_accessed=LAYERS * width * (4 * width + 6 * rows),
            transcendentals=LAYERS * rows * width,
        ),
    )(gathered, features)


def backward_kernel(
    slope_ref, own_inputs_ref, slopes_in, weights, kept_ref, given_ref, kept_narrow, given_narrow,
    held, slopes, slots, sems,
):
    copies = {}
    for layer in range(LAYERS - 1, 0, -1):
        below = layer - 1
        copies[layer] = (
            pltpu.make_async_copy(weights.at[below], held.at[below], sems.at[0, below]),
            pltpu.make_async_copy(slopes_in.at[below], slopes.at[below], sems.at[1, below]),
        )
    for layer in (LAYERS - 1, LAYERS - 2):
        for copy in copies[layer]:
            copy.start()
    now = slope_ref
    for layer in range(LAYERS - 1, -1, -1):
        if layer > 0:
            later = slots.at[layer % 2]
            for copy in copies[layer]:
                copy.wait()
            for copy in copies.get(layer - 2, ()):
                copy.start()
            for first in range(0, held.shape[1], COLUMNS):
                columns = pl.ds(first, COLUMNS)
                upstream = lax.dot_general(
                    now[...],
                    held[layer - 1, columns, :],
                    (((1,), (1,)), ((), ())),
                    preferred_element_type=jnp.float32,
                )
                later[:, columns] = (upstream * slopes[layer - 1, :, columns]).astype(jnp.bfloat16)
        grads = jnp.dot(own_inputs_ref[layer], now[...], preferred_element_type=jnp.float32)
        kept_ref[layer] = grads[:UNITS]
        given_ref[layer] = grads[UNITS:]
        kept_narrow[layer] = grads[:UNITS].astype(jnp.bfloat16)
        given_narrow[layer] = grads[UNITS:].astype(jnp.bfloat16)
        if layer > 0:
            now = later


def backward(slope, own_inputs, slopes, weights):
    rows, width = slope.shape
    vmem = pl.BlockSpec(memory_space=pltpu.VMEM)
    hbm = pl.BlockSpec(memory_space=pltpu.HBM)
    return pl.pallas_call(
        backward_kernel,
        out_shape=tuple(
            jax.ShapeDtypeStruct((LAYERS, UNITS, width), kind)
            for kind in (jnp.float32, jnp.float32, jnp.bfloat16, jnp.bfloat16)
        ),
        in_specs=[vmem, vmem, hbm, hbm],
        out_specs=(vmem,) * 4,
        scratch_shapes=[
            pltpu.VMEM((LAYERS - 1, width, width), jnp.bfloat16),
            pltpu.VMEM((LAYERS - 1, rows, width), jnp.float32),
            pltpu.VMEM((2, rows, width), jnp.bfloat16),
            pltpu.SemaphoreType.DMA((2, LAYERS - 1)),
        ],
        compiler_params=pltpu.CompilerParams(vmem_limit_bytes=WIDE_VMEM),
        cost_estimate=pl.CostEstimate(
            flops=2 * (LAYERS - 1) * rows * width * width,
            bytes_accessed=LAYERS * width * (2 * width + 4 * rows),
            transcendentals=0,
        ),
    )(slope, own_inputs, slopes, weights)


def output_kernel(place_ref, activation_ref, fields_ref, weights_ref, left_ref, right_ref, partial_ref, residual_ref):
    del place_ref
    chunk = left_ref.shape[1]
    for first in range(0, weights_ref.shape[1], COLUMNS):
        columns = pl.ds(first, COLUMNS)
        predicted = jnp.dot(
            activation_ref[...], weights_ref[:, columns], preferred_element_type=jnp.float32
        )
        residual = ((predicted - fields_ref[:, columns]) / BATCH).astype(jnp.bfloat16)
        residual_ref[:, columns] = residual
        part = left_ref if first < chunk else right_ref
        part[:, first % chunk : first % chunk + COLUMNS] = residual
    for first in range(0, weights_ref.shape[0], COLUMNS):
        columns = pl.ds(first, COLUMNS)
        partial_ref[:, columns] = lax.dot_general(
            residual_ref[...],
            weights_ref[columns, :],
            (((1,), (1,)), ((), ())),
            preferred_element_type=jnp.float32,
        ).astype(partial_ref.dtype)


def output_layer(place, activation, fields, weights, kind):
    rows, width = activation.shape
    cells = fields.shape[1]
    return pl.pallas_call(
        output_kernel,
        out_shape=(
            jax.ShapeDtypeStruct((rows, cells // 2), jnp.bfloat16),
            jax.ShapeDtypeStruct((rows, cells // 2), jnp.bfloat16),
            jax.ShapeDtypeStruct((rows, width), kind),
        ),
        grid_spec=pltpu.PrefetchScalarGridSpec(
            num_scalar_prefetch=1,
            grid=(1,),
            in_specs=[
                pl.BlockSpec((rows, width), lambda i, place: (0, 0)),
                pl.BlockSpec((rows, cells), lambda i, place: (place[0], 0)),
                pl.BlockSpec((width, cells), lambda i, place: (0, 0)),
            ],
            out_specs=(
                pl.BlockSpec((rows, cells // 2), lambda i, place: (0, 0)),
                pl.BlockSpec((rows, cells // 2), lambda i, place: (0, 0)),
                pl.BlockSpec((rows, width), lambda i, place: (0, 0)),
            ),
            scratch_shapes=[pltpu.VMEM((rows, cells), jnp.bfloat16)],
        ),
        compiler_params=pltpu.CompilerParams(vmem_limit_bytes=VMEM_BYTES),
        cost_estimate=pl.CostEstimate(
            flops=4 * rows * width * cells,
            bytes_accessed=2 * width * cells + 12 * rows * cells,
            transcendentals=0,
        ),
    )(place, activation, fields, weights)


def update_kernel(
    solver_ref, own_ref, other_ref, last_ref, other_last_ref, here_ref, far_ref, begun, next_ref, residual
):
    del begun
    solver_side = solver_ref[0] == 1
    half = last_ref.shape[0]

    @pl.when(jnp.logical_and(pl.program_id(0) == 0, solver_side))
    def _():
        residual[...] = far_ref[...]

    @pl.when(jnp.logical_and(pl.program_id(0) == 0, jnp.logical_not(solver_side)))
    def _():
        residual[...] = here_ref[...]

    gradient = lax.dot_general(
        last_ref[...], residual[:half], (((0,), (0,)), ((), ())), preferred_element_type=jnp.float32
    ) + lax.dot_general(
        other_last_ref[...], residual[half:], (((0,), (0,)), ((), ())), preferred_element_type=jnp.float32
    )

    @pl.when(solver_side)
    def _():
        next_ref[...] = momentum_decay * own_ref[...] + gradient

    @pl.when(jnp.logical_not(solver_side))
    def _():
        momentum = momentum_decay * other_ref[...].astype(jnp.float32) + gradient
        next_ref[...] = own_ref[...] - step_size * momentum


def updated(chunk, begun, solver_side, own, other, last, other_last, here, far):
    width, cells = own.shape
    half = last.shape[0]
    columns = pl.BlockSpec((half, BLOCK), lambda i, flag: (0, i))
    whole = pl.BlockSpec((2 * half, cells // 2), lambda i, flag: (0, 0))
    block = pl.BlockSpec((BLOCK, cells // 2), lambda i, flag: (i, chunk))
    return pl.pallas_call(
        update_kernel,
        out_shape=jax.ShapeDtypeStruct(own.shape, jnp.float32),
        grid_spec=pltpu.PrefetchScalarGridSpec(
            num_scalar_prefetch=1,
            grid=(width // BLOCK,),
            in_specs=[
                block,
                pl.BlockSpec((BLOCK, cells // 2), lambda i, flag: (i, 0)),
                columns,
                columns,
                whole,
                whole,
                pl.BlockSpec(memory_space=pl.ANY),
            ],
            out_specs=block,
            scratch_shapes=[pltpu.VMEM((2 * half, cells // 2), jnp.bfloat16)],
        ),
        input_output_aliases={} if begun is None else {7: 0},
        compiler_params=pltpu.CompilerParams(vmem_limit_bytes=VMEM_BYTES),
        cost_estimate=pl.CostEstimate(
            flops=2 * half * width * cells, bytes_accessed=5 * width * cells, transcendentals=0
        ),
    )(
        solver_side.astype(jnp.int32)[None], own, other, last, other_last, here, far,
        jnp.zeros((8, LANES), jnp.float32) if begun is None else begun,
    )


BLOCK = 256


def body(fields_pair, velocity, growth, features, assignment, out_pair, hidden_pair):
    solver_side = lax.axis_index("role") == 0
    core = lax.axis_index("tile_3")
    chip = lax.axis_index(CHIPS)
    fields = fields_pair[0]
    own_out = out_pair[0]
    own_hidden = hidden_pair[0]
    units = own_hidden.shape[1]
    width = own_hidden.shape[2]
    half = BATCH // 2

    hidden_narrow = own_hidden.astype(jnp.bfloat16)
    out_narrow = own_out.astype(jnp.bfloat16)
    edge = jnp.concatenate(
        [fields[:, -128:], jnp.broadcast_to(velocity[None, -128:], (8, 128))], axis=0
    )

    partner_hidden = swapped(hidden_narrow, "role")
    near = jnp.where(solver_side, partner_hidden, hidden_narrow)
    far = jnp.where(solver_side, from_trainers(hidden_narrow, 0), from_trainers(hidden_narrow, 1))
    gathered = lax.all_gather(jnp.stack([near, far]), PLANE, axis=0)

    middle = own_out.shape[1] // 2
    momentum = to_trainer(own_out[:, :middle].astype(jnp.bfloat16))
    count = lax.axis_size(TILE)
    up = [(i, (i + 1) % count) for i in range(count)]
    down = [(j, i) for i, j in up]
    before = lax.ppermute(edge, TILE, up)
    after = lax.ppermute(fields[:, :128], TILE, down)
    advanced = advance(fields, before, after, velocity, growth)
    carried = jnp.take(advanced.astype(jnp.bfloat16), assignment, axis=0)
    next_batch = to_trainer(carried)
    gathered, advanced, momentum, next_batch = lax.optimization_barrier(
        (gathered, advanced, momentum, next_batch)
    )
    tiles, last, slopes, weights = forward(
        gathered, lax.dynamic_slice_in_dim(features, core * half, half, 0)
    )
    place = core.astype(jnp.int32)[None]
    other_last = swapped(last, "tile_3")
    left, right, kept = output_layer(place, last, fields, out_narrow, jnp.float32)
    other_left, other_right, given = output_layer(
        1 - place, tied(other_last, kept), fields, out_narrow, jnp.bfloat16
    )
    arrived = swapped(given, "tile_3")
    chip_sum = (kept + arrived.astype(jnp.float32)).astype(jnp.bfloat16)
    chips = lax.axis_size(FLOOR)
    rows = half // chips
    first = lax.axis_index(FLOOR) * rows
    shares = lax.all_to_all(
        chip_sum.reshape(chips, rows, width), FLOOR, split_axis=0, concat_axis=0, tiled=True
    )
    plane_sum = shares.astype(jnp.float32).sum(axis=0)
    upstream = plane_sum + swapped(plane_sum, "tile_0")
    upstream, left, right, rest = lax.optimization_barrier(
        (
            upstream,
            jnp.concatenate([left, other_left]),
            jnp.concatenate([right, other_right]),
            own_out[:, middle:].astype(jnp.bfloat16),
        )
    )
    left_far, right_far, momentum_rest = to_solver(left), to_solver(right), to_trainer(rest)
    own_factor = lax.dynamic_slice_in_dim(slopes[LAYERS - 1], first, rows, 0)
    own_slope = (upstream * own_factor).astype(jnp.bfloat16)
    slope = from_everyone(own_slope, FLOOR).reshape(half, width)

    own_inputs = jnp.concatenate(
        [
            lax.dynamic_slice_in_dim(tiles, (chip * 2 + side) * units % LANES, units, 2)
            for side in (core, 1 - core)
        ],
        axis=2,
    )
    slope, own_inputs = lax.optimization_barrier((slope, own_inputs.swapaxes(1, 2)))
    kept, given, kept_narrow, given_narrow = backward(slope, own_inputs, slopes, weights)
    crossing = [
        (flat(SIZES, (1, *place, core)), flat(SIZES, (0, *place, 1 - core)))
        for *place, core in itertools.product(*map(range, SIZES[1:]))
    ]
    kept_far = to_solver(kept_narrow)
    given_far = lax.ppermute(given_narrow, ALL, crossing)
    grad_hidden = kept + swapped(given, "tile_3")
    grad_hidden_far = kept_far.astype(jnp.float32) + given_far.astype(jnp.float32)

    other_hidden = partner_hidden.astype(jnp.float32)
    out_next = updated(
        0, None, solver_side, own_out, momentum, last, other_last, left, left_far
    )
    out_next = updated(
        1, out_next, solver_side, own_out, momentum_rest, last, other_last, right, right_far
    )
    hidden_next = jnp.where(
        solver_side,
        momentum_decay * own_hidden + grad_hidden_far,
        own_hidden - step_size * (momentum_decay * other_hidden + grad_hidden),
    )
    fields_next = jnp.where(solver_side, advanced, next_batch.astype(jnp.float32))
    return (fields_next[None], out_next[None], hidden_next[None])


def solution(mesh):
    finer = Mesh(
        mesh.devices.reshape(SIZES), ALL
    )
    in_specs = (
        P("role", None, TILE),
        P(TILE),
        P(TILE),
        P(),
        P(),
        P("role", None, TILE),
        P("role", None, TILE, None),
    )
    out_specs = (P("role", None, TILE), P("role", None, TILE), P("role", None, TILE, None))
    return jax.shard_map(body, mesh=finer, in_specs=in_specs, out_specs=out_specs, check_vma=False)
```

time: 232 us -> 177 us (0.76); the launches traced: 228 us -> 176 us
  matrix products: 29.4 us -> 0 us
  starting transfers between devices: 69.8 us -> 46.1 us
  waiting for transfers between devices: 71.8 us -> 51.6 us
  Pallas kernels: 13.5 us -> 29 us
  between operations: 1.06 us -> 14.5 us
  other arithmetic: 29 us -> 19.7 us
    dot_general x11 -> x0, matrix products: 29.4 us -> none  [the longest x5 11.5 us: body(): lax.dot_general(own_inputs, slope, (((0,), (0,)), ((), ())), preferred_el...]
    ppermute x3, starting transfers between devices: 35.6 us -> 15.6 us  [to_trainer(): return lax.ppermute(value, 'role', [(0, 1)])]
    all_to_all x1, waiting for transfers between devices: 26.7 us -> 9 us  [body(): lax.all_to_all(chip_sum.reshape(chips, rows, width), FLOOR, split_axis=0,...]
    pallas_call x1 -> x6, Pallas kernels: 13.5 us -> 29 us  [the longest x1 11 us: forward(): pl.pallas_call(forward_kernel, out_shape=(jax.ShapeDtypeStruct((LAYERS, r...]
    ppermute x2 -> x3, waiting for transfers between devices: 14.7 us -> 2.15 us  [to_solver(): return lax.ppermute(value, 'role', [(1, 0)])]
    ppermute x11 -> x3, starting transfers between devices: 15 us -> 3.9 us  [the longest x2 2.62 us: from_trainers(): return lax.ppermute(value, ALL, pairs)]
    all_gather x0 -> x1, waiting for transfers between devices: none -> 8.64 us  [body(): gathered = lax.all_gather(jnp.stack([near, far]), PLANE, axis=0)]
    ppermute x3, waiting for transfers between devices: 17.6 us -> 24.9 us  [to_trainer(): return lax.ppermute(value, 'role', [(0, 1)])]
  transfers between devices with their start and end apart: 23 -> 19, of which waited for: 8 -> 9; matrix products, arithmetic and copies ran while one was open for 23% -> 15% of each run, Pallas kernels for 0% -> 8%
where the time goes in v2:
time: 177 us; the launch traced here: 176 us
  waiting for transfers between devices  51.6 us (29%)
  starting transfers between devices  46.1 us (26%)
  Pallas kernels  29 us (16%)
  other arithmetic  19.7 us (11%)
  local copies, waits for them, and re-layouts  14.7 us (8%)
  between operations  14.5 us (8%)
    ppermute x3, waiting for transfers between devices, to_trainer(): return lax.ppermute(value, 'role', [(0, 1)])  24.9 us
    ppermute x3, starting transfers between devices, to_trainer(): return lax.ppermute(value, 'role', [(0, 1)])  15.6 us
    pallas_call x1, Pallas kernels, forward(): pl.pallas_call(forward_kernel, out_shape=(jax.ShapeDtypeStruct((LAYERS, r...  11 us
    ppermute x5, starting transfers between devices, swapped(): return lax.ppermute(value, axis, [(0, 1), (1, 0)])  9.8 us
    all_to_all x1, waiting for transfers between devices, body(): lax.all_to_all(chip_sum.reshape(chips, rows, width), FLOOR, split_axis=0,...  9 us
    all_gather x1, waiting for transfers between devices, body(): gathered = lax.all_gather(jnp.stack([near, far]), PLANE, axis=0)  8.64 us
    pallas_call x1, Pallas kernels, backward(): pl.pallas_call(backward_kernel, out_shape=tuple((jax.ShapeDtypeStruct((LA...  7.75 us
    pallas_call x2, Pallas kernels, updated(): pl.pallas_call(update_kernel, out_shape=jax.ShapeDtypeStruct(own.shape, j...  7.73 us
  transfers between devices with their start and end apart: 19, of which 9 were waited for; matrix products, arithmetic and copies ran while one was open for 15% of the time, Pallas kernels for 8%

profile of v2, /device:TPU:1, one launch (start us, length us, event | category | flops | bytes accessed | tf_op | source)
XLA Modules:
  0.0 175.6 jit_solution(6050056879171643480)
XLA Ops:
  7.2 1.8 %bitcast_convert_fusion = bf16[5,16,1024]{2,1,0:T(8,128)(2,1)} fusion(f32[1,5,16,1024]{3,2,1,0:T(8,128)} %param.13), kind=kLoop, calls=%fused_computation.16 | loop fusion | flops 81920 | bytes 491520 | tf_op jit(solution)/shard_map/convert_element_type | solution.py:373
  9.1 3.7 %collective-permute-start = (bf16[5,16,1024]{2,1,0:T(8,128)(2,1)}, bf16[5,16,1024]{2,1,0:T(8,128)(2,1)S(1)}, u32[]{:S(2)}, u32[]{:S(2)}) collective-permute-start(bf16[5,16,1024]{2,1,0:T(8,128)(2,1)} %bitcast_convert_fusion), channel_id=1, source_target_pairs={{0,64},{64,0},{1,65},{65,1},{2,66},{66,2},{3,67},{67,3},{4,68},{68... | collective-permute-start | bytes 491528 | tf_op jit(solution)/shard_map/ppermute | solution.py:32
  12.8 1.3 collective-permute-start.1
  14.1 1.3 collective-permute-start.2
  15.4 1.2 collective-permute-done
  16.7 1.1 select_bitcast_fusion.2
  17.7 3.1 %collective-permute-done.1 = bf16[5,16,1024]{2,1,0:T(8,128)(2,1)S(1)} collective-permute-done((bf16[5,16,1024]{2,1,0:T(8,128)(2,1)}, bf16[5,16,1024]{2,1,0:T(8,128)(2,1)S(1)}, u32[]{:S(2)}, u32[]{:S(2)}) %collective-permute-start.1) | collective-permute-done | bytes 163872 | tf_op jit(solution)/shard_map/ppermute | solution.py:60
  20.9 0.8 pad_maximum_fusion.2
  21.8 3.5 %collective-permute-start.3 = (f32[520,128]{1,0:T(8,128)S(1)}, f32[520,128]{1,0:T(8,128)S(1)}, u32[]{:S(2)}, u32[]{:S(2)}) collective-permute-start(f32[520,128]{1,0:T(8,128)S(1)} %pad_maximum_fusion.3), channel_id=1, source_target_pairs={{0,1},{1,2},{2,3},{3,4},{4,5},{5,6},{6,7},{7,8},{8,9},{9,10},{10,1... | collective-permute-start | bytes 798728 | tf_op jit(solution)/shard_map/ppermute | solution.py:389
  25.2 2.5 %bitcast_convert_fusion.1.weights_ref = bf16[1024,1024]{1,0:T(8,128)(2,1)S(1)} fusion(f32[1,1024,1024]{2,1,0:T(8,128)} %param.12), kind=kLoop, calls=%fused_computation.35 | loop fusion | flops 1048576 | bytes 6291456 | tf_op jit(solution)/shard_map/convert.2
  27.8 1.6 fusion.8
  29.8 7.0 %collective-permute-start.5 = (bf16[1024,512]{1,0:T(8,128)(2,1)}, bf16[1024,512]{1,0:T(8,128)(2,1)}, u32[]{:S(2)}, u32[]{:S(2)}) collective-permute-start(bf16[1024,512]{1,0:T(8,128)(2,1)} %get-tuple-element.56), channel_id=1, source_target_pairs={{0,64},{1,65},{2,66},{3,67},{4,68},{5,69},{6,70},{7,71},{8,72},{9,... | collective-permute-start | bytes 3145736 | tf_op jit(solution)/shard_map/ppermute | solution.py:24
  39.0 2.5 %fusion.7 = (bf16[512,1024]{1,0:T(8,128)(2,1)}, f32[512,1024]{1,0:T(8,128)}) fusion(f32[1024]{0:T(1024)S(1)} %copy-done.21, f32[512,1025]{1,0:T(8,128)S(1)} %fusion, f32[1,512,1024]{2,1,0:T(8,128)S(1)} %copy-done.2), kind=kLoop, calls=%fused_computation.36 | loop fusion | flops 3670016 | bytes 9441280 | tf_op jit(solution)/shard_map/convert_element_type | solution.py:392
  41.4 4.8 %gather_fusion = bf16[512,1024]{1,0:T(8,128)(2,1)} fusion(bf16[512,1024]{1,0:T(8,128)(2,1)} %get-tuple-element.53, s32[1024]{0:T(1024)S(1)} %pad_clamp_fusion), kind=kCustom, calls=%fused_computation | custom fusion | bytes 2099200 | tf_op jit(solution)/shard_map/jit(_take)/gather | solution.py:392
  46.3 2.4 %broadcast_select_fusion = bf16[512,1024]{1,0:T(8,128)(2,1)} fusion(bf16[512,1024]{1,0:T(8,128)(2,1)} %gather_fusion, pred[512]{0:T(512)(128)(4,1)S(1)} %compare_and_fusion), kind=kLoop, calls=%fused_computation.10 | loop fusion | flops 524288 | bytes 2097664 | tf_op jit(solution)/shard_map/jit(_take)/select_n | solution.py:392
  48.7 2.2 %collective-permute-start.6 = (bf16[512,1024]{1,0:T(8,128)(2,1)}, bf16[512,1024]{1,0:T(8,128)(2,1)}, u32[]{:S(2)}, u32[]{:S(2)}) collective-permute-start(bf16[512,1024]{1,0:T(8,128)(2,1)} %broadcast_select_fusion), channel_id=1, source_target_pairs={{0,64},{1,65},{2,66},{3,67},{4,68},{5,69},{6,70},{7,71},{8,72},{9,... | collective-permute-start | bytes 3145736 | tf_op jit(solution)/shard_map/ppermute | solution.py:24
  50.9 0.8 constant_dynamic-slice_fusion.2.features_ref
  51.7 2.4 %collective-permute-done.5.other_ref = bf16[1024,512]{1,0:T(8,128)(2,1)} collective-permute-done((bf16[1024,512]{1,0:T(8,128)(2,1)}, bf16[1024,512]{1,0:T(8,128)(2,1)}, u32[]{:S(2)}, u32[]{:S(2)}) %collective-permute-start.5) | collective-permute-done | bytes 1048608 | tf_op jit(solution)/shard_map/ppermute | solution.py:24
  54.1 22.5 %collective-permute-done.6 = bf16[512,1024]{1,0:T(8,128)(2,1)} collective-permute-done((bf16[512,1024]{1,0:T(8,128)(2,1)}, bf16[512,1024]{1,0:T(8,128)(2,1)}, u32[]{:S(2)}, u32[]{:S(2)}) %collective-permute-start.6) | collective-permute-done | bytes 1048608 | tf_op jit(solution)/shard_map/ppermute | solution.py:24
  76.6 8.6 %all-gather.3.cloned.1.call-done = bf16[64,5,16,1024]{3,2,1,0:T(8,128)(2,1)} async-done(((bf16[2,5,16,1024]{3,2,1,0:T(8,128)(2,1)}), bf16[64,5,16,1024]{3,2,1,0:T(8,128)(2,1)}) %all-gather.3.cloned.1.call-update) | async-done | bytes 10485776 | tf_op jit(solution)/shard_map/all_gather | solution.py:382
  85.2 11.0 %shard_map.94 = (bf16[5,256,128]{2,1,0:T(8,128)(2,1)}, bf16[256,1024]{1,0:T(8,128)(2,1)}, f32[5,256,1024]{2,1,0:T(8,128)}, bf16[4,1024,1024]{2,1,0:T(8,128)(2,1)}) custom-call(bf16[32,2,5,16,1024]{4,3,2,1,0:T(8,128)(2,1)} %bitcast.48, bf16[256,1024]{1,0:T(8,128)(2,1)} %constant_dynamic-slice_fusion.2.features_ref), custom_call_target="tpu_custom_call" | custom-call | flops 2684354560 | bytes 28835840 | tf_op jit(solution)/shard_map/pallas_call | solution.py:143
  96.5 1.6 copy-done.5
  98.1 1.0 copy-done.7
  99.2 1.3 shard_map.95
  100.8 1.3 shard_map.96
  102.4 1.7 collective-permute-done.8
  104.0 0.9 add_convert_fusion
  105.0 5.0 %all-to-all-start = ((bf16[16,16,1024]{2,1,0:T(8,128)(2,1)}), bf16[16,16,1024]{2,1,0:T(8,128)(2,1)S(1)}, u32[]{:S(2)}, u32[]{:S(2)}) async-start(bf16[16,16,1024]{2,1,0:T(8,128)(2,1)} %bitcast.10), calls=%async_computation | async-start | bytes 1048576 | tf_op jit(solution)/shard_map/all_to_all | solution.py:411
  110.0 1.3 slice.49
  111.3 9.0 %all-to-all-done = bf16[16,16,1024]{2,1,0:T(8,128)(2,1)S(1)} async-done(((bf16[16,16,1024]{2,1,0:T(8,128)(2,1)}), bf16[16,16,1024]{2,1,0:T(8,128)(2,1)S(1)}, u32[]{:S(2)}, u32[]{:S(2)}) %all-to-all-start) | async-done | bytes 524320 | tf_op jit(solution)/shard_map/all_to_all | solution.py:411
  120.4 1.5 collective-permute-start.9
  121.9 1.0 pad_maximum_fusion
  122.9 0.9 collective-permute-done.9
  123.8 0.9 broadcast_in_dim.55
  124.7 4.2 %all-to-all-start.1 = ((bf16[16,16,1024]{2,1,0:T(8,128)(2,1)}), bf16[16,16,1024]{2,1,0:T(8,128)(2,1)}, u32[]{:S(2)}, u32[]{:S(2)}) async-start(bf16[16,16,1024]{2,1,0:T(8,128)(2,1)} %broadcast_in_dim.55), calls=%async_computation.1 | async-start | bytes 1048576 | tf_op jit(solution)/shard_map/all_to_all | solution.py:37
  128.9 1.3 collective-permute-start.12
  130.3 1.1 copy.13
  131.4 6.3 %collective-permute-start.10 = (bf16[1024,512]{1,0:T(8,128)(2,1)}, bf16[1024,512]{1,0:T(8,128)(2,1)S(1)}, u32[]{:S(2)}, u32[]{:S(2)}) collective-permute-start(bf16[1024,512]{1,0:T(8,128)(2,1)} %get-tuple-element.39), channel_id=1, source_target_pairs={{0,64},{1,65},{2,66},{3,67},{4,68},{5,69},{6,70},{7,71},{8,72},{9,... | collective-permute-start | bytes 3145736 | tf_op jit(solution)/shard_map/ppermute | solution.py:24
  138.4 1.3 collective-permute-start.11
  139.7 7.8 %shard_map.99 = (f32[5,16,1024]{2,1,0:T(8,128)}, f32[5,16,1024]{2,1,0:T(8,128)}, bf16[5,16,1024]{2,1,0:T(8,128)(2,1)}, bf16[5,16,1024]{2,1,0:T(8,128)(2,1)}) custom-call(bf16[256,1024]{1,0:T(8,128)(2,1)} %bitcast.13.slope_ref, bf16[5,32,256]{2,1,0:T(8,128)(2,1)} %maximum_bitcast_fusion.own_inputs_ref, f32[5,256,1024]{2,1,0:T(8,128)} %get-tuple-element.44.slopes_in, ...), custom_call_target="tpu_custom_call" | custom-call | flops 2147483648 | bytes 15728640 | tf_op jit(solution)/shard_map/pallas_call | solution.py:214
  147.4 3.9 %collective-permute-start.15 = (f32[5,16,1024]{2,1,0:T(8,128)}, f32[5,16,1024]{2,1,0:T(8,128)S(1)}, u32[]{:S(2)}, u32[]{:S(2)}) collective-permute-start(f32[5,16,1024]{2,1,0:T(8,128)} %get-tuple-element.52), channel_id=1, source_target_pairs={{0,1},{1,0},{2,3},{3,2},{4,5},{5,4},{6,7},{7,6},{8,9},{9,8},{10,11... | collective-permute-start | bytes 983048 | tf_op jit(solution)/shard_map/ppermute | solution.py:32
  151.4 1.3 collective-permute-start.14
  152.7 1.6 collective-permute-start.13
  154.2 3.6 %select_bitcast_fusion = f32[1,512,1024]{2,1,0:T(8,128)} fusion(f32[512,1024]{1,0:T(8,128)} %get-tuple-element.28, bf16[512,1024]{1,0:T(8,128)(2,1)} %collective-permute-done.6, pred[]{:T(512)S(6)} %eq.6), kind=kLoop, calls=%fused_computation.6 | loop fusion | flops 1048576 | bytes 5242881 | tf_op jit(solution)/shard_map/broadcast_in_dim | solution.py:460
  157.9 4.6 %shard_map.97.begun = f32[1024,1024]{1,0:T(8,128)} custom-call(s32[1]{0:T(128)} %bitcast.8.solver_ref, f32[1024,1024]{1,0:T(8,128)S(1)} %bitcast.45, bf16[1024,512]{1,0:T(8,128)(2,1)} %collective-permute-done.5.other_ref, bf16[256,1024]{1,0:T(8,128)(2,1)S(1)} %copy-done.8, bf16[256,1024]{1,0:T(8,128)(2,1)S(1)} %collective-permute-done.7.activation_ref.other_last_ref, ...), custom_call_target="tpu_custom_call" | custom-call | flops 536870912 | bytes 5242880 | tf_op jit(solution)/shard_map/pallas_call | solution.py:330
  162.6 2.1 %collective-permute-done.13 = bf16[5,16,1024]{2,1,0:T(8,128)(2,1)S(1)} collective-permute-done((bf16[5,16,1024]{2,1,0:T(8,128)(2,1)}, bf16[5,16,1024]{2,1,0:T(8,128)(2,1)S(1)}, u32[]{:S(2)}, u32[]{:S(2)}) %collective-permute-start.13) | collective-permute-done | bytes 163872 | tf_op jit(solution)/shard_map/ppermute | solution.py:28
  164.7 0.9 fusion.3
  165.6 3.1 %shard_map.98 = f32[1024,1024]{1,0:T(8,128)} custom-call(s32[1]{0:T(128)} %bitcast.8.solver_ref, f32[1024,1024]{1,0:T(8,128)S(1)} %bitcast.46, bf16[1024,512]{1,0:T(8,128)(2,1)S(1)} %collective-permute-done.10.other_ref, bf16[256,1024]{1,0:T(8,128)(2,1)S(1)} %copy-done.8, bf16[256,1024]{1,0:T(8,128)(2,1)S(1)} %copy-done.10, ...), custom_call_target="tpu_custom_call", output_to_operand_aliasing={{}: (7, {})} | custom-call | flops 536870912 | bytes 5242880 | tf_op jit(solution)/shard_map/pallas_call | solution.py:330
  (77 shorter events, 4.5 us)
Async XLA Ops:
  7.2 43.8 %copy-start = (bf16[512,1024]{1,0:T(8,128)(2,1)S(1)}, bf16[512,1024]{1,0:T(8,128)(2,1)}, u32[]{:S(2)}) copy-start(bf16[512,1024]{1,0:T(8,128)(2,1)} %param.10) | copy-start | bytes 3145732
  7.2 14.5 %copy-start.22 = (f32[1024]{0:T(1024)S(1)}, f32[1024]{0:T(1024)}, u32[]{:S(2)}) copy-start(f32[1024]{0:T(1024)} %param.8) | copy-start | bytes 12292
  7.2 14.5 %copy-start.2 = (f32[1,512,1024]{2,1,0:T(8,128)S(1)}, f32[1,512,1024]{2,1,0:T(8,128)}, u32[]{:S(2)}) copy-start(f32[1,512,1024]{2,1,0:T(8,128)} %param.7) | copy-start | bytes 6291460
  7.2 78.0 %all-gather.3.cloned.1.call-start = ((), (), s32[]{:S(2)}) async-start(), calls=%async_computation.2 | async-start | bytes 10813440 | tf_op jit(solution)/shard_map/all_gather | solution.py:382
  9.1 7.6 %collective-permute-start = (bf16[5,16,1024]{2,1,0:T(8,128)(2,1)}, bf16[5,16,1024]{2,1,0:T(8,128)(2,1)S(1)}, u32[]{:S(2)}, u32[]{:S(2)}) collective-permute-start(bf16[5,16,1024]{2,1,0:T(8,128)(2,1)} %bitcast_convert_fusion), channel_id=1, source_target_pairs={{0,64},{64,0},{1,65},{65,1},{2,66},{66,2},{3,67},{67,3},{4,68},{68... | collective-permute-start | bytes 491528 | tf_op jit(solution)/shard_map/ppermute | solution.py:32
  12.8 8.1 %collective-permute-start.1 = (bf16[5,16,1024]{2,1,0:T(8,128)(2,1)}, bf16[5,16,1024]{2,1,0:T(8,128)(2,1)S(1)}, u32[]{:S(2)}, u32[]{:S(2)}) collective-permute-start(bf16[5,16,1024]{2,1,0:T(8,128)(2,1)} %bitcast_convert_fusion), channel_id=1, source_target_pairs={{64,32},{65,33},{66,34},{67,35},{68,36},{69,37},{70,38},{71,39},{7... | collective-permute-start | bytes 491528 | tf_op jit(solution)/shard_map/ppermute | solution.py:60
  14.1 6.8 %collective-permute-start.2 = (bf16[5,16,1024]{2,1,0:T(8,128)(2,1)}, bf16[5,16,1024]{2,1,0:T(8,128)(2,1)}, u32[]{:S(2)}, u32[]{:S(2)}) collective-permute-start(bf16[5,16,1024]{2,1,0:T(8,128)(2,1)} %bitcast_convert_fusion), channel_id=1, source_target_pairs={{64,96},{65,97},{66,98},{67,99},{68,100},{69,101},{70,102},{71,103... | collective-permute-start | bytes 491528 | tf_op jit(solution)/shard_map/ppermute | solution.py:60
  16.6 11.1 %copy-start.17 = (bf16[5,16,1024]{2,1,0:T(8,128)(2,1)}, bf16[5,16,1024]{2,1,0:T(8,128)(2,1)S(1)}, u32[]{:S(2)}) copy-start(bf16[5,16,1024]{2,1,0:T(8,128)(2,1)S(1)} %collective-permute-done) | copy-start | bytes 491524
  21.8 15.0 %collective-permute-start.3 = (f32[520,128]{1,0:T(8,128)S(1)}, f32[520,128]{1,0:T(8,128)S(1)}, u32[]{:S(2)}, u32[]{:S(2)}) collective-permute-start(f32[520,128]{1,0:T(8,128)S(1)} %pad_maximum_fusion.3), channel_id=1, source_target_pairs={{0,1},{1,2},{2,3},{3,4},{4,5},{5,6},{6,7},{7,8},{8,9},{9,10},{10,1... | collective-permute-start | bytes 798728 | tf_op jit(solution)/shard_map/ppermute | solution.py:389
  25.2 13.0 %collective-permute-start.4 = (f32[512,128]{1,0:T(8,128)S(1)}, f32[512,128]{1,0:T(8,128)S(1)}, u32[]{:S(2)}, u32[]{:S(2)}) collective-permute-start(f32[512,128]{1,0:T(8,128)S(1)} %get-tuple-element.57), channel_id=1, source_target_pairs={{1,0},{2,1},{3,2},{4,3},{5,4},{6,5},{7,6},{8,7},{9,8},{10,9},{11,1... | collective-permute-start | bytes 786440 | tf_op jit(solution)/shard_map/ppermute | solution.py:390
  27.8 2.0 %copy-start.4 = (bf16[1024,1024]{1,0:T(8,128)(2,1)}, bf16[1024,1024]{1,0:T(8,128)(2,1)S(1)}, u32[]{:S(2)}) copy-start(bf16[1024,1024]{1,0:T(8,128)(2,1)S(1)} %bitcast_convert_fusion.1.weights_ref) | copy-start | bytes 6291460
  27.8 9.0 %copy-start.20 = (s32[512]{0:T(512)S(1)}, s32[512]{0:T(512)}, u32[]{:S(2)}) copy-start(s32[512]{0:T(512)} %param.11) | copy-start | bytes 6148
  29.8 24.3 %collective-permute-start.5 = (bf16[1024,512]{1,0:T(8,128)(2,1)}, bf16[1024,512]{1,0:T(8,128)(2,1)}, u32[]{:S(2)}, u32[]{:S(2)}) collective-permute-start(bf16[1024,512]{1,0:T(8,128)(2,1)} %get-tuple-element.56), channel_id=1, source_target_pairs={{0,64},{1,65},{2,66},{3,67},{4,68},{5,69},{6,70},{7,71},{8,72},{9,... | collective-permute-start | bytes 3145736 | tf_op jit(solution)/shard_map/ppermute | solution.py:24
  38.3 0.7 copy-start.21
  48.7 27.9 %collective-permute-start.6 = (bf16[512,1024]{1,0:T(8,128)(2,1)}, bf16[512,1024]{1,0:T(8,128)(2,1)}, u32[]{:S(2)}, u32[]{:S(2)}) collective-permute-start(bf16[512,1024]{1,0:T(8,128)(2,1)} %broadcast_select_fusion), channel_id=1, source_target_pairs={{0,64},{1,65},{2,66},{3,67},{4,68},{5,69},{6,70},{7,71},{8,72},{9,... | collective-permute-start | bytes 3145736 | tf_op jit(solution)/shard_map/ppermute | solution.py:24
  96.2 4.2 %collective-permute-start.7 = (bf16[256,1024]{1,0:T(8,128)(2,1)}, bf16[256,1024]{1,0:T(8,128)(2,1)S(1)}, u32[]{:S(2)}, u32[]{:S(2)}) collective-permute-start(bf16[256,1024]{1,0:T(8,128)(2,1)} %get-tuple-element.31.activation_ref.last_ref), channel_id=1, source_target_pairs={{0,1},{1,0},{2,3},{3,2},{4,5},{5,4},{6,7},{7,6},{8,9},{9,8},{10,11... | collective-permute-start | bytes 1572872 | tf_op jit(solution)/shard_map/ppermute | solution.py:32
  96.5 1.6 copy-start.5
  98.1 1.0 copy-start.7
  99.2 1.6 copy-start.6
  100.4 1.6 copy-start.11
  100.5 57.4 %copy-start.9 = (bf16[256,1024]{1,0:T(8,128)(2,1)}, bf16[256,1024]{1,0:T(8,128)(2,1)S(1)}, u32[]{:S(2)}) copy-start(bf16[256,1024]{1,0:T(8,128)(2,1)S(1)} %collective-permute-done.7.activation_ref.other_last_ref) | copy-start | bytes 1572868
  102.0 3.0 %copy-start.14 = (bf16[256,512]{1,0:T(8,128)(2,1)}, bf16[256,512]{1,0:T(8,128)(2,1)S(1)}, u32[]{:S(2)}) copy-start(bf16[256,512]{1,0:T(8,128)(2,1)S(1)} %get-tuple-element.38) | copy-start | bytes 786436
  102.0 9.3 %copy-start.13 = (bf16[256,512]{1,0:T(8,128)(2,1)}, bf16[256,512]{1,0:T(8,128)(2,1)S(1)}, u32[]{:S(2)}) copy-start(bf16[256,512]{1,0:T(8,128)(2,1)S(1)} %get-tuple-element.36) | copy-start | bytes 786436
  102.1 2.0 %collective-permute-start.8 = (bf16[256,1024]{1,0:T(8,128)(2,1)S(1)}, bf16[256,1024]{1,0:T(8,128)(2,1)S(1)}, u32[]{:S(2)}, u32[]{:S(2)}) collective-permute-start(bf16[256,1024]{1,0:T(8,128)(2,1)S(1)} %get-tuple-element.34), channel_id=1, source_target_pairs={{0,1},{1,0},{2,3},{3,2},{4,5},{5,4},{6,7},{7,6},{8,9},{9,8},{10,11... | collective-permute-start | bytes 1572872 | tf_op jit(solution)/shard_map/ppermute | solution.py:32
  105.0 16.9 %copy-start.12 = (bf16[256,512]{1,0:T(8,128)(2,1)S(1)}, bf16[256,512]{1,0:T(8,128)(2,1)}, u32[]{:S(2)}) copy-start(bf16[256,512]{1,0:T(8,128)(2,1)} %copy-done.11) | copy-start | bytes 786436
  105.0 16.9 %copy-start.15 = (bf16[256,512]{1,0:T(8,128)(2,1)S(1)}, bf16[256,512]{1,0:T(8,128)(2,1)}, u32[]{:S(2)}) copy-start(bf16[256,512]{1,0:T(8,128)(2,1)} %copy-done.14) | copy-start | bytes 786436
  105.0 15.3 %all-to-all-start = ((bf16[16,16,1024]{2,1,0:T(8,128)(2,1)}), bf16[16,16,1024]{2,1,0:T(8,128)(2,1)S(1)}, u32[]{:S(2)}, u32[]{:S(2)}) async-start(bf16[16,16,1024]{2,1,0:T(8,128)(2,1)} %bitcast.10), calls=%async_computation | async-start | bytes 1048576 | tf_op jit(solution)/shard_map/all_to_all | solution.py:411
  120.4 3.4 %collective-permute-start.9 = (f32[16,1024]{1,0:T(8,128)S(1)}, f32[16,1024]{1,0:T(8,128)S(1)}, u32[]{:S(2)}, u32[]{:S(2)}) collective-permute-start(f32[16,1024]{1,0:T(8,128)S(1)} %convert_reduce_fusion), channel_id=1, source_target_pairs={{0,32},{32,0},{1,33},{33,1},{2,34},{34,2},{3,35},{35,3},{4,36},{36... | collective-permute-start | bytes 196616 | tf_op jit(solution)/shard_map/ppermute | solution.py:32
  124.7 15.0 %all-to-all-start.1 = ((bf16[16,16,1024]{2,1,0:T(8,128)(2,1)}), bf16[16,16,1024]{2,1,0:T(8,128)(2,1)}, u32[]{:S(2)}, u32[]{:S(2)}) async-start(bf16[16,16,1024]{2,1,0:T(8,128)(2,1)} %broadcast_in_dim.55), calls=%async_computation.1 | async-start | bytes 1048576 | tf_op jit(solution)/shard_map/all_to_all | solution.py:37
  128.9 23.7 %collective-permute-start.12 = (bf16[512,512]{1,0:T(8,128)(2,1)S(1)}, bf16[512,512]{1,0:T(8,128)(2,1)}, u32[]{:S(2)}, u32[]{:S(2)}) collective-permute-start(bf16[512,512]{1,0:T(8,128)(2,1)S(1)} %get-tuple-element.42.here_ref), channel_id=1, source_target_pairs={{64,0},{65,1},{66,2},{67,3},{68,4},{69,5},{70,6},{71,7},{72,8},{73... | collective-permute-start | bytes 1572872 | tf_op jit(solution)/shard_map/ppermute | solution.py:28
  131.4 34.2 %collective-permute-start.10 = (bf16[1024,512]{1,0:T(8,128)(2,1)}, bf16[1024,512]{1,0:T(8,128)(2,1)S(1)}, u32[]{:S(2)}, u32[]{:S(2)}) collective-permute-start(bf16[1024,512]{1,0:T(8,128)(2,1)} %get-tuple-element.39), channel_id=1, source_target_pairs={{0,64},{1,65},{2,66},{3,67},{4,68},{5,69},{6,70},{7,71},{8,72},{9,... | collective-permute-start | bytes 3145736 | tf_op jit(solution)/shard_map/ppermute | solution.py:24
  138.4 27.2 %collective-permute-start.11 = (bf16[512,512]{1,0:T(8,128)(2,1)S(1)}, bf16[512,512]{1,0:T(8,128)(2,1)S(1)}, u32[]{:S(2)}, u32[]{:S(2)}) collective-permute-start(bf16[512,512]{1,0:T(8,128)(2,1)S(1)} %get-tuple-element.40.here_ref), channel_id=1, source_target_pairs={{64,0},{65,1},{66,2},{67,3},{68,4},{69,5},{70,6},{71,7},{72,8},{73... | collective-permute-start | bytes 1572872 | tf_op jit(solution)/shard_map/ppermute | solution.py:28
  147.4 17.3 %collective-permute-start.15 = (f32[5,16,1024]{2,1,0:T(8,128)}, f32[5,16,1024]{2,1,0:T(8,128)S(1)}, u32[]{:S(2)}, u32[]{:S(2)}) collective-permute-start(f32[5,16,1024]{2,1,0:T(8,128)} %get-tuple-element.52), channel_id=1, source_target_pairs={{0,1},{1,0},{2,3},{3,2},{4,5},{5,4},{6,7},{7,6},{8,9},{9,8},{10,11... | collective-permute-start | bytes 983048 | tf_op jit(solution)/shard_map/ppermute | solution.py:32
  151.4 11.2 %collective-permute-start.14 = (bf16[5,16,1024]{2,1,0:T(8,128)(2,1)}, bf16[5,16,1024]{2,1,0:T(8,128)(2,1)S(1)}, u32[]{:S(2)}, u32[]{:S(2)}) collective-permute-start(bf16[5,16,1024]{2,1,0:T(8,128)(2,1)} %get-tuple-element.50), channel_id=1, source_target_pairs={{64,1},{65,0},{66,3},{67,2},{68,5},{69,4},{70,7},{71,6},{72,9},{73... | collective-permute-start | bytes 491528 | tf_op jit(solution)/shard_map/ppermute | solution.py:443
  152.7 5.2 %copy-start.3 = (f32[1,1024,1024]{2,1,0:T(8,128)S(1)}, f32[1,1024,1024]{2,1,0:T(8,128)}, u32[]{:S(2)}) copy-start(f32[1,1024,1024]{2,1,0:T(8,128)} %param.12) | copy-start | bytes 12582916
  152.7 5.2 %copy-start.8 = (bf16[256,1024]{1,0:T(8,128)(2,1)S(1)}, bf16[256,1024]{1,0:T(8,128)(2,1)}, u32[]{:S(2)}) copy-start(bf16[256,1024]{1,0:T(8,128)(2,1)} %get-tuple-element.31.activation_ref.last_ref) | copy-start | bytes 1572868
  152.7 12.0 %collective-permute-start.13 = (bf16[5,16,1024]{2,1,0:T(8,128)(2,1)}, bf16[5,16,1024]{2,1,0:T(8,128)(2,1)S(1)}, u32[]{:S(2)}, u32[]{:S(2)}) collective-permute-start(bf16[5,16,1024]{2,1,0:T(8,128)(2,1)} %get-tuple-element.49), channel_id=1, source_target_pairs={{64,0},{65,1},{66,2},{67,3},{68,4},{69,5},{70,6},{71,7},{72,8},{73... | collective-permute-start | bytes 491528 | tf_op jit(solution)/shard_map/ppermute | solution.py:28
  157.9 6.8 %copy-start.16 = (f32[1,5,16,1024]{3,2,1,0:T(8,128)S(1)}, f32[1,5,16,1024]{3,2,1,0:T(8,128)}, u32[]{:S(2)}) copy-start(f32[1,5,16,1024]{3,2,1,0:T(8,128)} %param.13) | copy-start | bytes 983044
  157.9 6.8 %copy-start.18 = (bf16[5,16,1024]{2,1,0:T(8,128)(2,1)S(1)}, bf16[5,16,1024]{2,1,0:T(8,128)(2,1)}, u32[]{:S(2)}) copy-start(bf16[5,16,1024]{2,1,0:T(8,128)(2,1)} %copy-done.17) | copy-start | bytes 491524
  157.9 6.8 %copy-start.19 = (f32[5,16,1024]{2,1,0:T(8,128)S(1)}, f32[5,16,1024]{2,1,0:T(8,128)}, u32[]{:S(2)}) copy-start(f32[5,16,1024]{2,1,0:T(8,128)} %get-tuple-element.51) | copy-start | bytes 983044
  162.6 3.1 %copy-start.10 = (bf16[256,1024]{1,0:T(8,128)(2,1)S(1)}, bf16[256,1024]{1,0:T(8,128)(2,1)}, u32[]{:S(2)}) copy-start(bf16[256,1024]{1,0:T(8,128)(2,1)} %copy-done.9) | copy-start | bytes 1572868
  165.6 3.1 %copy-start.1 = (bf16[512,1024]{1,0:T(8,128)(2,1)S(1)}, bf16[512,1024]{1,0:T(8,128)(2,1)}, u32[]{:S(2)}) copy-start(bf16[512,1024]{1,0:T(8,128)(2,1)} %param.10) | copy-start | bytes 3145732
Sparse Core Ops, SparseCore 0:
  21.8 63.3 all-gather.2

commit v3 on v2

--- a/solution.py
+++ b/solution.py
@@ -73,48 +73,48 @@
 
 SIZES = (2, 2, 4, 4, 2)
 UNITS = 16
+AHEAD = 3
+CUT = 512
 COLUMNS = 256
 LANES = 128
 VMEM_BYTES = 24 * 1024 * 1024
 WIDE_VMEM = 60 * 1024 * 1024
+FORWARD_VMEM = 57 * 1024 * 1024
+
+
+def fetch(gathered, layer, weights, sem):
+    plane = lax.axis_index("tile_0")
+    places = gathered.shape[0]
+
+    def step(place, carry):
+        for number, half in enumerate((plane, 1 - plane)):
+            row = pl.multiple_of((half * places + place) * UNITS, UNITS)
+            pltpu.make_async_copy(
+                gathered.at[place, number, layer], weights.at[layer, pl.ds(row, UNITS)], sem
+            ).start()
+        return carry
+
+    lax.fori_loop(0, places, step, 0)
 
 
 def forward_kernel(
     gathered, features_ref, tiles_ref, last_ref, slopes_out, weights_out,
-    weights, inputs, slopes, first_sem, rest_sem, out_sems,
+    weights, inputs, slopes, in_sems, out_sems,
 ):
     chip = lax.axis_index(CHIPS)
     own_tile = pl.ds(pl.multiple_of((chip * 2 * UNITS // LANES) * LANES, LANES), LANES)
-    places = gathered.shape[0]
-    plane = lax.axis_index("tile_0")
-
-    def start(first, layers, sem):
-        def step(place, carry):
-            for number, half in enumerate((plane, 1 - plane)):
-                row = pl.multiple_of((half * places + place) * UNITS, UNITS)
-                pltpu.make_async_copy(
-                    gathered.at[place, number, pl.ds(first, layers)],
-                    weights.at[pl.ds(first, layers), pl.ds(row, UNITS)],
-                    sem,
-                ).start()
-            return carry
-
-        lax.fori_loop(0, places, step, 0)
-
-    def finish(first, layers, sem):
-        part = weights.at[pl.ds(first, layers)]
-        pltpu.make_async_copy(part, part, sem).wait()
-
-    start(0, 1, first_sem)
-    start(1, LAYERS - 1, rest_sem)
+    for layer in range(AHEAD):
+        fetch(gathered, layer, weights, in_sems.at[layer])
     inputs[0] = features_ref[...]
-    finish(0, 1, first_sem)
     kept = []
     for layer in range(LAYERS):
-        if layer == 1:
-            finish(1, LAYERS - 1, rest_sem)
+        part = weights.at[layer]
+        pltpu.make_async_copy(part, part, in_sems.at[layer]).wait()
+        if layer + AHEAD < LAYERS:
+            fetch(gathered, layer + AHEAD, weights, in_sems.at[layer + AHEAD])
+        if layer > 0:
             kept.append(
-                pltpu.make_async_copy(weights.at[pl.ds(1, LAYERS - 1)], weights_out, out_sems.at[LAYERS])
+                pltpu.make_async_copy(part, weights_out.at[layer - 1], out_sems.at[LAYERS - 1 + layer])
             )
             kept[-1].start()
         for first in range(0, weights.shape[2], COLUMNS):
@@ -154,11 +154,10 @@
             pltpu.VMEM((LAYERS, width, width), jnp.bfloat16),
             pltpu.VMEM((LAYERS, rows, width), jnp.bfloat16),
             pltpu.VMEM((LAYERS, rows, width), jnp.float32),
-            pltpu.SemaphoreType.DMA(()),
-            pltpu.SemaphoreType.DMA(()),
-            pltpu.SemaphoreType.DMA((LAYERS + 1,)),
+            pltpu.SemaphoreType.DMA((LAYERS,)),
+            pltpu.SemaphoreType.DMA((2 * LAYERS - 1,)),
         ],
-        compiler_params=pltpu.CompilerParams(vmem_limit_bytes=WIDE_VMEM),
+        compiler_params=pltpu.CompilerParams(vmem_limit_bytes=FORWARD_VMEM),
         cost_estimate=pl.CostEstimate(
             flops=2 * LAYERS * rows * width * width,
             bytes_accessed=LAYERS * width * (4 * width + 6 * rows),
@@ -236,7 +235,6 @@
 
 def output_kernel(place_ref, activation_ref, fields_ref, weights_ref, left_ref, right_ref, partial_ref, residual_ref):
     del place_ref
-    chunk = left_ref.shape[1]
     for first in range(0, weights_ref.shape[1], COLUMNS):
         columns = pl.ds(first, COLUMNS)
         predicted = jnp.dot(
@@ -244,8 +242,10 @@
         )
         residual = ((predicted - fields_ref[:, columns]) / BATCH).astype(jnp.bfloat16)
         residual_ref[:, columns] = residual
-        part = left_ref if first < chunk else right_ref
-        part[:, first % chunk : first % chunk + COLUMNS] = residual
+        if first < CUT:
+            left_ref[:, columns] = residual
+        else:
+            right_ref[:, first - CUT : first - CUT + COLUMNS] = residual
     for first in range(0, weights_ref.shape[0], COLUMNS):
         columns = pl.ds(first, COLUMNS)
         partial_ref[:, columns] = lax.dot_general(
@@ -262,8 +262,8 @@
     return pl.pallas_call(
         output_kernel,
         out_shape=(
-            jax.ShapeDtypeStruct((rows, cells // 2), jnp.bfloat16),
-            jax.ShapeDtypeStruct((rows, cells // 2), jnp.bfloat16),
+            jax.ShapeDtypeStruct((rows, CUT), jnp.bfloat16),
+            jax.ShapeDtypeStruct((rows, cells - CUT), jnp.bfloat16),
             jax.ShapeDtypeStruct((rows, width), kind),
         ),
         grid_spec=pltpu.PrefetchScalarGridSpec(
@@ -275,8 +275,8 @@
                 pl.BlockSpec((width, cells), lambda i, place: (0, 0)),
             ],
             out_specs=(
-                pl.BlockSpec((rows, cells // 2), lambda i, place: (0, 0)),
-                pl.BlockSpec((rows, cells // 2), lambda i, place: (0, 0)),
+                pl.BlockSpec((rows, CUT), lambda i, place: (0, 0)),
+                pl.BlockSpec((rows, cells - CUT), lambda i, place: (0, 0)),
                 pl.BlockSpec((rows, width), lambda i, place: (0, 0)),
             ),
             scratch_shapes=[pltpu.VMEM((rows, cells), jnp.bfloat16)],
@@ -291,17 +291,19 @@
 
 
 def update_kernel(
-    solver_ref, own_ref, other_ref, last_ref, other_last_ref, here_ref, far_ref, begun, next_ref, residual
+    solver_ref, own_ref, upper_ref, lower_ref, last_ref, other_last_ref, here_ref, far_ref, begun, next_ref, residual
 ):
     del begun
     solver_side = solver_ref[0] == 1
+    step = pl.program_id(0)
+    upper = step < pl.num_programs(0) // 2
     half = last_ref.shape[0]
 
-    @pl.when(jnp.logical_and(pl.program_id(0) == 0, solver_side))
+    @pl.when(jnp.logical_and(step == 0, solver_side))
     def _():
         residual[...] = far_ref[...]
 
-    @pl.when(jnp.logical_and(pl.program_id(0) == 0, jnp.logical_not(solver_side)))
+    @pl.when(jnp.logical_and(step == 0, jnp.logical_not(solver_side)))
     def _():
         residual[...] = here_ref[...]
 
@@ -311,31 +313,43 @@
         other_last_ref[...], residual[half:], (((0,), (0,)), ((), ())), preferred_element_type=jnp.float32
     )
 
+    def trained(other_ref):
+        momentum = momentum_decay * other_ref[...].astype(jnp.float32) + gradient
+        next_ref[...] = own_ref[...] - step_size * momentum
+
     @pl.when(solver_side)
     def _():
         next_ref[...] = momentum_decay * own_ref[...] + gradient
 
-    @pl.when(jnp.logical_not(solver_side))
+    @pl.when(jnp.logical_and(upper, jnp.logical_not(solver_side)))
     def _():
-        momentum = momentum_decay * other_ref[...].astype(jnp.float32) + gradient
-        next_ref[...] = own_ref[...] - step_size * momentum
-
-
-def updated(chunk, begun, solver_side, own, other, last, other_last, here, far):
+        trained(upper_ref)
+
+    @pl.when(jnp.logical_not(jnp.logical_or(upper, solver_side)))
+    def _():
+        trained(lower_ref)
+
+
+def updated(begun, solver_side, own, upper, lower, last, other_last, here, far):
     width, cells = own.shape
+    size = here.shape[1]
+    steps = width // BLOCK
+    chunk = 0 if begun is None else 1
+    skipped = 0 if lower.shape[0] == width else steps // 2
     half = last.shape[0]
     columns = pl.BlockSpec((half, BLOCK), lambda i, flag: (0, i))
-    whole = pl.BlockSpec((2 * half, cells // 2), lambda i, flag: (0, 0))
-    block = pl.BlockSpec((BLOCK, cells // 2), lambda i, flag: (i, chunk))
+    whole = pl.BlockSpec((2 * half, size), lambda i, flag: (0, 0))
+    block = pl.BlockSpec((BLOCK, size), lambda i, flag: (i, chunk))
     return pl.pallas_call(
         update_kernel,
         out_shape=jax.ShapeDtypeStruct(own.shape, jnp.float32),
         grid_spec=pltpu.PrefetchScalarGridSpec(
             num_scalar_prefetch=1,
-            grid=(width // BLOCK,),
+            grid=(steps,),
             in_specs=[
                 block,
-                pl.BlockSpec((BLOCK, cells // 2), lambda i, flag: (i, 0)),
+                pl.BlockSpec((BLOCK, size), lambda i, flag: (jnp.minimum(i, steps // 2 - 1), 0)),
+                pl.BlockSpec((BLOCK, size), lambda i, flag: (jnp.maximum(i, steps // 2) - skipped, 0)),
                 columns,
                 columns,
                 whole,
@@ -343,16 +357,18 @@
                 pl.BlockSpec(memory_space=pl.ANY),
             ],
             out_specs=block,
-            scratch_shapes=[pltpu.VMEM((2 * half, cells // 2), jnp.bfloat16)],
-        ),
-        input_output_aliases={} if begun is None else {7: 0},
-        compiler_params=pltpu.CompilerParams(vmem_limit_bytes=VMEM_BYTES),
+            scratch_shapes=[pltpu.VMEM((2 * half, size), jnp.bfloat16)],
+        ),
+        input_output_aliases={} if begun is None else {8: 0},
+        compiler_params=pltpu.CompilerParams(
+            vmem_limit_bytes=WIDE_VMEM if begun is None else VMEM_BYTES
+        ),
         cost_estimate=pl.CostEstimate(
-            flops=2 * half * width * cells, bytes_accessed=5 * width * cells, transcendentals=0
+            flops=4 * half * width * size, bytes_accessed=10 * width * size, transcendentals=0
         ),
     )(
-        solver_side.astype(jnp.int32)[None], own, other, last, other_last, here, far,
-        jnp.zeros((8, LANES), jnp.float32) if begun is None else begun,
+        solver_side.astype(jnp.int32)[None], own, upper, lower, last, other_last, here, far,
+        own if begun is None else begun,
     )
 
 
@@ -371,29 +387,33 @@
     half = BATCH // 2
 
     hidden_narrow = own_hidden.astype(jnp.bfloat16)
-    out_narrow = own_out.astype(jnp.bfloat16)
-    edge = jnp.concatenate(
-        [fields[:, -128:], jnp.broadcast_to(velocity[None, -128:], (8, 128))], axis=0
-    )
-
+    first_narrow = own_out[:, :CUT].astype(jnp.bfloat16)
+    upper_narrow = own_out[:BATCH, CUT:].astype(jnp.bfloat16)
+    lower_narrow = own_out[BATCH:, CUT:].astype(jnp.bfloat16)
     partner_hidden = swapped(hidden_narrow, "role")
     near = jnp.where(solver_side, partner_hidden, hidden_narrow)
     far = jnp.where(solver_side, from_trainers(hidden_narrow, 0), from_trainers(hidden_narrow, 1))
     gathered = lax.all_gather(jnp.stack([near, far]), PLANE, axis=0)
 
-    middle = own_out.shape[1] // 2
-    momentum = to_trainer(own_out[:, :middle].astype(jnp.bfloat16))
+    momentum = to_trainer(first_narrow)
+    early, first_narrow = lax.optimization_barrier((fields, first_narrow))
+    edge = jnp.concatenate(
+        [early[:, -128:], jnp.broadcast_to(velocity[None, -128:], (8, 128))], axis=0
+    )
+
     count = lax.axis_size(TILE)
     up = [(i, (i + 1) % count) for i in range(count)]
     down = [(j, i) for i, j in up]
     before = lax.ppermute(edge, TILE, up)
-    after = lax.ppermute(fields[:, :128], TILE, down)
+    after = lax.ppermute(early[:, :128], TILE, down)
+    out_narrow = tied(own_out, before, after).astype(jnp.bfloat16)
     advanced = advance(fields, before, after, velocity, growth)
     carried = jnp.take(advanced.astype(jnp.bfloat16), assignment, axis=0)
     next_batch = to_trainer(carried)
-    gathered, advanced, momentum, next_batch = lax.optimization_barrier(
-        (gathered, advanced, momentum, next_batch)
-    )
+    gathered, advanced, momentum, next_batch, out_narrow = lax.optimization_barrier(
+        (gathered, advanced, momentum, next_batch, out_narrow)
+    )
+    fields_next = jnp.where(solver_side, advanced, next_batch.astype(jnp.float32))
     tiles, last, slopes, weights = forward(
         gathered, lax.dynamic_slice_in_dim(features, core * half, half, 0)
     )
@@ -411,30 +431,36 @@
     shares = lax.all_to_all(
         chip_sum.reshape(chips, rows, width), FLOOR, split_axis=0, concat_axis=0, tiled=True
     )
+    left = jnp.concatenate([left, other_left])
+    left_far = swapped(jnp.where(solver_side, upper_narrow, left), "role")
+    right = jnp.concatenate([right, other_right])
+    payload = jnp.where(solver_side, lower_narrow, right)
+    shares, left_far, fields_next, payload = lax.optimization_barrier(
+        (shares, left_far, fields_next, payload)
+    )
     plane_sum = shares.astype(jnp.float32).sum(axis=0)
     upstream = plane_sum + swapped(plane_sum, "tile_0")
-    upstream, left, right, rest = lax.optimization_barrier(
-        (
-            upstream,
-            jnp.concatenate([left, other_left]),
-            jnp.concatenate([right, other_right]),
-            own_out[:, middle:].astype(jnp.bfloat16),
-        )
-    )
-    left_far, right_far, momentum_rest = to_solver(left), to_solver(right), to_trainer(rest)
     own_factor = lax.dynamic_slice_in_dim(slopes[LAYERS - 1], first, rows, 0)
     own_slope = (upstream * own_factor).astype(jnp.bfloat16)
     slope = from_everyone(own_slope, FLOOR).reshape(half, width)
 
+    tiles = tied(tiles, own_slope)
     own_inputs = jnp.concatenate(
         [
             lax.dynamic_slice_in_dim(tiles, (chip * 2 + side) * units % LANES, units, 2)
             for side in (core, 1 - core)
         ],
         axis=2,
-    )
-    slope, own_inputs = lax.optimization_barrier((slope, own_inputs.swapaxes(1, 2)))
+    ).swapaxes(1, 2)
+    right_far = swapped(tied(payload, own_inputs), "role")
+    out_next = updated(
+        None, solver_side, own_out, momentum, momentum, last, other_last, left, left_far
+    )
+    slope, own_inputs, out_next = lax.optimization_barrier((slope, own_inputs, out_next))
     kept, given, kept_narrow, given_narrow = backward(slope, own_inputs, slopes, weights)
+    kept_narrow, given_narrow, right_far = lax.optimization_barrier(
+        (kept_narrow, given_narrow, right_far)
+    )
     crossing = [
         (flat(SIZES, (1, *place, core)), flat(SIZES, (0, *place, 1 - core)))
         for *place, core in itertools.product(*map(range, SIZES[1:]))
@@ -446,17 +472,13 @@
 
     other_hidden = partner_hidden.astype(jnp.float32)
     out_next = updated(
-        0, None, solver_side, own_out, momentum, last, other_last, left, left_far
-    )
-    out_next = updated(
-        1, out_next, solver_side, own_out, momentum_rest, last, other_last, right, right_far
+        out_next, solver_side, own_out, left_far, right_far, last, other_last, right, right_far
     )
     hidden_next = jnp.where(
         solver_side,
         momentum_decay * own_hidden + grad_hidden_far,
         own_hidden - step_size * (momentum_decay * other_hidden + grad_hidden),
     )
-    fields_next = jnp.where(solver_side, advanced, next_batch.astype(jnp.float32))
     return (fields_next[None], out_next[None], hidden_next[None])
 
 

time: 177 us -> 171 us (0.966)
  starting transfers between devices: 46.1 us -> 37.9 us
  other arithmetic: 19.7 us -> 22 us
    ppermute x3 -> x2, waiting for transfers between devices: 24.9 us -> 7.4 us  [to_trainer(): return lax.ppermute(value, 'role', [(0, 1)])]
    all_gather x1, waiting for transfers between devices: 8.64 us -> 18.3 us  [body(): gathered = lax.all_gather(jnp.stack([near, far]), PLANE, axis=0)]
    ppermute x3 -> x2, starting transfers between devices: 15.6 us -> 8.28 us  [to_trainer(): return lax.ppermute(value, 'role', [(0, 1)])]
    all_to_all x1, waiting for transfers between devices: 9 us -> 3.92 us  [body(): lax.all_to_all(chip_sum.reshape(chips, rows, width), FLOOR, split_axis=0,...]
    ppermute x1, waiting for transfers between devices: 0.01 us -> 5.09 us  [body(): before = lax.ppermute(edge, TILE, up)]
    select_n x0 -> x2, other arithmetic: none -> 4.01 us  [the longest x1 2.83 us: body(): jnp.where(solver_side, advanced, next_batch.astype(jnp.float32))]
    convert_element_type x0 -> x1, other arithmetic: none -> 3.83 us  [body(): out_narrow = tied(own_out, before, after).astype(jnp.bfloat16)]
    ppermute x1, waiting for transfers between devices: 0.01 us -> 3.64 us  [body(): given_far = lax.ppermute(given_narrow, ALL, crossing)]
  transfers between devices with their start and end apart: 19 -> 18, of which waited for: 9 -> 11; matrix products, arithmetic and copies ran while one was open for 15% -> 17% of each run, Pallas kernels for 8% -> 10%
where the time goes in v3:
time: 171 us; the launch traced here: 169 us
  waiting for transfers between devices  51.8 us (30%)
  starting transfers between devices  37.9 us (22%)
  Pallas kernels  29 us (17%)
  other arithmetic  22 us (13%)
  between operations  14.5 us (8%)
  local copies, waits for them, and re-layouts  14.2 us (8%)
    all_gather x1, waiting for transfers between devices, body(): gathered = lax.all_gather(jnp.stack([near, far]), PLANE, axis=0)  18.3 us
    ppermute x7, starting transfers between devices, swapped(): return lax.ppermute(value, axis, [(0, 1), (1, 0)])  12.6 us
    pallas_call x1, Pallas kernels, forward(): pl.pallas_call(forward_kernel, out_shape=(jax.ShapeDtypeStruct((LAYERS, r...  10.1 us
    pallas_call x2, Pallas kernels, updated(): pl.pallas_call(update_kernel, out_shape=jax.ShapeDtypeStruct(own.shape, j...  8.5 us
    ppermute x2, starting transfers between devices, to_trainer(): return lax.ppermute(value, 'role', [(0, 1)])  8.28 us
    pallas_call x1, Pallas kernels, backward(): pl.pallas_call(backward_kernel, out_shape=tuple((jax.ShapeDtypeStruct((LA...  7.9 us
    ppermute x2, waiting for transfers between devices, to_trainer(): return lax.ppermute(value, 'role', [(0, 1)])  7.4 us
    ppermute x7, waiting for transfers between devices, swapped(): return lax.ppermute(value, axis, [(0, 1), (1, 0)])  6.68 us
  transfers between devices with their start and end apart: 18, of which 11 were waited for; matrix products, arithmetic and copies ran while one was open for 17% of the time, Pallas kernels for 10%

profile of v3, /device:TPU:1, one launch (start us, length us, event | category | flops | bytes accessed | tf_op | source)
XLA Modules:
  0.0 169.4 jit_solution(8918194515019113194)
XLA Ops:
  7.2 1.1 bitcast_convert_fusion
  8.3 3.8 %collective-permute-start = (bf16[5,16,1024]{2,1,0:T(8,128)(2,1)S(1)}, bf16[5,16,1024]{2,1,0:T(8,128)(2,1)S(1)}, u32[]{:S(2)}, u32[]{:S(2)}) collective-permute-start(bf16[5,16,1024]{2,1,0:T(8,128)(2,1)S(1)} %bitcast_convert_fusion), channel_id=1, source_target_pairs={{0,64},{64,0},{1,65},{65,1},{2,66},{66,2},{3,67},{67,3},{4,68},{68... | collective-permute-start | bytes 491528 | tf_op jit(solution)/shard_map/ppermute | solution.py:32
  12.1 1.3 collective-permute-start.1
  14.1 1.7 collective-permute-done
  15.8 1.0 select_bitcast_fusion.1
  16.8 3.2 %collective-permute-done.1 = bf16[5,16,1024]{2,1,0:T(8,128)(2,1)S(1)} collective-permute-done((bf16[5,16,1024]{2,1,0:T(8,128)(2,1)S(1)}, bf16[5,16,1024]{2,1,0:T(8,128)(2,1)S(1)}, u32[]{:S(2)}, u32[]{:S(2)}) %collective-permute-start.1) | collective-permute-done | bytes 163872 | tf_op jit(solution)/shard_map/ppermute | solution.py:60
  20.0 0.8 pad_maximum_fusion
  20.8 2.5 %bitcast_convert_fusion.1 = bf16[1024,1024]{1,0:T(8,128)(2,1)S(1)} fusion(f32[1,1024,1024]{2,1,0:T(8,128)} %param.12), kind=kLoop, calls=%fused_computation.39 | loop fusion | flops 1048576 | bytes 6291456 | tf_op jit(solution)/shard_map/convert.3
  23.3 1.1 slice.57
  24.4 6.0 %collective-permute-start.5 = (bf16[1024,512]{1,0:T(8,128)(2,1)}, bf16[1024,512]{1,0:T(8,128)(2,1)}, u32[]{:S(2)}, u32[]{:S(2)}) collective-permute-start(bf16[1024,512]{1,0:T(8,128)(2,1)} %slice.57), channel_id=1, source_target_pairs={{0,64},{1,65},{2,66},{3,67},{4,68},{5,69},{6,70},{7,71},{8,72},{9,... | collective-permute-start | bytes 3145736 | tf_op jit(solution)/shard_map/ppermute | solution.py:24
  30.5 2.3 %collective-permute-start.4 = (f32[512,128]{1,0:T(8,128)S(1)}, f32[512,128]{1,0:T(8,128)S(1)}, u32[]{:S(2)}, u32[]{:S(2)}) collective-permute-start(f32[512,128]{1,0:T(8,128)S(1)} %get-tuple-element.75), channel_id=1, source_target_pairs={{1,0},{2,1},{3,2},{4,3},{5,4},{6,5},{7,6},{8,7},{9,8},{10,9},{11,1... | collective-permute-start | bytes 786440 | tf_op jit(solution)/shard_map/ppermute | solution.py:408
  32.8 1.6 collective-permute-start.3
  34.5 5.1 %collective-permute-done.3 = f32[520,128]{1,0:T(8,128)S(1)} collective-permute-done((f32[520,128]{1,0:T(8,128)S(1)}, f32[520,128]{1,0:T(8,128)S(1)}, u32[]{:S(2)}, u32[]{:S(2)}) %collective-permute-start.3) | collective-permute-done | bytes 266272 | tf_op jit(solution)/shard_map/ppermute | solution.py:407
  41.7 2.4 %fusion.7 = (bf16[512,1024]{1,0:T(8,128)(2,1)}, f32[512,1024]{1,0:T(8,128)}) fusion(f32[1024]{0:T(1024)S(1)} %copy-done.22, f32[512,1025]{1,0:T(8,128)S(1)} %fusion, f32[1,512,1024]{2,1,0:T(8,128)S(1)} %copy-done.3), kind=kLoop, calls=%fused_computation.40 | loop fusion | flops 3670016 | bytes 9441280 | tf_op jit(solution)/shard_map/convert_element_type | solution.py:411
  44.1 4.9 %gather_fusion = bf16[512,1024]{1,0:T(8,128)(2,1)} fusion(bf16[512,1024]{1,0:T(8,128)(2,1)} %get-tuple-element.71, s32[1024]{0:T(1024)S(1)} %pad_clamp_fusion), kind=kCustom, calls=%fused_computation | custom fusion | bytes 2099200 | tf_op jit(solution)/shard_map/jit(_take)/gather | solution.py:411
  49.0 2.4 %broadcast_select_fusion = bf16[512,1024]{1,0:T(8,128)(2,1)} fusion(bf16[512,1024]{1,0:T(8,128)(2,1)} %gather_fusion, pred[512]{0:T(512)(128)(4,1)S(1)} %compare_and_fusion), kind=kLoop, calls=%fused_computation.10 | loop fusion | flops 524288 | bytes 2097664 | tf_op jit(solution)/shard_map/jit(_take)/select_n | solution.py:411
  51.4 2.2 %collective-permute-start.6 = (bf16[512,1024]{1,0:T(8,128)(2,1)}, bf16[512,1024]{1,0:T(8,128)(2,1)}, u32[]{:S(2)}, u32[]{:S(2)}) collective-permute-start(bf16[512,1024]{1,0:T(8,128)(2,1)} %broadcast_select_fusion), channel_id=1, source_target_pairs={{0,64},{1,65},{2,66},{3,67},{4,68},{5,69},{6,70},{7,71},{8,72},{9,... | collective-permute-start | bytes 3145736 | tf_op jit(solution)/shard_map/ppermute | solution.py:24
  53.7 0.9 constant_dynamic-slice_fusion.2.features_ref
  54.6 3.8 %convert_element_type.40.weights_ref = bf16[1024,1024]{1,0:T(8,128)(2,1)} convert(f32[1024,1024]{1,0:T(8,128)} %bitcast.40) | non-fusion elementwise | flops 1048576 | bytes 6291456 | tf_op jit(solution)/shard_map/convert_element_type | solution.py:409
  58.4 7.4 %collective-permute-done.6 = bf16[512,1024]{1,0:T(8,128)(2,1)} collective-permute-done((bf16[512,1024]{1,0:T(8,128)(2,1)}, bf16[512,1024]{1,0:T(8,128)(2,1)}, u32[]{:S(2)}, u32[]{:S(2)}) %collective-permute-start.6) | collective-permute-done | bytes 1048608 | tf_op jit(solution)/shard_map/ppermute | solution.py:24
  65.8 18.3 %all-gather.3.cloned.1.call-done = bf16[64,5,16,1024]{3,2,1,0:T(8,128)(2,1)} async-done(((bf16[2,5,16,1024]{3,2,1,0:T(8,128)(2,1)}), bf16[64,5,16,1024]{3,2,1,0:T(8,128)(2,1)}) %all-gather.3.cloned.1.call-update) | async-done | bytes 10485776 | tf_op jit(solution)/shard_map/all_gather | solution.py:396
  84.1 10.1 %shard_map.94 = (bf16[5,256,128]{2,1,0:T(8,128)(2,1)}, bf16[256,1024]{1,0:T(8,128)(2,1)}, f32[5,256,1024]{2,1,0:T(8,128)}, bf16[4,1024,1024]{2,1,0:T(8,128)(2,1)}) custom-call(bf16[32,2,5,16,1024]{4,3,2,1,0:T(8,128)(2,1)} %bitcast.49, bf16[256,1024]{1,0:T(8,128)(2,1)} %constant_dynamic-slice_fusion.2.features_ref), custom_call_target="tpu_custom_call" | custom-call | flops 2684354560 | bytes 28835840 | tf_op jit(solution)/shard_map/pallas_call | solution.py:143
  94.6 1.0 copy-done.5
  95.6 1.3 shard_map.95
  96.9 1.3 shard_map.96
  98.7 1.2 slice_select_fusion
  99.9 2.7 %collective-permute-start.9 = (bf16[512,512]{1,0:T(8,128)(2,1)}, bf16[512,512]{1,0:T(8,128)(2,1)S(1)}, u32[]{:S(2)}, u32[]{:S(2)}) collective-permute-start(bf16[512,512]{1,0:T(8,128)(2,1)} %get-tuple-element.74), channel_id=1, source_target_pairs={{0,64},{64,0},{1,65},{65,1},{2,66},{66,2},{3,67},{67,3},{4,68},{68... | collective-permute-start | bytes 1572872 | tf_op jit(solution)/shard_map/ppermute | solution.py:32
  102.6 1.0 add_convert_fusion
  103.6 4.9 %all-to-all-start = ((bf16[16,16,1024]{2,1,0:T(8,128)(2,1)}), bf16[16,16,1024]{2,1,0:T(8,128)(2,1)S(1)}, u32[]{:S(2)}, u32[]{:S(2)}) async-start(bf16[16,16,1024]{2,1,0:T(8,128)(2,1)} %bitcast.52), calls=%async_computation | async-start | bytes 1048576 | tf_op jit(solution)/shard_map/all_to_all | solution.py:431
  108.5 2.8 %convert_select_fusion = f32[512,1024]{1,0:T(8,128)} fusion(f32[512,1024]{1,0:T(8,128)S(1)} %copy-done.15, bf16[512,1024]{1,0:T(8,128)(2,1)} %collective-permute-done.6, pred[]{:T(512)S(6)} %eq.6), kind=kLoop, calls=%fused_computation.6 | loop fusion | flops 1048576 | bytes 5242881 | tf_op jit(solution)/shard_map/jit(_where)/select_n | solution.py:416
  111.3 3.5 %collective-permute-done.9.far_ref.upper_ref = bf16[512,512]{1,0:T(8,128)(2,1)S(1)} collective-permute-done((bf16[512,512]{1,0:T(8,128)(2,1)}, bf16[512,512]{1,0:T(8,128)(2,1)S(1)}, u32[]{:S(2)}, u32[]{:S(2)}) %collective-permute-start.9) | collective-permute-done | bytes 524320 | tf_op jit(solution)/shard_map/ppermute | solution.py:32
  114.9 3.9 %all-to-all-done = bf16[16,16,1024]{2,1,0:T(8,128)(2,1)S(1)} async-done(((bf16[16,16,1024]{2,1,0:T(8,128)(2,1)}), bf16[16,16,1024]{2,1,0:T(8,128)(2,1)S(1)}, u32[]{:S(2)}, u32[]{:S(2)}) %all-to-all-start) | async-done | bytes 524320 | tf_op jit(solution)/shard_map/all_to_all | solution.py:431
  119.3 1.3 slice.54
  120.6 1.5 collective-permute-done.10
  122.1 0.8 broadcast_in_dim.50
  122.9 3.6 %all-to-all-start.1 = ((bf16[16,16,1024]{2,1,0:T(8,128)(2,1)}), bf16[16,16,1024]{2,1,0:T(8,128)(2,1)S(1)}, u32[]{:S(2)}, u32[]{:S(2)}) async-start(bf16[16,16,1024]{2,1,0:T(8,128)(2,1)} %broadcast_in_dim.50), calls=%async_computation.1 | async-start | bytes 1048576 | tf_op jit(solution)/shard_map/all_to_all | solution.py:37
  128.1 5.4 %shard_map.97.begun = f32[1024,1024]{1,0:T(8,128)} custom-call(s32[1]{0:T(128)} %bitcast.10.solver_ref, f32[1024,1024]{1,0:T(8,128)} %bitcast.41, bf16[1024,512]{1,0:T(8,128)(2,1)} %collective-permute-done.5.upper_ref.lower_ref, bf16[1024,512]{1,0:T(8,128)(2,1)} %collective-permute-done.5.upper_ref.lower_ref, ...), custom_call_target="tpu_custom_call" | custom-call | flops 536870912 | bytes 5242880 | tf_op jit(solution)/shard_map/pallas_call | solution.py:343
  133.5 2.1 %all-to-all-done.1 = bf16[16,16,1024]{2,1,0:T(8,128)(2,1)S(1)} async-done(((bf16[16,16,1024]{2,1,0:T(8,128)(2,1)}), bf16[16,16,1024]{2,1,0:T(8,128)(2,1)S(1)}, u32[]{:S(2)}, u32[]{:S(2)}) %all-to-all-start.1) | async-done | bytes 524320 | tf_op jit(solution)/shard_map/all_to_all | solution.py:37
  135.5 0.8 copy-done.18
  136.3 7.9 %shard_map.98 = (f32[5,16,1024]{2,1,0:T(8,128)}, f32[5,16,1024]{2,1,0:T(8,128)}, bf16[5,16,1024]{2,1,0:T(8,128)(2,1)}, bf16[5,16,1024]{2,1,0:T(8,128)(2,1)}) custom-call(bf16[256,1024]{1,0:T(8,128)(2,1)} %bitcast.50, bf16[5,32,256]{2,1,0:T(8,128)(2,1)} %maximum_bitcast_fusion.own_inputs_ref, f32[5,256,1024]{2,1,0:T(8,128)} %get-tuple-element.54.slopes_in, ...), custom_call_target="tpu_custom_call" | custom-call | flops 2147483648 | bytes 15728640 | tf_op jit(solution)/shard_map/pallas_call | solution.py:213
  144.2 4.4 %collective-permute-start.14 = (f32[5,16,1024]{2,1,0:T(8,128)}, f32[5,16,1024]{2,1,0:T(8,128)S(1)}, u32[]{:S(2)}, u32[]{:S(2)}) collective-permute-start(f32[5,16,1024]{2,1,0:T(8,128)} %get-tuple-element.70), channel_id=1, source_target_pairs={{0,1},{1,0},{2,3},{3,2},{4,5},{5,4},{6,7},{7,6},{8,9},{9,8},{10,11... | collective-permute-start | bytes 983048 | tf_op jit(solution)/shard_map/ppermute | solution.py:32
  148.6 1.3 collective-permute-start.12
  149.9 1.3 collective-permute-start.13
  151.3 2.2 %copy-done.2 = f32[1,1024,1024]{2,1,0:T(8,128)S(1)} copy-done((f32[1,1024,1024]{2,1,0:T(8,128)S(1)}, f32[1,1024,1024]{2,1,0:T(8,128)}, u32[]{:S(2)}) %copy-start.2) | copy-done | bytes 4194328
  153.5 3.1 %shard_map.99 = f32[1024,1024]{1,0:T(8,128)} custom-call(s32[1]{0:T(128)} %bitcast.10.solver_ref, f32[1024,1024]{1,0:T(8,128)S(1)} %bitcast.43, bf16[512,512]{1,0:T(8,128)(2,1)S(1)} %copy-done.12, bf16[512,512]{1,0:T(8,128)(2,1)S(1)} %collective-permute-done.11.lower_ref.far_ref, bf16[256,1024]{1,0:T(8,128)(2,1)S(1)} %copy-done.6, ...), custom_call_target="tpu_custom_call", output_to_operand_aliasing={{}: (8, {})} | custom-call | flops 536870912 | bytes 5242880 | tf_op jit(solution)/shard_map/pallas_call | solution.py:343
  156.6 1.5 collective-permute-done.12
  158.0 3.6 %collective-permute-done.13 = bf16[5,16,1024]{2,1,0:T(8,128)(2,1)S(1)} collective-permute-done((bf16[5,16,1024]{2,1,0:T(8,128)(2,1)}, bf16[5,16,1024]{2,1,0:T(8,128)(2,1)S(1)}, u32[]{:S(2)}, u32[]{:S(2)}) %collective-permute-start.13) | collective-permute-done | bytes 163872 | tf_op jit(solution)/shard_map/ppermute | solution.py:469
  161.7 0.9 fusion.3
  (79 shorter events, 5.8 us)
Async XLA Ops:
  7.2 46.5 %copy-start = (bf16[512,1024]{1,0:T(8,128)(2,1)S(1)}, bf16[512,1024]{1,0:T(8,128)(2,1)}, u32[]{:S(2)}) copy-start(bf16[512,1024]{1,0:T(8,128)(2,1)} %param.10) | copy-start | bytes 3145732
  7.2 76.9 %all-gather.3.cloned.1.call-start = ((), (), s32[]{:S(2)}) async-start(), calls=%async_computation.2 | async-start | bytes 10813440 | tf_op jit(solution)/shard_map/all_gather | solution.py:396
  8.3 7.5 %collective-permute-start = (bf16[5,16,1024]{2,1,0:T(8,128)(2,1)S(1)}, bf16[5,16,1024]{2,1,0:T(8,128)(2,1)S(1)}, u32[]{:S(2)}, u32[]{:S(2)}) collective-permute-start(bf16[5,16,1024]{2,1,0:T(8,128)(2,1)S(1)} %bitcast_convert_fusion), channel_id=1, source_target_pairs={{0,64},{64,0},{1,65},{65,1},{2,66},{66,2},{3,67},{67,3},{4,68},{68... | collective-permute-start | bytes 491528 | tf_op jit(solution)/shard_map/ppermute | solution.py:32
  12.1 7.8 %collective-permute-start.1 = (bf16[5,16,1024]{2,1,0:T(8,128)(2,1)S(1)}, bf16[5,16,1024]{2,1,0:T(8,128)(2,1)S(1)}, u32[]{:S(2)}, u32[]{:S(2)}) collective-permute-start(bf16[5,16,1024]{2,1,0:T(8,128)(2,1)S(1)} %bitcast_convert_fusion), channel_id=1, source_target_pairs={{64,32},{65,33},{66,34},{67,35},{68,36},{69,37},{70,38},{71,39},{7... | collective-permute-start | bytes 491528 | tf_op jit(solution)/shard_map/ppermute | solution.py:60
  13.4 6.6 %collective-permute-start.2 = (bf16[5,16,1024]{2,1,0:T(8,128)(2,1)S(1)}, bf16[5,16,1024]{2,1,0:T(8,128)(2,1)S(1)}, u32[]{:S(2)}, u32[]{:S(2)}) collective-permute-start(bf16[5,16,1024]{2,1,0:T(8,128)(2,1)S(1)} %bitcast_convert_fusion), channel_id=1, source_target_pairs={{64,96},{65,97},{66,98},{67,99},{68,100},{69,101},{70,102},{71,103... | collective-permute-start | bytes 491528 | tf_op jit(solution)/shard_map/ppermute | solution.py:60
  23.3 17.0 %copy-start.13 = (bf16[1024,1024]{1,0:T(8,128)(2,1)}, bf16[1024,1024]{1,0:T(8,128)(2,1)S(1)}, u32[]{:S(2)}) copy-start(bf16[1024,1024]{1,0:T(8,128)(2,1)S(1)} %bitcast_convert_fusion.1) | copy-start | bytes 6291460
  23.3 7.1 %copy-start.3 = (f32[1,512,1024]{2,1,0:T(8,128)S(1)}, f32[1,512,1024]{2,1,0:T(8,128)}, u32[]{:S(2)}) copy-start(f32[1,512,1024]{2,1,0:T(8,128)} %param.7) | copy-start | bytes 6291460
  23.3 9.5 %copy-start.23 = (f32[1024]{0:T(1024)S(1)}, f32[1024]{0:T(1024)}, u32[]{:S(2)}) copy-start(f32[1024]{0:T(1024)} %param.8) | copy-start | bytes 12292
  23.3 11.1 %copy-start.21 = (s32[512]{0:T(512)S(1)}, s32[512]{0:T(512)}, u32[]{:S(2)}) copy-start(s32[512]{0:T(512)} %param.11) | copy-start | bytes 6148
  24.4 34.0 %collective-permute-start.5 = (bf16[1024,512]{1,0:T(8,128)(2,1)}, bf16[1024,512]{1,0:T(8,128)(2,1)}, u32[]{:S(2)}, u32[]{:S(2)}) collective-permute-start(bf16[1024,512]{1,0:T(8,128)(2,1)} %slice.57), channel_id=1, source_target_pairs={{0,64},{1,65},{2,66},{3,67},{4,68},{5,69},{6,70},{7,71},{8,72},{9,... | collective-permute-start | bytes 3145736 | tf_op jit(solution)/shard_map/ppermute | solution.py:24
  30.5 10.5 %collective-permute-start.4 = (f32[512,128]{1,0:T(8,128)S(1)}, f32[512,128]{1,0:T(8,128)S(1)}, u32[]{:S(2)}, u32[]{:S(2)}) collective-permute-start(f32[512,128]{1,0:T(8,128)S(1)} %get-tuple-element.75), channel_id=1, source_target_pairs={{1,0},{2,1},{3,2},{4,3},{5,4},{6,5},{7,6},{8,7},{9,8},{10,9},{11,1... | collective-permute-start | bytes 786440 | tf_op jit(solution)/shard_map/ppermute | solution.py:408
  32.8 6.7 %collective-permute-start.3 = (f32[520,128]{1,0:T(8,128)S(1)}, f32[520,128]{1,0:T(8,128)S(1)}, u32[]{:S(2)}, u32[]{:S(2)}) collective-permute-start(f32[520,128]{1,0:T(8,128)S(1)} %pad_maximum_fusion.1), channel_id=1, source_target_pairs={{0,1},{1,2},{2,3},{3,4},{4,5},{5,6},{6,7},{7,8},{8,9},{9,10},{10,1... | collective-permute-start | bytes 798728 | tf_op jit(solution)/shard_map/ppermute | solution.py:407
  41.0 0.7 copy-start.22
  51.4 14.4 %collective-permute-start.6 = (bf16[512,1024]{1,0:T(8,128)(2,1)}, bf16[512,1024]{1,0:T(8,128)(2,1)}, u32[]{:S(2)}, u32[]{:S(2)}) collective-permute-start(bf16[512,1024]{1,0:T(8,128)(2,1)} %broadcast_select_fusion), channel_id=1, source_target_pairs={{0,64},{1,65},{2,66},{3,67},{4,68},{5,69},{6,70},{7,71},{8,72},{9,... | collective-permute-start | bytes 3145736 | tf_op jit(solution)/shard_map/ppermute | solution.py:24
  84.1 10.5 %copy-start.4 = (bf16[1024,1024]{1,0:T(8,128)(2,1)S(1)}, bf16[1024,1024]{1,0:T(8,128)(2,1)}, u32[]{:S(2)}) copy-start(bf16[1024,1024]{1,0:T(8,128)(2,1)} %convert_element_type.40.weights_ref) | copy-start | bytes 6291460
  94.2 2.7 %collective-permute-start.7 = (bf16[256,1024]{1,0:T(8,128)(2,1)}, bf16[256,1024]{1,0:T(8,128)(2,1)S(1)}, u32[]{:S(2)}, u32[]{:S(2)}) collective-permute-start(bf16[256,1024]{1,0:T(8,128)(2,1)} %get-tuple-element.40.activation_ref.last_ref), channel_id=1, source_target_pairs={{0,1},{1,0},{2,3},{3,2},{4,5},{5,4},{6,7},{7,6},{8,9},{9,8},{10,11... | collective-permute-start | bytes 1572872 | tf_op jit(solution)/shard_map/ppermute | solution.py:32
  94.6 1.0 copy-start.5
  96.9 1.3 copy-start.7
  96.9 1.8 %copy-start.14 = (bf16[1024,1024]{1,0:T(8,128)(2,1)S(1)}, bf16[1024,1024]{1,0:T(8,128)(2,1)}, u32[]{:S(2)}) copy-start(bf16[1024,1024]{1,0:T(8,128)(2,1)} %copy-done.13) | copy-start | bytes 6291460
  98.2 4.4 %collective-permute-start.8 = (bf16[256,1024]{1,0:T(8,128)(2,1)S(1)}, bf16[256,1024]{1,0:T(8,128)(2,1)S(1)}, u32[]{:S(2)}, u32[]{:S(2)}) collective-permute-start(bf16[256,1024]{1,0:T(8,128)(2,1)S(1)} %get-tuple-element.44), channel_id=1, source_target_pairs={{0,1},{1,0},{2,3},{3,2},{4,5},{5,4},{6,7},{7,6},{8,9},{9,8},{10,11... | collective-permute-start | bytes 1572872 | tf_op jit(solution)/shard_map/ppermute | solution.py:32
  98.6 5.0 %copy-start.16 = (bf16[512,512]{1,0:T(8,128)(2,1)}, bf16[512,512]{1,0:T(8,128)(2,1)S(1)}, u32[]{:S(2)}) copy-start(bf16[512,512]{1,0:T(8,128)(2,1)S(1)} %constant_dynamic-update-slice_fusion.here_ref) | copy-start | bytes 1572868
  98.7 4.9 %copy-start.9 = (bf16[512,512]{1,0:T(8,128)(2,1)}, bf16[512,512]{1,0:T(8,128)(2,1)S(1)}, u32[]{:S(2)}) copy-start(bf16[512,512]{1,0:T(8,128)(2,1)S(1)} %constant_dynamic-update-slice_fusion.2.here_ref) | copy-start | bytes 1572868
  99.9 8.6 %copy-start.15 = (f32[512,1024]{1,0:T(8,128)S(1)}, f32[512,1024]{1,0:T(8,128)}, u32[]{:S(2)}) copy-start(f32[512,1024]{1,0:T(8,128)} %get-tuple-element.47) | copy-start | bytes 6291460
  99.9 15.0 %collective-permute-start.9 = (bf16[512,512]{1,0:T(8,128)(2,1)}, bf16[512,512]{1,0:T(8,128)(2,1)S(1)}, u32[]{:S(2)}, u32[]{:S(2)}) collective-permute-start(bf16[512,512]{1,0:T(8,128)(2,1)} %get-tuple-element.74), channel_id=1, source_target_pairs={{0,64},{64,0},{1,65},{65,1},{2,66},{66,2},{3,67},{67,3},{4,68},{68... | collective-permute-start | bytes 1572872 | tf_op jit(solution)/shard_map/ppermute | solution.py:32
  103.6 15.2 %all-to-all-start = ((bf16[16,16,1024]{2,1,0:T(8,128)(2,1)}), bf16[16,16,1024]{2,1,0:T(8,128)(2,1)S(1)}, u32[]{:S(2)}, u32[]{:S(2)}) async-start(bf16[16,16,1024]{2,1,0:T(8,128)(2,1)} %bitcast.52), calls=%async_computation | async-start | bytes 1048576 | tf_op jit(solution)/shard_map/all_to_all | solution.py:431
  114.9 8.1 %copy-start.11 = (bf16[512,512]{1,0:T(8,128)(2,1)}, bf16[512,512]{1,0:T(8,128)(2,1)S(1)}, u32[]{:S(2)}) copy-start(bf16[512,512]{1,0:T(8,128)(2,1)S(1)} %collective-permute-done.9.far_ref.upper_ref) | copy-start | bytes 1572868
  118.9 7.8 %copy-start.19 = (bf16[5,256,128]{2,1,0:T(8,128)(2,1)S(1)}, bf16[5,256,128]{2,1,0:T(8,128)(2,1)}, u32[]{:S(2)}) copy-start(bf16[5,256,128]{2,1,0:T(8,128)(2,1)} %get-tuple-element.56) | copy-start | bytes 983044
  118.9 3.2 %collective-permute-start.10 = (f32[16,1024]{1,0:T(8,128)S(1)}, f32[16,1024]{1,0:T(8,128)S(1)}, u32[]{:S(2)}, u32[]{:S(2)}) collective-permute-start(f32[16,1024]{1,0:T(8,128)S(1)} %convert_reduce_fusion), channel_id=1, source_target_pairs={{0,32},{32,0},{1,33},{33,1},{2,34},{34,2},{3,35},{35,3},{4,36},{36... | collective-permute-start | bytes 196616 | tf_op jit(solution)/shard_map/ppermute | solution.py:32
  122.9 12.6 %all-to-all-start.1 = ((bf16[16,16,1024]{2,1,0:T(8,128)(2,1)}), bf16[16,16,1024]{2,1,0:T(8,128)(2,1)S(1)}, u32[]{:S(2)}, u32[]{:S(2)}) async-start(bf16[16,16,1024]{2,1,0:T(8,128)(2,1)} %broadcast_in_dim.50), calls=%async_computation.1 | async-start | bytes 1048576 | tf_op jit(solution)/shard_map/all_to_all | solution.py:37
  127.5 21.2 %collective-permute-start.11 = (bf16[512,512]{1,0:T(8,128)(2,1)}, bf16[512,512]{1,0:T(8,128)(2,1)S(1)}, u32[]{:S(2)}, u32[]{:S(2)}) collective-permute-start(bf16[512,512]{1,0:T(8,128)(2,1)} %get-tuple-element.64), channel_id=1, source_target_pairs={{0,64},{64,0},{1,65},{65,1},{2,66},{66,2},{3,67},{67,3},{4,68},{68... | collective-permute-start | bytes 1572872 | tf_op jit(solution)/shard_map/ppermute | solution.py:32
  135.5 0.8 copy-start.18
  136.3 14.9 %copy-start.6 = (bf16[256,1024]{1,0:T(8,128)(2,1)S(1)}, bf16[256,1024]{1,0:T(8,128)(2,1)}, u32[]{:S(2)}) copy-start(bf16[256,1024]{1,0:T(8,128)(2,1)} %get-tuple-element.40.activation_ref.last_ref) | copy-start | bytes 1572868
  136.3 14.9 %copy-start.8 = (bf16[256,1024]{1,0:T(8,128)(2,1)S(1)}, bf16[256,1024]{1,0:T(8,128)(2,1)}, u32[]{:S(2)}) copy-start(bf16[256,1024]{1,0:T(8,128)(2,1)} %copy-done.7) | copy-start | bytes 1572868
  136.3 14.9 %copy-start.10 = (bf16[512,512]{1,0:T(8,128)(2,1)S(1)}, bf16[512,512]{1,0:T(8,128)(2,1)}, u32[]{:S(2)}) copy-start(bf16[512,512]{1,0:T(8,128)(2,1)} %copy-done.9) | copy-start | bytes 1572868
  136.3 14.9 %copy-start.12 = (bf16[512,512]{1,0:T(8,128)(2,1)S(1)}, bf16[512,512]{1,0:T(8,128)(2,1)}, u32[]{:S(2)}) copy-start(bf16[512,512]{1,0:T(8,128)(2,1)} %copy-done.11) | copy-start | bytes 1572868
  144.2 17.4 %collective-permute-start.14 = (f32[5,16,1024]{2,1,0:T(8,128)}, f32[5,16,1024]{2,1,0:T(8,128)S(1)}, u32[]{:S(2)}, u32[]{:S(2)}) collective-permute-start(f32[5,16,1024]{2,1,0:T(8,128)} %get-tuple-element.70), channel_id=1, source_target_pairs={{0,1},{1,0},{2,3},{3,2},{4,5},{5,4},{6,7},{7,6},{8,9},{9,8},{10,11... | collective-permute-start | bytes 983048 | tf_op jit(solution)/shard_map/ppermute | solution.py:32
  148.6 9.4 %collective-permute-start.12 = (bf16[5,16,1024]{2,1,0:T(8,128)(2,1)}, bf16[5,16,1024]{2,1,0:T(8,128)(2,1)S(1)}, u32[]{:S(2)}, u32[]{:S(2)}) collective-permute-start(bf16[5,16,1024]{2,1,0:T(8,128)(2,1)} %get-tuple-element.67), channel_id=1, source_target_pairs={{64,0},{65,1},{66,2},{67,3},{68,4},{69,5},{70,6},{71,7},{72,8},{73... | collective-permute-start | bytes 491528 | tf_op jit(solution)/shard_map/ppermute | solution.py:28
  149.9 11.7 %collective-permute-start.13 = (bf16[5,16,1024]{2,1,0:T(8,128)(2,1)}, bf16[5,16,1024]{2,1,0:T(8,128)(2,1)S(1)}, u32[]{:S(2)}, u32[]{:S(2)}) collective-permute-start(bf16[5,16,1024]{2,1,0:T(8,128)(2,1)} %get-tuple-element.68), channel_id=1, source_target_pairs={{64,1},{65,0},{66,3},{67,2},{68,5},{69,4},{70,7},{71,6},{72,9},{73... | collective-permute-start | bytes 491528 | tf_op jit(solution)/shard_map/ppermute | solution.py:469
  151.3 2.2 %copy-start.2 = (f32[1,1024,1024]{2,1,0:T(8,128)S(1)}, f32[1,1024,1024]{2,1,0:T(8,128)}, u32[]{:S(2)}) copy-start(f32[1,1024,1024]{2,1,0:T(8,128)} %param.12) | copy-start | bytes 12582916
  153.5 8.2 %copy-start.17 = (f32[1,5,16,1024]{3,2,1,0:T(8,128)S(1)}, f32[1,5,16,1024]{3,2,1,0:T(8,128)}, u32[]{:S(2)}) copy-start(f32[1,5,16,1024]{3,2,1,0:T(8,128)} %param.13) | copy-start | bytes 983044
  153.5 8.2 %copy-start.20 = (f32[5,16,1024]{2,1,0:T(8,128)S(1)}, f32[5,16,1024]{2,1,0:T(8,128)}, u32[]{:S(2)}) copy-start(f32[5,16,1024]{2,1,0:T(8,128)} %get-tuple-element.69) | copy-start | bytes 983044
  153.5 9.1 %copy-start.1 = (bf16[512,1024]{1,0:T(8,128)(2,1)S(1)}, bf16[512,1024]{1,0:T(8,128)(2,1)}, u32[]{:S(2)}) copy-start(bf16[512,1024]{1,0:T(8,128)(2,1)} %param.10) | copy-start | bytes 3145732
Sparse Core Ops, SparseCore 0:
  20.9 63.1 all-gather.2

commit v4 on v3

--- a/solution.py
+++ b/solution.py
@@ -73,7 +73,7 @@
 
 SIZES = (2, 2, 4, 4, 2)
 UNITS = 16
-AHEAD = 3
+AHEAD = 5
 CUT = 512
 COLUMNS = 256
 LANES = 128
@@ -82,7 +82,7 @@
 FORWARD_VMEM = 57 * 1024 * 1024
 
 
-def fetch(gathered, layer, weights, sem):
+def fetch(gathered, layer, weights, to, sem):
     plane = lax.axis_index("tile_0")
     places = gathered.shape[0]
 
@@ -90,7 +90,7 @@
         for number, half in enumerate((plane, 1 - plane)):
             row = pl.multiple_of((half * places + place) * UNITS, UNITS)
             pltpu.make_async_copy(
-                gathered.at[place, number, layer], weights.at[layer, pl.ds(row, UNITS)], sem
+                gathered.at[place, number, layer], weights.at[to, pl.ds(row, UNITS)], sem
             ).start()
         return carry
 
@@ -98,25 +98,21 @@
 
 
 def forward_kernel(
-    gathered, features_ref, tiles_ref, last_ref, slopes_out, weights_out,
+    gathered, features_ref, tiles_ref, last_ref, slopes_out,
     weights, inputs, slopes, in_sems, out_sems,
 ):
     chip = lax.axis_index(CHIPS)
     own_tile = pl.ds(pl.multiple_of((chip * 2 * UNITS // LANES) * LANES, LANES), LANES)
     for layer in range(AHEAD):
-        fetch(gathered, layer, weights, in_sems.at[layer])
+        fetch(gathered, layer, weights, layer, in_sems.at[layer])
     inputs[0] = features_ref[...]
     kept = []
     for layer in range(LAYERS):
         part = weights.at[layer]
         pltpu.make_async_copy(part, part, in_sems.at[layer]).wait()
         if layer + AHEAD < LAYERS:
-            fetch(gathered, layer + AHEAD, weights, in_sems.at[layer + AHEAD])
-        if layer > 0:
-            kept.append(
-                pltpu.make_async_copy(part, weights_out.at[layer - 1], out_sems.at[LAYERS - 1 + layer])
-            )
-            kept[-1].start()
+            later = layer + AHEAD
+            fetch(gathered, later, weights, later, in_sems.at[later])
         for first in range(0, weights.shape[2], COLUMNS):
             columns = pl.ds(first, COLUMNS)
             total = jnp.dot(
@@ -146,16 +142,15 @@
             jax.ShapeDtypeStruct((LAYERS, rows, LANES), jnp.bfloat16),
             jax.ShapeDtypeStruct((rows, width), jnp.bfloat16),
             jax.ShapeDtypeStruct((LAYERS, rows, width), jnp.float32),
-            jax.ShapeDtypeStruct((LAYERS - 1, width, width), jnp.bfloat16),
         ),
         in_specs=[hbm, vmem],
-        out_specs=(vmem, vmem, hbm, hbm),
+        out_specs=(vmem, vmem, hbm),
         scratch_shapes=[
             pltpu.VMEM((LAYERS, width, width), jnp.bfloat16),
             pltpu.VMEM((LAYERS, rows, width), jnp.bfloat16),
             pltpu.VMEM((LAYERS, rows, width), jnp.float32),
             pltpu.SemaphoreType.DMA((LAYERS,)),
-            pltpu.SemaphoreType.DMA((2 * LAYERS - 1,)),
+            pltpu.SemaphoreType.DMA((LAYERS,)),
         ],
         compiler_params=pltpu.CompilerParams(vmem_limit_bytes=FORWARD_VMEM),
         cost_estimate=pl.CostEstimate(
@@ -167,27 +162,26 @@
 
 
 def backward_kernel(
-    slope_ref, own_inputs_ref, slopes_in, weights, kept_ref, given_ref, kept_narrow, given_narrow,
+    slope_ref, own_inputs_ref, slopes_in, gathered, kept_ref, given_ref,
     held, slopes, slots, sems,
 ):
-    copies = {}
+    def factor(layer):
+        below = layer - 1
+        return pltpu.make_async_copy(slopes_in.at[below], slopes.at[below], sems.at[1, below])
+
+    def start(layer):
+        fetch(gathered, layer, held, layer - 1, sems.at[0, layer - 1])
+        factor(layer).start()
+
     for layer in range(LAYERS - 1, 0, -1):
-        below = layer - 1
-        copies[layer] = (
-            pltpu.make_async_copy(weights.at[below], held.at[below], sems.at[0, below]),
-            pltpu.make_async_copy(slopes_in.at[below], slopes.at[below], sems.at[1, below]),
-        )
-    for layer in (LAYERS - 1, LAYERS - 2):
-        for copy in copies[layer]:
-            copy.start()
+        start(layer)
     now = slope_ref
     for layer in range(LAYERS - 1, -1, -1):
         if layer > 0:
             later = slots.at[layer % 2]
-            for copy in copies[layer]:
-                copy.wait()
-            for copy in copies.get(layer - 2, ()):
-                copy.start()
+            part = held.at[layer - 1]
+            pltpu.make_async_copy(part, part, sems.at[0, layer - 1]).wait()
+            factor(layer).wait()
             for first in range(0, held.shape[1], COLUMNS):
                 columns = pl.ds(first, COLUMNS)
                 upstream = lax.dot_general(
@@ -200,24 +194,19 @@
         grads = jnp.dot(own_inputs_ref[layer], now[...], preferred_element_type=jnp.float32)
         kept_ref[layer] = grads[:UNITS]
         given_ref[layer] = grads[UNITS:]
-        kept_narrow[layer] = grads[:UNITS].astype(jnp.bfloat16)
-        given_narrow[layer] = grads[UNITS:].astype(jnp.bfloat16)
         if layer > 0:
             now = later
 
 
-def backward(slope, own_inputs, slopes, weights):
+def backward(slope, own_inputs, slopes, gathered):
     rows, width = slope.shape
     vmem = pl.BlockSpec(memory_space=pltpu.VMEM)
     hbm = pl.BlockSpec(memory_space=pltpu.HBM)
     return pl.pallas_call(
         backward_kernel,
-        out_shape=tuple(
-            jax.ShapeDtypeStruct((LAYERS, UNITS, width), kind)
-            for kind in (jnp.float32, jnp.float32, jnp.bfloat16, jnp.bfloat16)
-        ),
+        out_shape=(jax.ShapeDtypeStruct((LAYERS, UNITS, width), jnp.float32),) * 2,
         in_specs=[vmem, vmem, hbm, hbm],
-        out_specs=(vmem,) * 4,
+        out_specs=(vmem,) * 2,
         scratch_shapes=[
             pltpu.VMEM((LAYERS - 1, width, width), jnp.bfloat16),
             pltpu.VMEM((LAYERS - 1, rows, width), jnp.float32),
@@ -230,7 +219,7 @@
             bytes_accessed=LAYERS * width * (2 * width + 4 * rows),
             transcendentals=0,
         ),
-    )(slope, own_inputs, slopes, weights)
+    )(slope, own_inputs, slopes, gathered)
 
 
 def output_kernel(place_ref, activation_ref, fields_ref, weights_ref, left_ref, right_ref, partial_ref, residual_ref):
@@ -390,9 +379,11 @@
     first_narrow = own_out[:, :CUT].astype(jnp.bfloat16)
     upper_narrow = own_out[:BATCH, CUT:].astype(jnp.bfloat16)
     lower_narrow = own_out[BATCH:, CUT:].astype(jnp.bfloat16)
+    across = from_trainers(hidden_narrow, 1)
+    across_far = from_trainers(hidden_narrow, 0)
     partner_hidden = swapped(hidden_narrow, "role")
     near = jnp.where(solver_side, partner_hidden, hidden_narrow)
-    far = jnp.where(solver_side, from_trainers(hidden_narrow, 0), from_trainers(hidden_narrow, 1))
+    far = jnp.where(solver_side, across_far, across)
     gathered = lax.all_gather(jnp.stack([near, far]), PLANE, axis=0)
 
     momentum = to_trainer(first_narrow)
@@ -414,7 +405,7 @@
         (gathered, advanced, momentum, next_batch, out_narrow)
     )
     fields_next = jnp.where(solver_side, advanced, next_batch.astype(jnp.float32))
-    tiles, last, slopes, weights = forward(
+    tiles, last, slopes = forward(
         gathered, lax.dynamic_slice_in_dim(features, core * half, half, 0)
     )
     place = core.astype(jnp.int32)[None]
@@ -439,7 +430,11 @@
         (shares, left_far, fields_next, payload)
     )
     plane_sum = shares.astype(jnp.float32).sum(axis=0)
-    upstream = plane_sum + swapped(plane_sum, "tile_0")
+    across = from_trainers(plane_sum, 1)
+    across_far = from_trainers(plane_sum, 0)
+    upstream = jnp.where(solver_side, to_solver(plane_sum), plane_sum) + jnp.where(
+        solver_side, across_far, across
+    )
     own_factor = lax.dynamic_slice_in_dim(slopes[LAYERS - 1], first, rows, 0)
     own_slope = (upstream * own_factor).astype(jnp.bfloat16)
     slope = from_everyone(own_slope, FLOOR).reshape(half, width)
@@ -457,18 +452,9 @@
         None, solver_side, own_out, momentum, momentum, last, other_last, left, left_far
     )
     slope, own_inputs, out_next = lax.optimization_barrier((slope, own_inputs, out_next))
-    kept, given, kept_narrow, given_narrow = backward(slope, own_inputs, slopes, weights)
-    kept_narrow, given_narrow, right_far = lax.optimization_barrier(
-        (kept_narrow, given_narrow, right_far)
-    )
-    crossing = [
-        (flat(SIZES, (1, *place, core)), flat(SIZES, (0, *place, 1 - core)))
-        for *place, core in itertools.product(*map(range, SIZES[1:]))
-    ]
-    kept_far = to_solver(kept_narrow)
-    given_far = lax.ppermute(given_narrow, ALL, crossing)
+    kept, given = backward(slope, own_inputs, slopes, gathered)
+    given, right_far = lax.optimization_barrier((given, right_far))
     grad_hidden = kept + swapped(given, "tile_3")
-    grad_hidden_far = kept_far.astype(jnp.float32) + given_far.astype(jnp.float32)
 
     other_hidden = partner_hidden.astype(jnp.float32)
     out_next = updated(
@@ -476,7 +462,7 @@
     )
     hidden_next = jnp.where(
         solver_side,
-        momentum_decay * own_hidden + grad_hidden_far,
+        momentum_decay * own_hidden + grad_hidden,
         own_hidden - step_size * (momentum_decay * other_hidden + grad_hidden),
     )
     return (fields_next[None], out_next[None], hidden_next[None])

time: 171 us -> 166 us (0.971)
  waiting for transfers between devices: 51.8 us -> 43.8 us
  starting transfers between devices: 37.9 us -> 40.6 us
    all_gather x1, waiting for transfers between devices: 18.3 us -> 7.99 us  [body(): gathered = lax.all_gather(jnp.stack([near, far]), PLANE, axis=0)]
    ppermute x2, waiting for transfers between devices: 7.4 us -> 14.6 us  [to_trainer(): return lax.ppermute(value, 'role', [(0, 1)])]
    ppermute x1 -> x0, waiting for transfers between devices: 3.64 us -> none  [body(): given_far = lax.ppermute(given_narrow, ALL, crossing)]
    ppermute x7 -> x6, waiting for transfers between devices: 6.68 us -> 4.27 us  [swapped(): return lax.ppermute(value, axis, [(0, 1), (1, 0)])]
    ppermute x1, starting transfers between devices: 2.29 us -> 0.01 us  [body(): after = lax.ppermute(early[:, :128], TILE, down)]
    ppermute x1, starting transfers between devices: 1.62 us -> 3.81 us  [body(): before = lax.ppermute(edge, TILE, up)]
    ppermute x7 -> x6, starting transfers between devices: 12.6 us -> 14.7 us  [swapped(): return lax.ppermute(value, axis, [(0, 1), (1, 0)])]
    all_to_all x1, waiting for transfers between devices: 2.06 us -> 0.01 us  [from_everyone(): return lax.all_to_all(copies, axes, split_axis=0, concat_axis=0, tiled=True)]
  transfers between devices with their start and end apart: 18 -> 18, of which waited for: 11 -> 10; matrix products, arithmetic and copies ran while one was open for 17% -> 18% of each run, Pallas kernels for 10% -> 11%
where the time goes in v4:
time: 166 us; the launch traced here: 165 us
  waiting for transfers between devices  43.8 us (26%)
  starting transfers between devices  40.6 us (24%)
  Pallas kernels  28.3 us (17%)
  other arithmetic  23.5 us (14%)
  between operations  14.4 us (9%)
  local copies, waits for them, and re-layouts  14.2 us (9%)
    ppermute x6, starting transfers between devices, swapped(): return lax.ppermute(value, axis, [(0, 1), (1, 0)])  14.7 us
    ppermute x2, waiting for transfers between devices, to_trainer(): return lax.ppermute(value, 'role', [(0, 1)])  14.6 us
    pallas_call x1, Pallas kernels, forward(): pl.pallas_call(forward_kernel, out_shape=(jax.ShapeDtypeStruct((LAYERS, r...  9.5 us
    pallas_call x2, Pallas kernels, updated(): pl.pallas_call(update_kernel, out_shape=jax.ShapeDtypeStruct(own.shape, j...  8.5 us
    ppermute x2, starting transfers between devices, to_trainer(): return lax.ppermute(value, 'role', [(0, 1)])  8.31 us
    all_gather x1, waiting for transfers between devices, body(): gathered = lax.all_gather(jnp.stack([near, far]), PLANE, axis=0)  7.99 us
    pallas_call x1, Pallas kernels, backward(): pl.pallas_call(backward_kernel, out_shape=(jax.ShapeDtypeStruct((LAYERS,...  7.78 us
    ppermute x1, waiting for transfers between devices, body(): before = lax.ppermute(edge, TILE, up)  5.08 us
  transfers between devices with their start and end apart: 18, of which 10 were waited for; matrix products, arithmetic and copies ran while one was open for 18% of the time, Pallas kernels for 11%

profile of v4, /device:TPU:1, one launch (start us, length us, event | category | flops | bytes accessed | tf_op | source)
XLA Modules:
  0.0 164.8 jit_solution(15048737096432501549)
XLA Ops:
  7.2 1.1 bitcast_convert_fusion
  8.3 3.8 %collective-permute-start = (bf16[5,16,1024]{2,1,0:T(8,128)(2,1)S(1)}, bf16[5,16,1024]{2,1,0:T(8,128)(2,1)S(1)}, u32[]{:S(2)}, u32[]{:S(2)}) collective-permute-start(bf16[5,16,1024]{2,1,0:T(8,128)(2,1)S(1)} %bitcast_convert_fusion), channel_id=1, source_target_pairs={{0,64},{64,0},{1,65},{65,1},{2,66},{66,2},{3,67},{67,3},{4,68},{68... | collective-permute-start | bytes 491528 | tf_op jit(solution)/shard_map/ppermute | solution.py:32
  12.1 1.3 collective-permute-start.1
  14.1 1.7 %collective-permute-done = bf16[5,16,1024]{2,1,0:T(8,128)(2,1)S(1)} collective-permute-done((bf16[5,16,1024]{2,1,0:T(8,128)(2,1)S(1)}, bf16[5,16,1024]{2,1,0:T(8,128)(2,1)S(1)}, u32[]{:S(2)}, u32[]{:S(2)}) %collective-permute-start) | collective-permute-done | bytes 163872 | tf_op jit(solution)/shard_map/ppermute | solution.py:32
  15.8 1.0 select_bitcast_fusion.1
  16.8 3.2 %collective-permute-done.1 = bf16[5,16,1024]{2,1,0:T(8,128)(2,1)S(1)} collective-permute-done((bf16[5,16,1024]{2,1,0:T(8,128)(2,1)S(1)}, bf16[5,16,1024]{2,1,0:T(8,128)(2,1)S(1)}, u32[]{:S(2)}, u32[]{:S(2)}) %collective-permute-start.1) | collective-permute-done | bytes 163872 | tf_op jit(solution)/shard_map/ppermute | solution.py:60
  20.0 0.8 pad_maximum_fusion
  20.8 2.5 %bitcast_convert_fusion.1 = bf16[1024,1024]{1,0:T(8,128)(2,1)S(1)} fusion(f32[1,1024,1024]{2,1,0:T(8,128)} %param.12), kind=kLoop, calls=%fused_computation.39 | loop fusion | flops 1048576 | bytes 6291456 | tf_op jit(solution)/shard_map/convert.3
  23.3 1.1 slice.57
  24.4 6.1 %collective-permute-start.5 = (bf16[1024,512]{1,0:T(8,128)(2,1)}, bf16[1024,512]{1,0:T(8,128)(2,1)}, u32[]{:S(2)}, u32[]{:S(2)}) collective-permute-start(bf16[1024,512]{1,0:T(8,128)(2,1)} %slice.57), channel_id=1, source_target_pairs={{0,64},{1,65},{2,66},{3,67},{4,68},{5,69},{6,70},{7,71},{8,72},{9,... | collective-permute-start | bytes 3145736 | tf_op jit(solution)/shard_map/ppermute | solution.py:24
  30.6 3.8 %collective-permute-start.3 = (f32[520,128]{1,0:T(8,128)S(1)}, f32[520,128]{1,0:T(8,128)S(1)}, u32[]{:S(2)}, u32[]{:S(2)}) collective-permute-start(f32[520,128]{1,0:T(8,128)S(1)} %pad_maximum_fusion.1), channel_id=1, source_target_pairs={{0,1},{1,2},{2,3},{3,4},{4,5},{5,6},{6,7},{7,8},{8,9},{9,10},{10,1... | collective-permute-start | bytes 798728 | tf_op jit(solution)/shard_map/ppermute | solution.py:398
  34.4 5.1 %collective-permute-done.3 = f32[520,128]{1,0:T(8,128)S(1)} collective-permute-done((f32[520,128]{1,0:T(8,128)S(1)}, f32[520,128]{1,0:T(8,128)S(1)}, u32[]{:S(2)}, u32[]{:S(2)}) %collective-permute-start.3) | collective-permute-done | bytes 266272 | tf_op jit(solution)/shard_map/ppermute | solution.py:398
  40.2 0.7 fusion.6
  40.9 1.6 collective-permute-done.4
  43.3 2.4 %fusion.7 = (bf16[512,1024]{1,0:T(8,128)(2,1)}, f32[512,1024]{1,0:T(8,128)}) fusion(f32[1024]{0:T(1024)S(1)} %copy-done.20, f32[512,1025]{1,0:T(8,128)S(1)} %fusion, f32[1,512,1024]{2,1,0:T(8,128)S(1)} %copy-done.2), kind=kLoop, calls=%fused_computation.40 | loop fusion | flops 3670016 | bytes 9441280 | tf_op jit(solution)/shard_map/convert_element_type | solution.py:402
  45.7 4.9 %gather_fusion = bf16[512,1024]{1,0:T(8,128)(2,1)} fusion(bf16[512,1024]{1,0:T(8,128)(2,1)} %get-tuple-element.63, s32[1024]{0:T(1024)S(1)} %pad_clamp_fusion), kind=kCustom, calls=%fused_computation | custom fusion | bytes 2099200 | tf_op jit(solution)/shard_map/jit(_take)/gather | solution.py:402
  50.6 2.4 %broadcast_select_fusion = bf16[512,1024]{1,0:T(8,128)(2,1)} fusion(bf16[512,1024]{1,0:T(8,128)(2,1)} %gather_fusion, pred[512]{0:T(512)(128)(4,1)S(1)} %compare_and_fusion), kind=kLoop, calls=%fused_computation.10 | loop fusion | flops 524288 | bytes 2097664 | tf_op jit(solution)/shard_map/jit(_take)/select_n | solution.py:402
  53.0 2.2 %collective-permute-start.6 = (bf16[512,1024]{1,0:T(8,128)(2,1)}, bf16[512,1024]{1,0:T(8,128)(2,1)}, u32[]{:S(2)}, u32[]{:S(2)}) collective-permute-start(bf16[512,1024]{1,0:T(8,128)(2,1)} %broadcast_select_fusion), channel_id=1, source_target_pairs={{0,64},{1,65},{2,66},{3,67},{4,68},{5,69},{6,70},{7,71},{8,72},{9,... | collective-permute-start | bytes 3145736 | tf_op jit(solution)/shard_map/ppermute | solution.py:24
  55.2 0.8 constant_dynamic-slice_fusion.2.features_ref
  56.1 4.7 %convert_element_type.34.weights_ref = bf16[1024,1024]{1,0:T(8,128)(2,1)} convert(f32[1024,1024]{1,0:T(8,128)} %bitcast.40) | non-fusion elementwise | flops 1048576 | bytes 6291456 | tf_op jit(solution)/shard_map/convert_element_type | solution.py:400
  60.7 14.6 %collective-permute-done.6 = bf16[512,1024]{1,0:T(8,128)(2,1)} collective-permute-done((bf16[512,1024]{1,0:T(8,128)(2,1)}, bf16[512,1024]{1,0:T(8,128)(2,1)}, u32[]{:S(2)}, u32[]{:S(2)}) %collective-permute-start.6) | collective-permute-done | bytes 1048608 | tf_op jit(solution)/shard_map/ppermute | solution.py:24
  75.3 8.0 %all-gather.3.cloned.1.call-done = bf16[64,5,16,1024]{3,2,1,0:T(8,128)(2,1)} async-done(((bf16[2,5,16,1024]{3,2,1,0:T(8,128)(2,1)}), bf16[64,5,16,1024]{3,2,1,0:T(8,128)(2,1)}) %all-gather.3.cloned.1.call-update) | async-done | bytes 10485776 | tf_op jit(solution)/shard_map/all_gather | solution.py:387
  83.3 9.5 %shard_map.94 = (bf16[5,256,128]{2,1,0:T(8,128)(2,1)}, bf16[256,1024]{1,0:T(8,128)(2,1)}, f32[5,256,1024]{2,1,0:T(8,128)}) custom-call(bf16[32,2,5,16,1024]{4,3,2,1,0:T(8,128)(2,1)} %bitcast.48, bf16[256,1024]{1,0:T(8,128)(2,1)} %constant_dynamic-slice_fusion.2.features_ref), custom_call_target="tpu_custom_call" | custom-call | flops 2684354560 | bytes 28835840 | tf_op jit(solution)/shard_map/pallas_call | solution.py:139
  93.2 1.0 copy-done.4
  94.2 1.3 shard_map.95
  95.5 1.3 shard_map.96
  97.3 1.0 slice_select_fusion
  98.3 2.7 %collective-permute-start.9 = (bf16[512,512]{1,0:T(8,128)(2,1)S(1)}, bf16[512,512]{1,0:T(8,128)(2,1)S(1)}, u32[]{:S(2)}, u32[]{:S(2)}) collective-permute-start(bf16[512,512]{1,0:T(8,128)(2,1)S(1)} %get-tuple-element.66), channel_id=1, source_target_pairs={{0,64},{64,0},{1,65},{65,1},{2,66},{66,2},{3,67},{67,3},{4,68},{68... | collective-permute-start | bytes 1572872 | tf_op jit(solution)/shard_map/ppermute | solution.py:32
  101.1 0.9 add_convert_fusion
  102.0 4.9 %all-to-all-start = ((bf16[16,16,1024]{2,1,0:T(8,128)(2,1)}), bf16[16,16,1024]{2,1,0:T(8,128)(2,1)S(1)}, u32[]{:S(2)}, u32[]{:S(2)}) async-start(bf16[16,16,1024]{2,1,0:T(8,128)(2,1)} %bitcast.8), calls=%async_computation | async-start | bytes 1048576 | tf_op jit(solution)/shard_map/all_to_all | solution.py:422
  106.9 3.6 %convert_select_fusion = f32[512,1024]{1,0:T(8,128)} fusion(f32[512,1024]{1,0:T(8,128)} %get-tuple-element.43, bf16[512,1024]{1,0:T(8,128)(2,1)} %collective-permute-done.6, pred[]{:T(512)S(6)} %eq.6), kind=kLoop, calls=%fused_computation.6 | loop fusion | flops 1048576 | bytes 5242881 | tf_op jit(solution)/shard_map/jit(_where)/select_n | solution.py:407
  110.5 2.6 %collective-permute-done.9.far_ref.upper_ref = bf16[512,512]{1,0:T(8,128)(2,1)S(1)} collective-permute-done((bf16[512,512]{1,0:T(8,128)(2,1)S(1)}, bf16[512,512]{1,0:T(8,128)(2,1)S(1)}, u32[]{:S(2)}, u32[]{:S(2)}) %collective-permute-start.9) | collective-permute-done | bytes 524320 | tf_op jit(solution)/shard_map/ppermute | solution.py:32
  113.1 4.1 %all-to-all-done = bf16[16,16,1024]{2,1,0:T(8,128)(2,1)S(1)} async-done(((bf16[16,16,1024]{2,1,0:T(8,128)(2,1)}), bf16[16,16,1024]{2,1,0:T(8,128)(2,1)S(1)}, u32[]{:S(2)}, u32[]{:S(2)}) %all-to-all-start) | async-done | bytes 524320 | tf_op jit(solution)/shard_map/all_to_all | solution.py:422
  117.3 1.3 collective-permute-start.10
  118.6 1.3 collective-permute-start.11
  120.6 1.3 slice.54
  121.9 1.9 %collective-permute-done.10 = f32[16,1024]{1,0:T(8,128)S(1)} collective-permute-done((f32[16,1024]{1,0:T(8,128)S(1)}, f32[16,1024]{1,0:T(8,128)S(1)}, u32[]{:S(2)}, u32[]{:S(2)}) %collective-permute-start.10) | collective-permute-done | bytes 65568 | tf_op jit(solution)/shard_map/ppermute | solution.py:28
  123.8 1.0 collective-permute-done.11
  125.1 0.9 broadcast_in_dim.50
  125.9 3.6 %all-to-all-start.1 = ((bf16[16,16,1024]{2,1,0:T(8,128)(2,1)}), bf16[16,16,1024]{2,1,0:T(8,128)(2,1)S(1)}, u32[]{:S(2)}, u32[]{:S(2)}) async-start(bf16[16,16,1024]{2,1,0:T(8,128)(2,1)} %broadcast_in_dim.50), calls=%async_computation.1 | async-start | bytes 1048576 | tf_op jit(solution)/shard_map/all_to_all | solution.py:37
  130.2 3.6 %collective-permute-start.13 = (bf16[512,512]{1,0:T(8,128)(2,1)}, bf16[512,512]{1,0:T(8,128)(2,1)S(1)}, u32[]{:S(2)}, u32[]{:S(2)}) collective-permute-start(bf16[512,512]{1,0:T(8,128)(2,1)} %get-tuple-element.58), channel_id=1, source_target_pairs={{0,64},{64,0},{1,65},{65,1},{2,66},{66,2},{3,67},{67,3},{4,68},{68... | collective-permute-start | bytes 1572872 | tf_op jit(solution)/shard_map/ppermute | solution.py:32
  133.9 5.4 %shard_map.97.begun = f32[1024,1024]{1,0:T(8,128)} custom-call(s32[1]{0:T(128)} %bitcast.10.solver_ref, f32[1024,1024]{1,0:T(8,128)} %bitcast.41, bf16[1024,512]{1,0:T(8,128)(2,1)} %collective-permute-done.5.upper_ref.lower_ref, bf16[1024,512]{1,0:T(8,128)(2,1)} %collective-permute-done.5.upper_ref.lower_ref, ...), custom_call_target="tpu_custom_call" | custom-call | flops 536870912 | bytes 5242880 | tf_op jit(solution)/shard_map/pallas_call | solution.py:332
  139.3 0.8 copy-done.16
  140.1 7.8 %shard_map.98 = (f32[5,16,1024]{2,1,0:T(8,128)}, f32[5,16,1024]{2,1,0:T(8,128)}) custom-call(bf16[256,1024]{1,0:T(8,128)(2,1)} %bitcast.51, bf16[5,32,256]{2,1,0:T(8,128)(2,1)} %maximum_bitcast_fusion.own_inputs_ref, f32[5,256,1024]{2,1,0:T(8,128)} %get-tuple-element.50.slopes_in, bf16[32,2,5,16,1024]{4,3,2,1,0:T(8,128)(2,1)} %bitcast.49), custom_call_target="tpu_custom_call" | custom-call | flops 2147483648 | bytes 15728640 | tf_op jit(solution)/shard_map/pallas_call | solution.py:205
  147.9 3.9 %collective-permute-start.14 = (f32[5,16,1024]{2,1,0:T(8,128)}, f32[5,16,1024]{2,1,0:T(8,128)S(1)}, u32[]{:S(2)}, u32[]{:S(2)}) collective-permute-start(f32[5,16,1024]{2,1,0:T(8,128)} %get-tuple-element.62), channel_id=1, source_target_pairs={{0,1},{1,0},{2,3},{3,2},{4,5},{5,4},{6,7},{7,6},{8,9},{9,8},{10,11... | collective-permute-start | bytes 983048 | tf_op jit(solution)/shard_map/ppermute | solution.py:32
  151.8 2.2 %copy-done.1 = f32[1,1024,1024]{2,1,0:T(8,128)S(1)} copy-done((f32[1,1024,1024]{2,1,0:T(8,128)S(1)}, f32[1,1024,1024]{2,1,0:T(8,128)}, u32[]{:S(2)}) %copy-start.1) | copy-done | bytes 4194328
  154.0 3.1 %shard_map.99 = f32[1024,1024]{1,0:T(8,128)} custom-call(s32[1]{0:T(128)} %bitcast.10.solver_ref, f32[1024,1024]{1,0:T(8,128)S(1)} %bitcast.43, bf16[512,512]{1,0:T(8,128)(2,1)S(1)} %copy-done.11, bf16[512,512]{1,0:T(8,128)(2,1)S(1)} %collective-permute-done.13.lower_ref.far_ref, bf16[256,1024]{1,0:T(8,128)(2,1)S(1)} %copy-done.5, ...), custom_call_target="tpu_custom_call", output_to_operand_aliasing={{}: (8, {})} | custom-call | flops 536870912 | bytes 5242880 | tf_op jit(solution)/shard_map/pallas_call | solution.py:332
  157.1 0.8 fusion.3
  (75 shorter events, 4.8 us)
Async XLA Ops:
  7.2 48.1 %copy-start = (bf16[512,1024]{1,0:T(8,128)(2,1)S(1)}, bf16[512,1024]{1,0:T(8,128)(2,1)}, u32[]{:S(2)}) copy-start(bf16[512,1024]{1,0:T(8,128)(2,1)} %param.10) | copy-start | bytes 3145732
  7.2 76.1 %all-gather.3.cloned.1.call-start = ((), (), s32[]{:S(2)}) async-start(), calls=%async_computation.2 | async-start | bytes 10813440 | tf_op jit(solution)/shard_map/all_gather | solution.py:387
  8.3 7.5 %collective-permute-start = (bf16[5,16,1024]{2,1,0:T(8,128)(2,1)S(1)}, bf16[5,16,1024]{2,1,0:T(8,128)(2,1)S(1)}, u32[]{:S(2)}, u32[]{:S(2)}) collective-permute-start(bf16[5,16,1024]{2,1,0:T(8,128)(2,1)S(1)} %bitcast_convert_fusion), channel_id=1, source_target_pairs={{0,64},{64,0},{1,65},{65,1},{2,66},{66,2},{3,67},{67,3},{4,68},{68... | collective-permute-start | bytes 491528 | tf_op jit(solution)/shard_map/ppermute | solution.py:32
  12.1 7.8 %collective-permute-start.1 = (bf16[5,16,1024]{2,1,0:T(8,128)(2,1)S(1)}, bf16[5,16,1024]{2,1,0:T(8,128)(2,1)S(1)}, u32[]{:S(2)}, u32[]{:S(2)}) collective-permute-start(bf16[5,16,1024]{2,1,0:T(8,128)(2,1)S(1)} %bitcast_convert_fusion), channel_id=1, source_target_pairs={{64,32},{65,33},{66,34},{67,35},{68,36},{69,37},{70,38},{71,39},{7... | collective-permute-start | bytes 491528 | tf_op jit(solution)/shard_map/ppermute | solution.py:60
  13.4 6.6 %collective-permute-start.2 = (bf16[5,16,1024]{2,1,0:T(8,128)(2,1)S(1)}, bf16[5,16,1024]{2,1,0:T(8,128)(2,1)S(1)}, u32[]{:S(2)}, u32[]{:S(2)}) collective-permute-start(bf16[5,16,1024]{2,1,0:T(8,128)(2,1)S(1)} %bitcast_convert_fusion), channel_id=1, source_target_pairs={{64,96},{65,97},{66,98},{67,99},{68,100},{69,101},{70,102},{71,103... | collective-permute-start | bytes 491528 | tf_op jit(solution)/shard_map/ppermute | solution.py:60
  20.8 9.7 %copy-start.21 = (f32[1024]{0:T(1024)S(1)}, f32[1024]{0:T(1024)}, u32[]{:S(2)}) copy-start(f32[1024]{0:T(1024)} %param.8) | copy-start | bytes 12292
  23.3 16.9 %copy-start.12 = (bf16[1024,1024]{1,0:T(8,128)(2,1)}, bf16[1024,1024]{1,0:T(8,128)(2,1)S(1)}, u32[]{:S(2)}) copy-start(bf16[1024,1024]{1,0:T(8,128)(2,1)S(1)} %bitcast_convert_fusion.1) | copy-start | bytes 6291460
  23.3 7.2 %copy-start.2 = (f32[1,512,1024]{2,1,0:T(8,128)S(1)}, f32[1,512,1024]{2,1,0:T(8,128)}, u32[]{:S(2)}) copy-start(f32[1,512,1024]{2,1,0:T(8,128)} %param.7) | copy-start | bytes 6291460
  23.3 11.0 %copy-start.19 = (s32[512]{0:T(512)S(1)}, s32[512]{0:T(512)}, u32[]{:S(2)}) copy-start(s32[512]{0:T(512)} %param.11) | copy-start | bytes 6148
  24.4 36.3 %collective-permute-start.5 = (bf16[1024,512]{1,0:T(8,128)(2,1)}, bf16[1024,512]{1,0:T(8,128)(2,1)}, u32[]{:S(2)}, u32[]{:S(2)}) collective-permute-start(bf16[1024,512]{1,0:T(8,128)(2,1)} %slice.57), channel_id=1, source_target_pairs={{0,64},{1,65},{2,66},{3,67},{4,68},{5,69},{6,70},{7,71},{8,72},{9,... | collective-permute-start | bytes 3145736 | tf_op jit(solution)/shard_map/ppermute | solution.py:24
  30.6 8.9 %collective-permute-start.3 = (f32[520,128]{1,0:T(8,128)S(1)}, f32[520,128]{1,0:T(8,128)S(1)}, u32[]{:S(2)}, u32[]{:S(2)}) collective-permute-start(f32[520,128]{1,0:T(8,128)S(1)} %pad_maximum_fusion.1), channel_id=1, source_target_pairs={{0,1},{1,2},{2,3},{3,4},{4,5},{5,6},{6,7},{7,8},{8,9},{9,10},{10,1... | collective-permute-start | bytes 798728 | tf_op jit(solution)/shard_map/ppermute | solution.py:398
  34.4 8.2 %collective-permute-start.4 = (f32[512,128]{1,0:T(8,128)S(1)}, f32[512,128]{1,0:T(8,128)S(1)}, u32[]{:S(2)}, u32[]{:S(2)}) collective-permute-start(f32[512,128]{1,0:T(8,128)S(1)} %get-tuple-element.67), channel_id=1, source_target_pairs={{1,0},{2,1},{3,2},{4,3},{5,4},{6,5},{7,6},{8,7},{9,8},{10,9},{11,1... | collective-permute-start | bytes 786440 | tf_op jit(solution)/shard_map/ppermute | solution.py:399
  42.5 0.7 copy-start.20
  53.0 22.3 %collective-permute-start.6 = (bf16[512,1024]{1,0:T(8,128)(2,1)}, bf16[512,1024]{1,0:T(8,128)(2,1)}, u32[]{:S(2)}, u32[]{:S(2)}) collective-permute-start(bf16[512,1024]{1,0:T(8,128)(2,1)} %broadcast_select_fusion), channel_id=1, source_target_pairs={{0,64},{1,65},{2,66},{3,67},{4,68},{5,69},{6,70},{7,71},{8,72},{9,... | collective-permute-start | bytes 3145736 | tf_op jit(solution)/shard_map/ppermute | solution.py:24
  83.3 9.8 %copy-start.3 = (bf16[1024,1024]{1,0:T(8,128)(2,1)S(1)}, bf16[1024,1024]{1,0:T(8,128)(2,1)}, u32[]{:S(2)}) copy-start(bf16[1024,1024]{1,0:T(8,128)(2,1)} %convert_element_type.34.weights_ref) | copy-start | bytes 6291460
  92.8 2.7 %collective-permute-start.7 = (bf16[256,1024]{1,0:T(8,128)(2,1)}, bf16[256,1024]{1,0:T(8,128)(2,1)S(1)}, u32[]{:S(2)}, u32[]{:S(2)}) collective-permute-start(bf16[256,1024]{1,0:T(8,128)(2,1)} %get-tuple-element.36.activation_ref.last_ref), channel_id=1, source_target_pairs={{0,1},{1,0},{2,3},{3,2},{4,5},{5,4},{6,7},{7,6},{8,9},{9,8},{10,11... | collective-permute-start | bytes 1572872 | tf_op jit(solution)/shard_map/ppermute | solution.py:32
  93.2 1.0 copy-start.4
  95.5 1.3 copy-start.6
  95.5 1.8 %copy-start.13 = (bf16[1024,1024]{1,0:T(8,128)(2,1)S(1)}, bf16[1024,1024]{1,0:T(8,128)(2,1)}, u32[]{:S(2)}) copy-start(bf16[1024,1024]{1,0:T(8,128)(2,1)} %copy-done.12) | copy-start | bytes 6291460
  96.8 4.3 %collective-permute-start.8 = (bf16[256,1024]{1,0:T(8,128)(2,1)S(1)}, bf16[256,1024]{1,0:T(8,128)(2,1)S(1)}, u32[]{:S(2)}, u32[]{:S(2)}) collective-permute-start(bf16[256,1024]{1,0:T(8,128)(2,1)S(1)} %get-tuple-element.40), channel_id=1, source_target_pairs={{0,1},{1,0},{2,3},{3,2},{4,5},{5,4},{6,7},{7,6},{8,9},{9,8},{10,11... | collective-permute-start | bytes 1572872 | tf_op jit(solution)/shard_map/ppermute | solution.py:32
  97.2 4.8 %copy-start.14 = (bf16[512,512]{1,0:T(8,128)(2,1)}, bf16[512,512]{1,0:T(8,128)(2,1)S(1)}, u32[]{:S(2)}) copy-start(bf16[512,512]{1,0:T(8,128)(2,1)S(1)} %constant_dynamic-update-slice_fusion.here_ref) | copy-start | bytes 1572868
  97.3 4.7 %copy-start.8 = (bf16[512,512]{1,0:T(8,128)(2,1)}, bf16[512,512]{1,0:T(8,128)(2,1)S(1)}, u32[]{:S(2)}) copy-start(bf16[512,512]{1,0:T(8,128)(2,1)S(1)} %constant_dynamic-update-slice_fusion.2.here_ref) | copy-start | bytes 1572868
  98.3 14.8 %collective-permute-start.9 = (bf16[512,512]{1,0:T(8,128)(2,1)S(1)}, bf16[512,512]{1,0:T(8,128)(2,1)S(1)}, u32[]{:S(2)}, u32[]{:S(2)}) collective-permute-start(bf16[512,512]{1,0:T(8,128)(2,1)S(1)} %get-tuple-element.66), channel_id=1, source_target_pairs={{0,64},{64,0},{1,65},{65,1},{2,66},{66,2},{3,67},{67,3},{4,68},{68... | collective-permute-start | bytes 1572872 | tf_op jit(solution)/shard_map/ppermute | solution.py:32
  102.0 15.2 %all-to-all-start = ((bf16[16,16,1024]{2,1,0:T(8,128)(2,1)}), bf16[16,16,1024]{2,1,0:T(8,128)(2,1)S(1)}, u32[]{:S(2)}, u32[]{:S(2)}) async-start(bf16[16,16,1024]{2,1,0:T(8,128)(2,1)} %bitcast.8), calls=%async_computation | async-start | bytes 1048576 | tf_op jit(solution)/shard_map/all_to_all | solution.py:422
  110.5 14.3 %copy-start.17 = (bf16[5,256,128]{2,1,0:T(8,128)(2,1)S(1)}, bf16[5,256,128]{2,1,0:T(8,128)(2,1)}, u32[]{:S(2)}) copy-start(bf16[5,256,128]{2,1,0:T(8,128)(2,1)} %get-tuple-element.52) | copy-start | bytes 983044
  113.1 12.8 %copy-start.10 = (bf16[512,512]{1,0:T(8,128)(2,1)}, bf16[512,512]{1,0:T(8,128)(2,1)S(1)}, u32[]{:S(2)}) copy-start(bf16[512,512]{1,0:T(8,128)(2,1)S(1)} %collective-permute-done.9.far_ref.upper_ref) | copy-start | bytes 1572868
  117.3 6.5 %collective-permute-start.10 = (f32[16,1024]{1,0:T(8,128)S(1)}, f32[16,1024]{1,0:T(8,128)S(1)}, u32[]{:S(2)}, u32[]{:S(2)}) collective-permute-start(f32[16,1024]{1,0:T(8,128)S(1)} %convert_reduce_fusion), channel_id=1, source_target_pairs={{64,0},{65,1},{66,2},{67,3},{68,4},{69,5},{70,6},{71,7},{72,8},{73... | collective-permute-start | bytes 196616 | tf_op jit(solution)/shard_map/ppermute | solution.py:28
  118.6 6.2 %collective-permute-start.11 = (f32[16,1024]{1,0:T(8,128)S(1)}, f32[16,1024]{1,0:T(8,128)S(1)}, u32[]{:S(2)}, u32[]{:S(2)}) collective-permute-start(f32[16,1024]{1,0:T(8,128)S(1)} %convert_reduce_fusion), channel_id=1, source_target_pairs={{64,32},{65,33},{66,34},{67,35},{68,36},{69,37},{70,38},{71,39},{7... | collective-permute-start | bytes 196616 | tf_op jit(solution)/shard_map/ppermute | solution.py:60
  119.9 4.9 %collective-permute-start.12 = (f32[16,1024]{1,0:T(8,128)S(1)}, f32[16,1024]{1,0:T(8,128)S(1)}, u32[]{:S(2)}, u32[]{:S(2)}) collective-permute-start(f32[16,1024]{1,0:T(8,128)S(1)} %convert_reduce_fusion), channel_id=1, source_target_pairs={{64,96},{65,97},{66,98},{67,99},{68,100},{69,101},{70,102},{71,103... | collective-permute-start | bytes 196616 | tf_op jit(solution)/shard_map/ppermute | solution.py:60
  125.9 13.4 %all-to-all-start.1 = ((bf16[16,16,1024]{2,1,0:T(8,128)(2,1)}), bf16[16,16,1024]{2,1,0:T(8,128)(2,1)S(1)}, u32[]{:S(2)}, u32[]{:S(2)}) async-start(bf16[16,16,1024]{2,1,0:T(8,128)(2,1)} %broadcast_in_dim.50), calls=%async_computation.1 | async-start | bytes 1048576 | tf_op jit(solution)/shard_map/all_to_all | solution.py:37
  130.2 17.6 %collective-permute-start.13 = (bf16[512,512]{1,0:T(8,128)(2,1)}, bf16[512,512]{1,0:T(8,128)(2,1)S(1)}, u32[]{:S(2)}, u32[]{:S(2)}) collective-permute-start(bf16[512,512]{1,0:T(8,128)(2,1)} %get-tuple-element.58), channel_id=1, source_target_pairs={{0,64},{64,0},{1,65},{65,1},{2,66},{66,2},{3,67},{67,3},{4,68},{68... | collective-permute-start | bytes 1572872 | tf_op jit(solution)/shard_map/ppermute | solution.py:32
  139.3 0.8 copy-start.16
  140.1 11.7 %copy-start.5 = (bf16[256,1024]{1,0:T(8,128)(2,1)S(1)}, bf16[256,1024]{1,0:T(8,128)(2,1)}, u32[]{:S(2)}) copy-start(bf16[256,1024]{1,0:T(8,128)(2,1)} %get-tuple-element.36.activation_ref.last_ref) | copy-start | bytes 1572868
  140.1 11.7 %copy-start.7 = (bf16[256,1024]{1,0:T(8,128)(2,1)S(1)}, bf16[256,1024]{1,0:T(8,128)(2,1)}, u32[]{:S(2)}) copy-start(bf16[256,1024]{1,0:T(8,128)(2,1)} %copy-done.6) | copy-start | bytes 1572868
  140.1 11.7 %copy-start.9 = (bf16[512,512]{1,0:T(8,128)(2,1)S(1)}, bf16[512,512]{1,0:T(8,128)(2,1)}, u32[]{:S(2)}) copy-start(bf16[512,512]{1,0:T(8,128)(2,1)} %copy-done.8) | copy-start | bytes 1572868
  140.1 11.7 %copy-start.11 = (bf16[512,512]{1,0:T(8,128)(2,1)S(1)}, bf16[512,512]{1,0:T(8,128)(2,1)}, u32[]{:S(2)}) copy-start(bf16[512,512]{1,0:T(8,128)(2,1)} %copy-done.10) | copy-start | bytes 1572868
  147.9 9.2 %collective-permute-start.14 = (f32[5,16,1024]{2,1,0:T(8,128)}, f32[5,16,1024]{2,1,0:T(8,128)S(1)}, u32[]{:S(2)}, u32[]{:S(2)}) collective-permute-start(f32[5,16,1024]{2,1,0:T(8,128)} %get-tuple-element.62), channel_id=1, source_target_pairs={{0,1},{1,0},{2,3},{3,2},{4,5},{5,4},{6,7},{7,6},{8,9},{9,8},{10,11... | collective-permute-start | bytes 983048 | tf_op jit(solution)/shard_map/ppermute | solution.py:32
  151.8 2.2 %copy-start.1 = (f32[1,1024,1024]{2,1,0:T(8,128)S(1)}, f32[1,1024,1024]{2,1,0:T(8,128)}, u32[]{:S(2)}) copy-start(f32[1,1024,1024]{2,1,0:T(8,128)} %param.12) | copy-start | bytes 12582916
  154.0 3.1 %copy-start.15 = (f32[1,5,16,1024]{3,2,1,0:T(8,128)S(1)}, f32[1,5,16,1024]{3,2,1,0:T(8,128)}, u32[]{:S(2)}) copy-start(f32[1,5,16,1024]{3,2,1,0:T(8,128)} %param.13) | copy-start | bytes 983044
  154.0 3.1 %copy-start.18 = (f32[5,16,1024]{2,1,0:T(8,128)S(1)}, f32[5,16,1024]{2,1,0:T(8,128)}, u32[]{:S(2)}) copy-start(f32[5,16,1024]{2,1,0:T(8,128)} %get-tuple-element.61) | copy-start | bytes 983044
Sparse Core Ops, SparseCore 0:
  20.9 62.3 all-gather.2

commit v5 on v4

--- a/solution.py
+++ b/solution.py
@@ -361,7 +361,7 @@
     )
 
 
-BLOCK = 256
+BLOCK = 512
 
 
 def body(fields_pair, velocity, growth, features, assignment, out_pair, hidden_pair):
@@ -430,11 +430,10 @@
         (shares, left_far, fields_next, payload)
     )
     plane_sum = shares.astype(jnp.float32).sum(axis=0)
+    straight = to_solver(plane_sum)
+    across_far = from_trainers(plane_sum, 0)
     across = from_trainers(plane_sum, 1)
-    across_far = from_trainers(plane_sum, 0)
-    upstream = jnp.where(solver_side, to_solver(plane_sum), plane_sum) + jnp.where(
-        solver_side, across_far, across
-    )
+    upstream = jnp.where(solver_side, straight, plane_sum) + jnp.where(solver_side, across_far, across)
     own_factor = lax.dynamic_slice_in_dim(slopes[LAYERS - 1], first, rows, 0)
     own_slope = (upstream * own_factor).astype(jnp.bfloat16)
     slope = from_everyone(own_slope, FLOOR).reshape(half, width)

time: 166 us -> 165 us (level)
  Pallas kernels: 28.3 us -> 26.6 us
    pallas_call x2, Pallas kernels: 8.5 us -> 6.79 us  [updated(): pl.pallas_call(update_kernel, out_shape=jax.ShapeDtypeStruct(own.shape, j...]
  transfers between devices with their start and end apart: 18 -> 18, of which waited for: 10 -> 11; matrix products, arithmetic and copies ran while one was open for 18% -> 18% of each run, Pallas kernels for 11% -> 10%
where the time goes in v5:
time: 165 us; the launch traced here: 164 us
  waiting for transfers between devices  44.1 us (27%)
  starting transfers between devices  41.1 us (25%)
  Pallas kernels  26.6 us (16%)
  other arithmetic  23.5 us (14%)
  between operations  14.4 us (9%)
  local copies, waits for them, and re-layouts  14.2 us (9%)
    ppermute x6, starting transfers between devices, swapped(): return lax.ppermute(value, axis, [(0, 1), (1, 0)])  15.3 us
    ppermute x2, waiting for transfers between devices, to_trainer(): return lax.ppermute(value, 'role', [(0, 1)])  14.6 us
    pallas_call x1, Pallas kernels, forward(): pl.pallas_call(forward_kernel, out_shape=(jax.ShapeDtypeStruct((LAYERS, r...  9.5 us
    ppermute x2, starting transfers between devices, to_trainer(): return lax.ppermute(value, 'role', [(0, 1)])  8.31 us
    all_gather x1, waiting for transfers between devices, body(): gathered = lax.all_gather(jnp.stack([near, far]), PLANE, axis=0)  7.99 us
    pallas_call x1, Pallas kernels, backward(): pl.pallas_call(backward_kernel, out_shape=(jax.ShapeDtypeStruct((LAYERS,...  7.79 us
    pallas_call x2, Pallas kernels, updated(): pl.pallas_call(update_kernel, out_shape=jax.ShapeDtypeStruct(own.shape, j...  6.79 us
    ppermute x1, waiting for transfers between devices, body(): before = lax.ppermute(edge, TILE, up)  5.08 us
  transfers between devices with their start and end apart: 18, of which 11 were waited for; matrix products, arithmetic and copies ran while one was open for 18% of the time, Pallas kernels for 10%

profile of v5, /device:TPU:1, one launch (start us, length us, event | category | flops | bytes accessed | tf_op | source)
XLA Modules:
  0.0 163.9 jit_solution(4025707776166847194)
XLA Ops:
  7.2 1.1 bitcast_convert_fusion
  8.3 3.8 %collective-permute-start = (bf16[5,16,1024]{2,1,0:T(8,128)(2,1)S(1)}, bf16[5,16,1024]{2,1,0:T(8,128)(2,1)S(1)}, u32[]{:S(2)}, u32[]{:S(2)}) collective-permute-start(bf16[5,16,1024]{2,1,0:T(8,128)(2,1)S(1)} %bitcast_convert_fusion), channel_id=1, source_target_pairs={{0,64},{64,0},{1,65},{65,1},{2,66},{66,2},{3,67},{67,3},{4,68},{68... | collective-permute-start | bytes 491528 | tf_op jit(solution)/shard_map/ppermute | solution.py:32
  12.1 1.3 collective-permute-start.1
  14.1 1.7 %collective-permute-done = bf16[5,16,1024]{2,1,0:T(8,128)(2,1)S(1)} collective-permute-done((bf16[5,16,1024]{2,1,0:T(8,128)(2,1)S(1)}, bf16[5,16,1024]{2,1,0:T(8,128)(2,1)S(1)}, u32[]{:S(2)}, u32[]{:S(2)}) %collective-permute-start) | collective-permute-done | bytes 163872 | tf_op jit(solution)/shard_map/ppermute | solution.py:32
  15.8 1.0 select_bitcast_fusion.1
  16.8 3.2 %collective-permute-done.1 = bf16[5,16,1024]{2,1,0:T(8,128)(2,1)S(1)} collective-permute-done((bf16[5,16,1024]{2,1,0:T(8,128)(2,1)S(1)}, bf16[5,16,1024]{2,1,0:T(8,128)(2,1)S(1)}, u32[]{:S(2)}, u32[]{:S(2)}) %collective-permute-start.1) | collective-permute-done | bytes 163872 | tf_op jit(solution)/shard_map/ppermute | solution.py:60
  20.0 0.8 pad_maximum_fusion
  20.8 2.5 %bitcast_convert_fusion.1 = bf16[1024,1024]{1,0:T(8,128)(2,1)S(1)} fusion(f32[1,1024,1024]{2,1,0:T(8,128)} %param.12), kind=kLoop, calls=%fused_computation.39 | loop fusion | flops 1048576 | bytes 6291456 | tf_op jit(solution)/shard_map/convert.3
  23.3 1.1 slice.57
  24.4 6.1 %collective-permute-start.5 = (bf16[1024,512]{1,0:T(8,128)(2,1)}, bf16[1024,512]{1,0:T(8,128)(2,1)}, u32[]{:S(2)}, u32[]{:S(2)}) collective-permute-start(bf16[1024,512]{1,0:T(8,128)(2,1)} %slice.57), channel_id=1, source_target_pairs={{0,64},{1,65},{2,66},{3,67},{4,68},{5,69},{6,70},{7,71},{8,72},{9,... | collective-permute-start | bytes 3145736 | tf_op jit(solution)/shard_map/ppermute | solution.py:24
  30.6 3.8 %collective-permute-start.3 = (f32[520,128]{1,0:T(8,128)S(1)}, f32[520,128]{1,0:T(8,128)S(1)}, u32[]{:S(2)}, u32[]{:S(2)}) collective-permute-start(f32[520,128]{1,0:T(8,128)S(1)} %pad_maximum_fusion.1), channel_id=1, source_target_pairs={{0,1},{1,2},{2,3},{3,4},{4,5},{5,6},{6,7},{7,8},{8,9},{9,10},{10,1... | collective-permute-start | bytes 798728 | tf_op jit(solution)/shard_map/ppermute | solution.py:398
  34.4 5.1 %collective-permute-done.3 = f32[520,128]{1,0:T(8,128)S(1)} collective-permute-done((f32[520,128]{1,0:T(8,128)S(1)}, f32[520,128]{1,0:T(8,128)S(1)}, u32[]{:S(2)}, u32[]{:S(2)}) %collective-permute-start.3) | collective-permute-done | bytes 266272 | tf_op jit(solution)/shard_map/ppermute | solution.py:398
  40.2 0.7 fusion.6
  40.9 1.6 collective-permute-done.4
  43.3 2.4 %fusion.7 = (bf16[512,1024]{1,0:T(8,128)(2,1)}, f32[512,1024]{1,0:T(8,128)}) fusion(f32[1024]{0:T(1024)S(1)} %copy-done.20, f32[512,1025]{1,0:T(8,128)S(1)} %fusion, f32[1,512,1024]{2,1,0:T(8,128)S(1)} %copy-done.2), kind=kLoop, calls=%fused_computation.40 | loop fusion | flops 3670016 | bytes 9441280 | tf_op jit(solution)/shard_map/convert_element_type | solution.py:402
  45.7 4.9 %gather_fusion = bf16[512,1024]{1,0:T(8,128)(2,1)} fusion(bf16[512,1024]{1,0:T(8,128)(2,1)} %get-tuple-element.63, s32[1024]{0:T(1024)S(1)} %pad_clamp_fusion), kind=kCustom, calls=%fused_computation | custom fusion | bytes 2099200 | tf_op jit(solution)/shard_map/jit(_take)/gather | solution.py:402
  50.6 2.4 %broadcast_select_fusion = bf16[512,1024]{1,0:T(8,128)(2,1)} fusion(bf16[512,1024]{1,0:T(8,128)(2,1)} %gather_fusion, pred[512]{0:T(512)(128)(4,1)S(1)} %compare_and_fusion), kind=kLoop, calls=%fused_computation.10 | loop fusion | flops 524288 | bytes 2097664 | tf_op jit(solution)/shard_map/jit(_take)/select_n | solution.py:402
  53.0 2.2 %collective-permute-start.6 = (bf16[512,1024]{1,0:T(8,128)(2,1)}, bf16[512,1024]{1,0:T(8,128)(2,1)}, u32[]{:S(2)}, u32[]{:S(2)}) collective-permute-start(bf16[512,1024]{1,0:T(8,128)(2,1)} %broadcast_select_fusion), channel_id=1, source_target_pairs={{0,64},{1,65},{2,66},{3,67},{4,68},{5,69},{6,70},{7,71},{8,72},{9,... | collective-permute-start | bytes 3145736 | tf_op jit(solution)/shard_map/ppermute | solution.py:24
  55.2 0.8 constant_dynamic-slice_fusion.2.features_ref
  56.1 4.7 %convert_element_type.34.weights_ref = bf16[1024,1024]{1,0:T(8,128)(2,1)} convert(f32[1024,1024]{1,0:T(8,128)} %bitcast.40) | non-fusion elementwise | flops 1048576 | bytes 6291456 | tf_op jit(solution)/shard_map/convert_element_type | solution.py:400
  60.7 14.6 %collective-permute-done.6 = bf16[512,1024]{1,0:T(8,128)(2,1)} collective-permute-done((bf16[512,1024]{1,0:T(8,128)(2,1)}, bf16[512,1024]{1,0:T(8,128)(2,1)}, u32[]{:S(2)}, u32[]{:S(2)}) %collective-permute-start.6) | collective-permute-done | bytes 1048608 | tf_op jit(solution)/shard_map/ppermute | solution.py:24
  75.3 8.0 %all-gather.3.cloned.1.call-done = bf16[64,5,16,1024]{3,2,1,0:T(8,128)(2,1)} async-done(((bf16[2,5,16,1024]{3,2,1,0:T(8,128)(2,1)}), bf16[64,5,16,1024]{3,2,1,0:T(8,128)(2,1)}) %all-gather.3.cloned.1.call-update) | async-done | bytes 10485776 | tf_op jit(solution)/shard_map/all_gather | solution.py:387
  83.3 9.5 %shard_map.94 = (bf16[5,256,128]{2,1,0:T(8,128)(2,1)}, bf16[256,1024]{1,0:T(8,128)(2,1)}, f32[5,256,1024]{2,1,0:T(8,128)}) custom-call(bf16[32,2,5,16,1024]{4,3,2,1,0:T(8,128)(2,1)} %bitcast.48, bf16[256,1024]{1,0:T(8,128)(2,1)} %constant_dynamic-slice_fusion.2.features_ref), custom_call_target="tpu_custom_call" | custom-call | flops 2684354560 | bytes 28835840 | tf_op jit(solution)/shard_map/pallas_call | solution.py:139
  93.2 1.0 copy-done.4
  94.2 1.3 shard_map.95
  95.5 1.3 shard_map.96
  97.3 1.0 slice_select_fusion
  98.3 2.7 %collective-permute-start.9 = (bf16[512,512]{1,0:T(8,128)(2,1)S(1)}, bf16[512,512]{1,0:T(8,128)(2,1)S(1)}, u32[]{:S(2)}, u32[]{:S(2)}) collective-permute-start(bf16[512,512]{1,0:T(8,128)(2,1)S(1)} %get-tuple-element.66), channel_id=1, source_target_pairs={{0,64},{64,0},{1,65},{65,1},{2,66},{66,2},{3,67},{67,3},{4,68},{68... | collective-permute-start | bytes 1572872 | tf_op jit(solution)/shard_map/ppermute | solution.py:32
  101.1 0.9 add_convert_fusion
  102.0 4.9 %all-to-all-start = ((bf16[16,16,1024]{2,1,0:T(8,128)(2,1)}), bf16[16,16,1024]{2,1,0:T(8,128)(2,1)S(1)}, u32[]{:S(2)}, u32[]{:S(2)}) async-start(bf16[16,16,1024]{2,1,0:T(8,128)(2,1)} %bitcast.8), calls=%async_computation | async-start | bytes 1048576 | tf_op jit(solution)/shard_map/all_to_all | solution.py:422
  106.9 3.6 %convert_select_fusion = f32[512,1024]{1,0:T(8,128)} fusion(f32[512,1024]{1,0:T(8,128)} %get-tuple-element.43, bf16[512,1024]{1,0:T(8,128)(2,1)} %collective-permute-done.6, pred[]{:T(512)S(6)} %eq.6), kind=kLoop, calls=%fused_computation.6 | loop fusion | flops 1048576 | bytes 5242881 | tf_op jit(solution)/shard_map/jit(_where)/select_n | solution.py:407
  110.5 2.6 %collective-permute-done.9.far_ref.upper_ref = bf16[512,512]{1,0:T(8,128)(2,1)S(1)} collective-permute-done((bf16[512,512]{1,0:T(8,128)(2,1)S(1)}, bf16[512,512]{1,0:T(8,128)(2,1)S(1)}, u32[]{:S(2)}, u32[]{:S(2)}) %collective-permute-start.9) | collective-permute-done | bytes 524320 | tf_op jit(solution)/shard_map/ppermute | solution.py:32
  113.1 4.1 %all-to-all-done = bf16[16,16,1024]{2,1,0:T(8,128)(2,1)S(1)} async-done(((bf16[16,16,1024]{2,1,0:T(8,128)(2,1)}), bf16[16,16,1024]{2,1,0:T(8,128)(2,1)S(1)}, u32[]{:S(2)}, u32[]{:S(2)}) %all-to-all-start) | async-done | bytes 524320 | tf_op jit(solution)/shard_map/all_to_all | solution.py:422
  117.3 1.3 collective-permute-start.10
  118.6 1.3 collective-permute-start.11
  120.6 1.3 slice.54
  121.9 1.9 %collective-permute-done.10 = f32[16,1024]{1,0:T(8,128)S(1)} collective-permute-done((f32[16,1024]{1,0:T(8,128)S(1)}, f32[16,1024]{1,0:T(8,128)S(1)}, u32[]{:S(2)}, u32[]{:S(2)}) %collective-permute-start.10) | collective-permute-done | bytes 65568 | tf_op jit(solution)/shard_map/ppermute | solution.py:28
  123.8 1.0 collective-permute-done.11
  125.1 0.9 broadcast_in_dim.50
  125.9 3.6 %all-to-all-start.1 = ((bf16[16,16,1024]{2,1,0:T(8,128)(2,1)}), bf16[16,16,1024]{2,1,0:T(8,128)(2,1)S(1)}, u32[]{:S(2)}, u32[]{:S(2)}) async-start(bf16[16,16,1024]{2,1,0:T(8,128)(2,1)} %broadcast_in_dim.50), calls=%async_computation.1 | async-start | bytes 1048576 | tf_op jit(solution)/shard_map/all_to_all | solution.py:37
  130.2 3.6 %collective-permute-start.13 = (bf16[512,512]{1,0:T(8,128)(2,1)}, bf16[512,512]{1,0:T(8,128)(2,1)S(1)}, u32[]{:S(2)}, u32[]{:S(2)}) collective-permute-start(bf16[512,512]{1,0:T(8,128)(2,1)} %get-tuple-element.58), channel_id=1, source_target_pairs={{0,64},{64,0},{1,65},{65,1},{2,66},{66,2},{3,67},{67,3},{4,68},{68... | collective-permute-start | bytes 1572872 | tf_op jit(solution)/shard_map/ppermute | solution.py:32
  133.9 4.3 %shard_map.97.begun = f32[1024,1024]{1,0:T(8,128)} custom-call(s32[1]{0:T(128)} %bitcast.10.solver_ref, f32[1024,1024]{1,0:T(8,128)} %bitcast.41, bf16[1024,512]{1,0:T(8,128)(2,1)} %collective-permute-done.5.upper_ref.lower_ref, bf16[1024,512]{1,0:T(8,128)(2,1)} %collective-permute-done.5.upper_ref.lower_ref, ...), custom_call_target="tpu_custom_call" | custom-call | flops 536870912 | bytes 5242880 | tf_op jit(solution)/shard_map/pallas_call | solution.py:332
  138.5 0.8 copy-done.16
  139.3 7.8 %shard_map.98 = (f32[5,16,1024]{2,1,0:T(8,128)}, f32[5,16,1024]{2,1,0:T(8,128)}) custom-call(bf16[256,1024]{1,0:T(8,128)(2,1)} %bitcast.51, bf16[5,32,256]{2,1,0:T(8,128)(2,1)} %maximum_bitcast_fusion.own_inputs_ref, f32[5,256,1024]{2,1,0:T(8,128)} %get-tuple-element.50.slopes_in, bf16[32,2,5,16,1024]{4,3,2,1,0:T(8,128)(2,1)} %bitcast.49), custom_call_target="tpu_custom_call" | custom-call | flops 2147483648 | bytes 15728640 | tf_op jit(solution)/shard_map/pallas_call | solution.py:205
  147.1 4.4 %collective-permute-start.14 = (f32[5,16,1024]{2,1,0:T(8,128)}, f32[5,16,1024]{2,1,0:T(8,128)S(1)}, u32[]{:S(2)}, u32[]{:S(2)}) collective-permute-start(f32[5,16,1024]{2,1,0:T(8,128)} %get-tuple-element.62), channel_id=1, source_target_pairs={{0,1},{1,0},{2,3},{3,2},{4,5},{5,4},{6,7},{7,6},{8,9},{9,8},{10,11... | collective-permute-start | bytes 983048 | tf_op jit(solution)/shard_map/ppermute | solution.py:32
  151.5 2.2 %copy-done.1 = f32[1,1024,1024]{2,1,0:T(8,128)S(1)} copy-done((f32[1,1024,1024]{2,1,0:T(8,128)S(1)}, f32[1,1024,1024]{2,1,0:T(8,128)}, u32[]{:S(2)}) %copy-start.1) | copy-done | bytes 4194328
  153.7 2.5 %shard_map.99 = f32[1024,1024]{1,0:T(8,128)} custom-call(s32[1]{0:T(128)} %bitcast.10.solver_ref, f32[1024,1024]{1,0:T(8,128)S(1)} %bitcast.43, bf16[512,512]{1,0:T(8,128)(2,1)S(1)} %copy-done.11, bf16[512,512]{1,0:T(8,128)(2,1)S(1)} %collective-permute-done.13.lower_ref.far_ref, bf16[256,1024]{1,0:T(8,128)(2,1)S(1)} %copy-done.5, ...), custom_call_target="tpu_custom_call", output_to_operand_aliasing={{}: (8, {})} | custom-call | flops 536870912 | bytes 5242880 | tf_op jit(solution)/shard_map/pallas_call | solution.py:332
  156.2 0.8 fusion.3
  (75 shorter events, 5.1 us)
Async XLA Ops:
  7.2 48.1 %copy-start = (bf16[512,1024]{1,0:T(8,128)(2,1)S(1)}, bf16[512,1024]{1,0:T(8,128)(2,1)}, u32[]{:S(2)}) copy-start(bf16[512,1024]{1,0:T(8,128)(2,1)} %param.10) | copy-start | bytes 3145732
  7.2 76.1 %all-gather.3.cloned.1.call-start = ((), (), s32[]{:S(2)}) async-start(), calls=%async_computation.2 | async-start | bytes 10813440 | tf_op jit(solution)/shard_map/all_gather | solution.py:387
  8.3 7.5 %collective-permute-start = (bf16[5,16,1024]{2,1,0:T(8,128)(2,1)S(1)}, bf16[5,16,1024]{2,1,0:T(8,128)(2,1)S(1)}, u32[]{:S(2)}, u32[]{:S(2)}) collective-permute-start(bf16[5,16,1024]{2,1,0:T(8,128)(2,1)S(1)} %bitcast_convert_fusion), channel_id=1, source_target_pairs={{0,64},{64,0},{1,65},{65,1},{2,66},{66,2},{3,67},{67,3},{4,68},{68... | collective-permute-start | bytes 491528 | tf_op jit(solution)/shard_map/ppermute | solution.py:32
  12.1 7.8 %collective-permute-start.1 = (bf16[5,16,1024]{2,1,0:T(8,128)(2,1)S(1)}, bf16[5,16,1024]{2,1,0:T(8,128)(2,1)S(1)}, u32[]{:S(2)}, u32[]{:S(2)}) collective-permute-start(bf16[5,16,1024]{2,1,0:T(8,128)(2,1)S(1)} %bitcast_convert_fusion), channel_id=1, source_target_pairs={{64,32},{65,33},{66,34},{67,35},{68,36},{69,37},{70,38},{71,39},{7... | collective-permute-start | bytes 491528 | tf_op jit(solution)/shard_map/ppermute | solution.py:60
  13.4 6.6 %collective-permute-start.2 = (bf16[5,16,1024]{2,1,0:T(8,128)(2,1)S(1)}, bf16[5,16,1024]{2,1,0:T(8,128)(2,1)S(1)}, u32[]{:S(2)}, u32[]{:S(2)}) collective-permute-start(bf16[5,16,1024]{2,1,0:T(8,128)(2,1)S(1)} %bitcast_convert_fusion), channel_id=1, source_target_pairs={{64,96},{65,97},{66,98},{67,99},{68,100},{69,101},{70,102},{71,103... | collective-permute-start | bytes 491528 | tf_op jit(solution)/shard_map/ppermute | solution.py:60
  20.8 9.7 %copy-start.21 = (f32[1024]{0:T(1024)S(1)}, f32[1024]{0:T(1024)}, u32[]{:S(2)}) copy-start(f32[1024]{0:T(1024)} %param.8) | copy-start | bytes 12292
  23.3 16.9 %copy-start.12 = (bf16[1024,1024]{1,0:T(8,128)(2,1)}, bf16[1024,1024]{1,0:T(8,128)(2,1)S(1)}, u32[]{:S(2)}) copy-start(bf16[1024,1024]{1,0:T(8,128)(2,1)S(1)} %bitcast_convert_fusion.1) | copy-start | bytes 6291460
  23.3 7.2 %copy-start.2 = (f32[1,512,1024]{2,1,0:T(8,128)S(1)}, f32[1,512,1024]{2,1,0:T(8,128)}, u32[]{:S(2)}) copy-start(f32[1,512,1024]{2,1,0:T(8,128)} %param.7) | copy-start | bytes 6291460
  23.3 11.0 %copy-start.19 = (s32[512]{0:T(512)S(1)}, s32[512]{0:T(512)}, u32[]{:S(2)}) copy-start(s32[512]{0:T(512)} %param.11) | copy-start | bytes 6148
  24.4 36.3 %collective-permute-start.5 = (bf16[1024,512]{1,0:T(8,128)(2,1)}, bf16[1024,512]{1,0:T(8,128)(2,1)}, u32[]{:S(2)}, u32[]{:S(2)}) collective-permute-start(bf16[1024,512]{1,0:T(8,128)(2,1)} %slice.57), channel_id=1, source_target_pairs={{0,64},{1,65},{2,66},{3,67},{4,68},{5,69},{6,70},{7,71},{8,72},{9,... | collective-permute-start | bytes 3145736 | tf_op jit(solution)/shard_map/ppermute | solution.py:24
  30.6 8.9 %collective-permute-start.3 = (f32[520,128]{1,0:T(8,128)S(1)}, f32[520,128]{1,0:T(8,128)S(1)}, u32[]{:S(2)}, u32[]{:S(2)}) collective-permute-start(f32[520,128]{1,0:T(8,128)S(1)} %pad_maximum_fusion.1), channel_id=1, source_target_pairs={{0,1},{1,2},{2,3},{3,4},{4,5},{5,6},{6,7},{7,8},{8,9},{9,10},{10,1... | collective-permute-start | bytes 798728 | tf_op jit(solution)/shard_map/ppermute | solution.py:398
  34.4 8.2 %collective-permute-start.4 = (f32[512,128]{1,0:T(8,128)S(1)}, f32[512,128]{1,0:T(8,128)S(1)}, u32[]{:S(2)}, u32[]{:S(2)}) collective-permute-start(f32[512,128]{1,0:T(8,128)S(1)} %get-tuple-element.67), channel_id=1, source_target_pairs={{1,0},{2,1},{3,2},{4,3},{5,4},{6,5},{7,6},{8,7},{9,8},{10,9},{11,1... | collective-permute-start | bytes 786440 | tf_op jit(solution)/shard_map/ppermute | solution.py:399
  42.5 0.7 copy-start.20
  53.0 22.3 %collective-permute-start.6 = (bf16[512,1024]{1,0:T(8,128)(2,1)}, bf16[512,1024]{1,0:T(8,128)(2,1)}, u32[]{:S(2)}, u32[]{:S(2)}) collective-permute-start(bf16[512,1024]{1,0:T(8,128)(2,1)} %broadcast_select_fusion), channel_id=1, source_target_pairs={{0,64},{1,65},{2,66},{3,67},{4,68},{5,69},{6,70},{7,71},{8,72},{9,... | collective-permute-start | bytes 3145736 | tf_op jit(solution)/shard_map/ppermute | solution.py:24
  83.3 9.8 %copy-start.3 = (bf16[1024,1024]{1,0:T(8,128)(2,1)S(1)}, bf16[1024,1024]{1,0:T(8,128)(2,1)}, u32[]{:S(2)}) copy-start(bf16[1024,1024]{1,0:T(8,128)(2,1)} %convert_element_type.34.weights_ref) | copy-start | bytes 6291460
  92.8 2.7 %collective-permute-start.7 = (bf16[256,1024]{1,0:T(8,128)(2,1)}, bf16[256,1024]{1,0:T(8,128)(2,1)S(1)}, u32[]{:S(2)}, u32[]{:S(2)}) collective-permute-start(bf16[256,1024]{1,0:T(8,128)(2,1)} %get-tuple-element.36.activation_ref.last_ref), channel_id=1, source_target_pairs={{0,1},{1,0},{2,3},{3,2},{4,5},{5,4},{6,7},{7,6},{8,9},{9,8},{10,11... | collective-permute-start | bytes 1572872 | tf_op jit(solution)/shard_map/ppermute | solution.py:32
  93.2 1.0 copy-start.4
  95.5 1.3 copy-start.6
  95.5 1.8 %copy-start.13 = (bf16[1024,1024]{1,0:T(8,128)(2,1)S(1)}, bf16[1024,1024]{1,0:T(8,128)(2,1)}, u32[]{:S(2)}) copy-start(bf16[1024,1024]{1,0:T(8,128)(2,1)} %copy-done.12) | copy-start | bytes 6291460
  96.8 4.3 %collective-permute-start.8 = (bf16[256,1024]{1,0:T(8,128)(2,1)S(1)}, bf16[256,1024]{1,0:T(8,128)(2,1)S(1)}, u32[]{:S(2)}, u32[]{:S(2)}) collective-permute-start(bf16[256,1024]{1,0:T(8,128)(2,1)S(1)} %get-tuple-element.40), channel_id=1, source_target_pairs={{0,1},{1,0},{2,3},{3,2},{4,5},{5,4},{6,7},{7,6},{8,9},{9,8},{10,11... | collective-permute-start | bytes 1572872 | tf_op jit(solution)/shard_map/ppermute | solution.py:32
  97.2 4.8 %copy-start.14 = (bf16[512,512]{1,0:T(8,128)(2,1)}, bf16[512,512]{1,0:T(8,128)(2,1)S(1)}, u32[]{:S(2)}) copy-start(bf16[512,512]{1,0:T(8,128)(2,1)S(1)} %constant_dynamic-update-slice_fusion.here_ref) | copy-start | bytes 1572868
  97.3 4.7 %copy-start.8 = (bf16[512,512]{1,0:T(8,128)(2,1)}, bf16[512,512]{1,0:T(8,128)(2,1)S(1)}, u32[]{:S(2)}) copy-start(bf16[512,512]{1,0:T(8,128)(2,1)S(1)} %constant_dynamic-update-slice_fusion.2.here_ref) | copy-start | bytes 1572868
  98.3 14.8 %collective-permute-start.9 = (bf16[512,512]{1,0:T(8,128)(2,1)S(1)}, bf16[512,512]{1,0:T(8,128)(2,1)S(1)}, u32[]{:S(2)}, u32[]{:S(2)}) collective-permute-start(bf16[512,512]{1,0:T(8,128)(2,1)S(1)} %get-tuple-element.66), channel_id=1, source_target_pairs={{0,64},{64,0},{1,65},{65,1},{2,66},{66,2},{3,67},{67,3},{4,68},{68... | collective-permute-start | bytes 1572872 | tf_op jit(solution)/shard_map/ppermute | solution.py:32
  102.0 15.2 %all-to-all-start = ((bf16[16,16,1024]{2,1,0:T(8,128)(2,1)}), bf16[16,16,1024]{2,1,0:T(8,128)(2,1)S(1)}, u32[]{:S(2)}, u32[]{:S(2)}) async-start(bf16[16,16,1024]{2,1,0:T(8,128)(2,1)} %bitcast.8), calls=%async_computation | async-start | bytes 1048576 | tf_op jit(solution)/shard_map/all_to_all | solution.py:422
  110.5 14.3 %copy-start.17 = (bf16[5,256,128]{2,1,0:T(8,128)(2,1)S(1)}, bf16[5,256,128]{2,1,0:T(8,128)(2,1)}, u32[]{:S(2)}) copy-start(bf16[5,256,128]{2,1,0:T(8,128)(2,1)} %get-tuple-element.52) | copy-start | bytes 983044
  113.1 12.8 %copy-start.10 = (bf16[512,512]{1,0:T(8,128)(2,1)}, bf16[512,512]{1,0:T(8,128)(2,1)S(1)}, u32[]{:S(2)}) copy-start(bf16[512,512]{1,0:T(8,128)(2,1)S(1)} %collective-permute-done.9.far_ref.upper_ref) | copy-start | bytes 1572868
  117.3 6.5 %collective-permute-start.10 = (f32[16,1024]{1,0:T(8,128)S(1)}, f32[16,1024]{1,0:T(8,128)S(1)}, u32[]{:S(2)}, u32[]{:S(2)}) collective-permute-start(f32[16,1024]{1,0:T(8,128)S(1)} %convert_reduce_fusion), channel_id=1, source_target_pairs={{64,0},{65,1},{66,2},{67,3},{68,4},{69,5},{70,6},{71,7},{72,8},{73... | collective-permute-start | bytes 196616 | tf_op jit(solution)/shard_map/ppermute | solution.py:28
  118.6 6.2 %collective-permute-start.11 = (f32[16,1024]{1,0:T(8,128)S(1)}, f32[16,1024]{1,0:T(8,128)S(1)}, u32[]{:S(2)}, u32[]{:S(2)}) collective-permute-start(f32[16,1024]{1,0:T(8,128)S(1)} %convert_reduce_fusion), channel_id=1, source_target_pairs={{64,32},{65,33},{66,34},{67,35},{68,36},{69,37},{70,38},{71,39},{7... | collective-permute-start | bytes 196616 | tf_op jit(solution)/shard_map/ppermute | solution.py:60
  119.9 4.9 %collective-permute-start.12 = (f32[16,1024]{1,0:T(8,128)S(1)}, f32[16,1024]{1,0:T(8,128)S(1)}, u32[]{:S(2)}, u32[]{:S(2)}) collective-permute-start(f32[16,1024]{1,0:T(8,128)S(1)} %convert_reduce_fusion), channel_id=1, source_target_pairs={{64,96},{65,97},{66,98},{67,99},{68,100},{69,101},{70,102},{71,103... | collective-permute-start | bytes 196616 | tf_op jit(solution)/shard_map/ppermute | solution.py:60
  125.9 12.6 %all-to-all-start.1 = ((bf16[16,16,1024]{2,1,0:T(8,128)(2,1)}), bf16[16,16,1024]{2,1,0:T(8,128)(2,1)S(1)}, u32[]{:S(2)}, u32[]{:S(2)}) async-start(bf16[16,16,1024]{2,1,0:T(8,128)(2,1)} %broadcast_in_dim.50), calls=%async_computation.1 | async-start | bytes 1048576 | tf_op jit(solution)/shard_map/all_to_all | solution.py:37
  130.2 16.9 %collective-permute-start.13 = (bf16[512,512]{1,0:T(8,128)(2,1)}, bf16[512,512]{1,0:T(8,128)(2,1)S(1)}, u32[]{:S(2)}, u32[]{:S(2)}) collective-permute-start(bf16[512,512]{1,0:T(8,128)(2,1)} %get-tuple-element.58), channel_id=1, source_target_pairs={{0,64},{64,0},{1,65},{65,1},{2,66},{66,2},{3,67},{67,3},{4,68},{68... | collective-permute-start | bytes 1572872 | tf_op jit(solution)/shard_map/ppermute | solution.py:32
  138.5 0.8 copy-start.16
  139.3 12.2 %copy-start.5 = (bf16[256,1024]{1,0:T(8,128)(2,1)S(1)}, bf16[256,1024]{1,0:T(8,128)(2,1)}, u32[]{:S(2)}) copy-start(bf16[256,1024]{1,0:T(8,128)(2,1)} %get-tuple-element.36.activation_ref.last_ref) | copy-start | bytes 1572868
  139.3 12.2 %copy-start.7 = (bf16[256,1024]{1,0:T(8,128)(2,1)S(1)}, bf16[256,1024]{1,0:T(8,128)(2,1)}, u32[]{:S(2)}) copy-start(bf16[256,1024]{1,0:T(8,128)(2,1)} %copy-done.6) | copy-start | bytes 1572868
  139.3 12.2 %copy-start.9 = (bf16[512,512]{1,0:T(8,128)(2,1)S(1)}, bf16[512,512]{1,0:T(8,128)(2,1)}, u32[]{:S(2)}) copy-start(bf16[512,512]{1,0:T(8,128)(2,1)} %copy-done.8) | copy-start | bytes 1572868
  139.3 12.2 %copy-start.11 = (bf16[512,512]{1,0:T(8,128)(2,1)S(1)}, bf16[512,512]{1,0:T(8,128)(2,1)}, u32[]{:S(2)}) copy-start(bf16[512,512]{1,0:T(8,128)(2,1)} %copy-done.10) | copy-start | bytes 1572868
  147.1 9.1 %collective-permute-start.14 = (f32[5,16,1024]{2,1,0:T(8,128)}, f32[5,16,1024]{2,1,0:T(8,128)S(1)}, u32[]{:S(2)}, u32[]{:S(2)}) collective-permute-start(f32[5,16,1024]{2,1,0:T(8,128)} %get-tuple-element.62), channel_id=1, source_target_pairs={{0,1},{1,0},{2,3},{3,2},{4,5},{5,4},{6,7},{7,6},{8,9},{9,8},{10,11... | collective-permute-start | bytes 983048 | tf_op jit(solution)/shard_map/ppermute | solution.py:32
  151.5 2.2 %copy-start.1 = (f32[1,1024,1024]{2,1,0:T(8,128)S(1)}, f32[1,1024,1024]{2,1,0:T(8,128)}, u32[]{:S(2)}) copy-start(f32[1,1024,1024]{2,1,0:T(8,128)} %param.12) | copy-start | bytes 12582916
  153.7 2.5 %copy-start.15 = (f32[1,5,16,1024]{3,2,1,0:T(8,128)S(1)}, f32[1,5,16,1024]{3,2,1,0:T(8,128)}, u32[]{:S(2)}) copy-start(f32[1,5,16,1024]{3,2,1,0:T(8,128)} %param.13) | copy-start | bytes 983044
  153.7 2.5 %copy-start.18 = (f32[5,16,1024]{2,1,0:T(8,128)S(1)}, f32[5,16,1024]{2,1,0:T(8,128)}, u32[]{:S(2)}) copy-start(f32[5,16,1024]{2,1,0:T(8,128)} %get-tuple-element.61) | copy-start | bytes 983044
Sparse Core Ops, SparseCore 0:
  20.9 62.3 all-gather.2
